TPU v7x, 32 devices: a whole 2x2x4 slice. The times are simulated.
32 devices in a mesh: groups: 2 (over y), tile: 4 (over z), image: 4 (over x, core).
Axes of the slice: x: 2, y: 2, z: 4, core: 2. Of those that a mesh axis runs over, the one named last changes fastest.
Arguments:
- images: bfloat16 [8, 16, 64, 256], P(('groups', 'image'), 'tile'), parts along dimension 0, may hold values from -12 to 12
- cotangent: bfloat16 [8, 16, 64, 256], P(('groups', 'image'), 'tile'), parts along dimension 0, may hold values from -12 to 12
- timesteps: int32 [8], P(('groups', 'image')), parts along dimension 0, may hold values from 0 to 999
- class_ids: int32 [8], P(('groups', 'image')), parts along dimension 0, may hold values from 0 to 999
- norm_gain: float32 [256], replicated, may hold values from 0.25 to 1.75
- norm_bias: float32 [256], replicated, may hold values from -3 to 3
- conv_first: bfloat16 [3, 3, 256, 256], replicated, may hold values from -0.125 to 0.125
- conv_second: bfloat16 [3, 3, 256, 256], replicated, may hold values from -0.125 to 0.125
- time_weight: bfloat16 [256, 1024], P(None, 'tile'), may hold values from -0.375 to 0.375
- time_bias: float32 [1024], P('tile'), may hold values from -3 to 3
- class_table: bfloat16 [1000, 1024], P(None, 'tile'), may hold values from -5 to 5
- adaptive_weight: bfloat16 [1024, 512], P('tile'), may hold values from -0.1875 to 0.1875
- adaptive_bias: float32 [512], replicated, may hold values from -2 to 2
Outputs:
- branch: bfloat16 [8, 16, 64, 256], P(('groups', 'image'), 'tile'), parts along dimension 0
- input_grad: bfloat16 [8, 16, 64, 256], P(('groups', 'image'), 'tile'), parts along dimension 0
- grad_adaptive_weight: float32 [2048, 512], P(('groups', 'tile')), parts along dimension 0
- grad_adaptive_bias: float32 [1024], P('groups'), parts along dimension 0
There are 2 independent parts, one for each index of `groups`. A program takes and returns all parts, laid end to end along the dimension named above; an argument that names none is the same for every part. Nothing has to cross between parts.
All inputs are finite; a program needn't handle non-finite values.
Results may differ from a plain program's by a relative error of at most 0.013.
Values may be sent and summed in bfloat16 or wider, within the bound.
No kernel may reach another device: no remote copies, remote signals or barrier semaphores. Data moves between devices by JAX's collectives and lax.ppermute only.
A program may use at most 64 MiB of HBM per device.

v0:
```python
import math

import jax
import jax.numpy as jnp
from jax import lax
from jax.sharding import PartitionSpec as P

GN_GROUPS = 32


EPSILON = 1e-05


def with_halo(block, sides, width):
    for axis, dim in sides:
        count = lax.axis_size(axis)
        forward = [(i, i + 1) for i in range(count - 1)]
        backward = [(target, source) for source, target in forward]
        low = lax.ppermute(
            lax.slice_in_dim(block, block.shape[dim] - width, None, axis=dim), axis, forward
        )
        high = lax.ppermute(lax.slice_in_dim(block, 0, width, axis=dim), axis, backward)
        block = jnp.concatenate([low, block, high], axis=dim)
    return block


def silu_grad(pre_values):
    sigma = jax.nn.sigmoid(pre_values)
    return sigma * (1.0 + pre_values * (1.0 - sigma))


def conv_rows(padded, kernel):
    row_count = padded.shape[1] - 2
    col_count = padded.shape[2]
    channels = padded.shape[3]
    padded_cols = jnp.pad(padded, ((0, 0), (0, 0), (1, 1), (0, 0)))
    widened = jnp.concatenate(
        [padded_cols[:, :, offset : offset + col_count] for offset in range(3)], axis=3
    )
    summed = None
    for offset in range(3):
        row_block = widened[:, offset : offset + row_count].reshape(-1, 3 * channels)
        product = jnp.dot(
            row_block, kernel[offset].reshape(3 * channels, -1), preferred_element_type=jnp.float32
        )
        summed = product if summed is None else summed + product
    return summed.reshape(padded.shape[0], row_count, col_count, -1)


def group_total(values):
    return values.reshape(values.shape[0], GN_GROUPS, -1).sum(axis=2)


def spread_groups(values, channels):
    return jnp.repeat(values, channels // GN_GROUPS, axis=1)[:, None, None, :]


def cell_total(values):
    return (
        values.shape[1] * values.shape[2] * lax.axis_size("tile") * (values.shape[3] // GN_GROUPS)
    )


def moments(values):
    channels = values.shape[3]
    cell_count = cell_total(values)
    first_sum = group_total(jnp.sum(values, axis=(1, 2)))
    square_sum = group_total(jnp.sum(values * values, axis=(1, 2)))
    first_sum, square_sum = lax.psum((first_sum, square_sum), "tile")
    centre = first_sum / cell_count
    spread = square_sum / cell_count - centre * centre
    centre = spread_groups(centre, channels)
    return (centre, spread_groups(lax.rsqrt(spread + EPSILON), channels))


def with_rims(active):
    return with_halo(active, (("tile", 1),), 1)


def first_rims(active, cotangent):
    padded_first = with_rims(active)
    padded_grad = with_halo(cotangent, (("tile", 1),), 1)
    return (padded_first, padded_grad)


def norm_back_first(grad_norm, normed, inverse):
    channels = grad_norm.shape[3]
    cell_count = cell_total(grad_norm)
    plain_sum = group_total(jnp.sum(grad_norm, axis=(1, 2)))
    paired_sum = group_total(jnp.sum(grad_norm * normed, axis=(1, 2)))
    plain_sum, paired_sum = lax.psum((plain_sum, paired_sum), "tile")
    return inverse * (
        grad_norm
        - spread_groups(plain_sum / cell_count, channels)
        - normed * spread_groups(paired_sum / cell_count, channels)
    )


def body(
    images,
    cotangent,
    timesteps,
    class_ids,
    norm_gain,
    norm_bias,
    conv_first,
    conv_second,
    time_weight,
    time_bias,
    class_table,
    adaptive_weight,
    adaptive_bias,
):
    channels = images.shape[3]
    half_freq = time_weight.shape[0] // 2
    frequencies = jnp.exp(-math.log(10000.0) * jnp.arange(half_freq, dtype=jnp.float32) / half_freq)
    angles = timesteps.astype(jnp.float32)[:, None] * frequencies[None]
    sinusoid = jnp.concatenate([jnp.cos(angles), jnp.sin(angles)], axis=1)
    hidden = (
        jnp.dot(sinusoid, time_weight.astype(jnp.float32), precision=lax.Precision.HIGHEST)
        + time_bias
    )
    onehot = (class_ids[:, None] == jnp.arange(class_table.shape[0], dtype=jnp.int32)[None]).astype(
        jnp.float32
    )
    embedding = jax.nn.silu(hidden) + jnp.dot(
        onehot, class_table.astype(jnp.float32), precision=lax.Precision.HIGHEST
    )
    activated = jax.nn.silu(embedding)
    partial_terms = jnp.dot(
        activated, adaptive_weight.astype(jnp.float32), precision=lax.Precision.HIGHEST
    )
    modulation = lax.psum(partial_terms, "tile") + adaptive_bias
    factor_row = 1.0 + modulation[:, :channels]
    factor = factor_row[:, None, None, :]
    shift_term = modulation[:, channels:][:, None, None, :]
    input_float = images.astype(jnp.float32)
    centre_first, inverse_first = moments(input_float)
    normed_first = (input_float - centre_first) * inverse_first
    pre_first = normed_first * norm_gain + norm_bias
    active_first = jax.nn.silu(pre_first).astype(jnp.bfloat16)
    padded_first, padded_grad = first_rims(active_first, cotangent)
    hidden_first = conv_rows(padded_first, conv_first).astype(jnp.bfloat16)
    hidden_float = hidden_first.astype(jnp.float32)
    centre_second, inverse_second = moments(hidden_float)
    normed_second = (hidden_float - centre_second) * inverse_second
    pre_second = normed_second * factor + shift_term
    active_second = jax.nn.silu(pre_second).astype(jnp.bfloat16)
    padded_second = with_rims(active_second)
    branch = conv_rows(padded_second, conv_second).astype(jnp.bfloat16)
    flipped_second = jnp.flip(conv_second, (0, 1)).transpose(0, 1, 3, 2)
    grad_active = conv_rows(padded_grad, flipped_second)
    grad_pre = grad_active * silu_grad(pre_second)
    scale_sum = jnp.sum(grad_pre * normed_second, axis=(1, 2))
    shift_sum = jnp.sum(grad_pre, axis=(1, 2))
    scale_sum, shift_sum = lax.psum((scale_sum, shift_sum), "tile")
    cell_count = cell_total(grad_pre)
    plain_mean = group_total(shift_sum * factor_row) / cell_count
    paired_mean = group_total(scale_sum * factor_row) / cell_count
    grad_norm = grad_pre * factor
    grad_hidden = (
        inverse_second
        * (
            grad_norm
            - spread_groups(plain_mean, channels)
            - normed_second * spread_groups(paired_mean, channels)
        )
    ).astype(jnp.bfloat16)
    flipped_first = jnp.flip(conv_first, (0, 1)).transpose(0, 1, 3, 2)
    padded_hidden = with_halo(grad_hidden, (("tile", 1),), 1)
    grad_active_first = conv_rows(padded_hidden, flipped_first)
    grad_first = grad_active_first * silu_grad(pre_first) * norm_gain
    input_grad = norm_back_first(grad_first, normed_first, inverse_first).astype(jnp.bfloat16)
    pairs = jnp.concatenate([scale_sum, shift_sum], axis=1)
    local_weight = jnp.dot(activated.T, pairs, precision=lax.Precision.HIGHEST)
    local_bias = jnp.sum(pairs, axis=0)
    grad_weight, grad_bias = (
        lax.psum(local_weight.astype(jnp.bfloat16), "image").astype(jnp.float32),
        lax.psum(local_bias.astype(jnp.bfloat16), "image").astype(jnp.float32),
    )
    return (branch, input_grad, grad_weight, grad_bias)


def solution(mesh):
    return jax.shard_map(
        body,
        mesh=mesh,
        in_specs=(
            P(("groups", "image"), "tile", None, None),
            P(("groups", "image"), "tile", None, None),
            P(("groups", "image")),
            P(("groups", "image")),
            P(),
            P(),
            P(),
            P(),
            P(None, "tile"),
            P("tile"),
            P(None, "tile"),
            P("tile", None),
            P(),
        ),
        out_specs=(
            P(("groups", "image"), "tile", None, None),
            P(("groups", "image"), "tile", None, None),
            P(("groups", "tile"), None),
            P("groups"),
        ),
        check_vma=False,
    )
```

profile of v0, /device:TPU:0, one launch (start us, length us, event | category | flops | bytes accessed | tf_op | source)
XLA Modules:
  0.0 124.9 jit_solution(5303490498117019014)
XLA Ops:
  7.2 1.0 convert_reduce_fusion
  8.6 13.5 %all-reduce.7 = (f32[1,32]{1,0:T(1,128)S(1)}, f32[1,32]{1,0:T(1,128)S(1)}) all-reduce(f32[1,32]{1,0:T(1,128)S(1)} %bitcast.139, f32[1,32]{1,0:T(1,128)S(1)} %bitcast.141), channel_id=1, replica_groups=mesh['groups'=2,'tile'=4,'image'=4] {'tile'}, use_global_device_ids=true, to_apply=%region_5.6 | all-reduce | flops 64 | bytes 512 | tf_op jit(solution)/shard_map/psum | solution.py:69
  22.5 1.0 fusion.15
  23.5 0.6 fusion.55
  24.1 1.3 %collective-permute-start.1 = (bf16[1,1,64,256]{3,2,1,0:T(8,128)(2,1)}, bf16[1,1,64,256]{3,2,1,0:T(8,128)(2,1)S(1)}, u32[]{:S(2)}, u32[]{:S(2)}) collective-permute-start(bf16[1,1,64,256]{3,2,1,0:T(8,128)(2,1)} %get-tuple-element.65), channel_id=1, source_target_pairs={{4,0},{8,4},{12,8},{5,1},{9,5},{13,9},{6,2},{10,6},{14,10},{7,3},{... | collective-permute-start | bytes 98312 | tf_op jit(solution)/shard_map/ppermute | solution.py:22
  25.4 4.5 %collective-permute-start = (bf16[1,1,64,256]{3,2,1,0:T(8,128)(2,1)}, bf16[1,1,64,256]{3,2,1,0:T(8,128)(2,1)S(1)}, u32[]{:S(2)}, u32[]{:S(2)}) collective-permute-start(bf16[1,1,64,256]{3,2,1,0:T(8,128)(2,1)} %get-tuple-element.64), channel_id=1, source_target_pairs={{0,4},{4,8},{8,12},{1,5},{5,9},{9,13},{2,6},{6,10},{10,14},{3,7},{... | collective-permute-start | bytes 98312 | tf_op jit(solution)/shard_map/ppermute | solution.py:19
  30.0 1.4 %fusion.53 = (bf16[1,1,64,256]{3,2,1,0:T(8,128)(2,1)}, bf16[1,1,64,256]{3,2,1,0:T(8,128)(2,1)}) fusion(bf16[1,4,64,256]{3,2,1,0:T(8,128)(2,1)} %param.14), kind=kLoop, calls=%fused_computation.107 | loop fusion | bytes 131072 | tf_op jit(solution)/shard_map/slice | solution.py:22
  31.3 1.9 %collective-permute-start.4 = (bf16[1,1,64,256]{3,2,1,0:T(8,128)(2,1)}, bf16[1,1,64,256]{3,2,1,0:T(8,128)(2,1)S(1)}, u32[]{:S(2)}, u32[]{:S(2)}) collective-permute-start(bf16[1,1,64,256]{3,2,1,0:T(8,128)(2,1)} %get-tuple-element.61), channel_id=1, source_target_pairs={{0,4},{4,8},{8,12},{1,5},{5,9},{9,13},{2,6},{6,10},{10,14},{3,7},{... | collective-permute-start | bytes 98312 | tf_op jit(solution)/shard_map/ppermute | solution.py:19
  33.3 1.4 %collective-permute-start.5 = (bf16[1,1,64,256]{3,2,1,0:T(8,128)(2,1)}, bf16[1,1,64,256]{3,2,1,0:T(8,128)(2,1)S(1)}, u32[]{:S(2)}, u32[]{:S(2)}) collective-permute-start(bf16[1,1,64,256]{3,2,1,0:T(8,128)(2,1)} %get-tuple-element.60), channel_id=1, source_target_pairs={{4,0},{8,4},{12,8},{5,1},{9,5},{13,9},{6,2},{10,6},{14,10},{7,3},{... | collective-permute-start | bytes 98312 | tf_op jit(solution)/shard_map/ppermute | solution.py:22
  34.7 2.4 %copy.17 = bf16[3,3,256,256]{2,3,1,0:T(8,128)(2,1)} copy(bf16[3,3,256,256]{3,2,1,0:T(8,128)(2,1)} %param.20) | data formatting | bytes 2359296 | tf_op args[7]
  37.1 1.0 fusion.43
  38.7 1.0 fusion.44
  39.7 1.6 %copy.18 = bf16[3,3,256,256]{2,3,1,0:T(8,128)(2,1)} copy(bf16[3,3,256,256]{3,2,1,0:T(8,128)(2,1)S(1)} %copy-done.2) | data formatting | bytes 2359296 | tf_op args[6]
  42.8 1.0 fusion.42
  43.7 0.6 copy-done.4
  44.7 0.6 copy-done.16
  46.1 0.9 copy-done.12
  48.7 11.0 %all-reduce.6 = (f32[1,512]{1,0:T(1,128)S(1)}, f32[1,32]{1,0:T(1,128)S(1)}, f32[1,32]{1,0:T(1,128)S(1)}) all-reduce(f32[1,512]{1,0:T(1,128)S(1)} %fusion.58, f32[1,32]{1,0:T(1,128)S(1)} %bitcast.134, f32[1,32]{1,0:T(1,128)S(1)} %bitcast.135), channel_id=1, replica_groups=mesh['groups'=2,'tile'=4,'image'=4] {'tile'}, use_global_device_ids=true, to_apply=%region_12.13 | all-reduce | flops 576 | bytes 4608 | tf_op jit(solution)/shard_map/psum | solution.py:133
  60.4 0.9 copy-done.8
  62.6 8.5 %all-reduce.5 = (f32[1,256]{1,0:T(1,128)S(1)}, f32[1,256]{1,0:T(1,128)S(1)}) all-reduce(f32[1,256]{1,0:T(1,128)S(1)} %bitcast.136, f32[1,256]{1,0:T(1,128)S(1)} %bitcast.137), channel_id=1, replica_groups=mesh['groups'=2,'tile'=4,'image'=4] {'tile'}, use_global_device_ids=true, to_apply=%region_14.15 | all-reduce | flops 512 | bytes 4096 | tf_op jit(solution)/shard_map/psum | solution.py:156
  72.1 1.3 %collective-permute-start.3 = (bf16[1,1,64,256]{3,2,1,0:T(8,128)(2,1)S(1)}, bf16[1,1,64,256]{3,2,1,0:T(8,128)(2,1)S(1)}, u32[]{:S(2)}, u32[]{:S(2)}) collective-permute-start(bf16[1,1,64,256]{3,2,1,0:T(8,128)(2,1)S(1)} %get-tuple-element.63), channel_id=1, source_target_pairs={{4,0},{8,4},{12,8},{5,1},{9,5},{13,9},{6,2},{10,6},{14,10},{7,3},{... | collective-permute-start | bytes 98312 | tf_op jit(solution)/shard_map/ppermute | solution.py:22
  73.4 4.5 %collective-permute-start.2 = (bf16[1,1,64,256]{3,2,1,0:T(8,128)(2,1)S(1)}, bf16[1,1,64,256]{3,2,1,0:T(8,128)(2,1)S(1)}, u32[]{:S(2)}, u32[]{:S(2)}) collective-permute-start(bf16[1,1,64,256]{3,2,1,0:T(8,128)(2,1)S(1)} %get-tuple-element.62), channel_id=1, source_target_pairs={{0,4},{4,8},{8,12},{1,5},{5,9},{9,13},{2,6},{6,10},{10,14},{3,7},{... | collective-permute-start | bytes 98312 | tf_op jit(solution)/shard_map/ppermute | solution.py:19
  77.9 0.8 multiply_convert_fusion
  78.7 1.3 %collective-permute-start.7 = (bf16[1,1,64,256]{3,2,1,0:T(8,128)(2,1)S(1)}, bf16[1,1,64,256]{3,2,1,0:T(8,128)(2,1)S(1)}, u32[]{:S(2)}, u32[]{:S(2)}) collective-permute-start(bf16[1,1,64,256]{3,2,1,0:T(8,128)(2,1)S(1)} %get-tuple-element.59), channel_id=1, source_target_pairs={{4,0},{8,4},{12,8},{5,1},{9,5},{13,9},{6,2},{10,6},{14,10},{7,3},{... | collective-permute-start | bytes 98312 | tf_op jit(solution)/shard_map/ppermute | solution.py:22
  80.0 4.5 %collective-permute-start.6 = (bf16[1,1,64,256]{3,2,1,0:T(8,128)(2,1)S(1)}, bf16[1,1,64,256]{3,2,1,0:T(8,128)(2,1)S(1)}, u32[]{:S(2)}, u32[]{:S(2)}) collective-permute-start(bf16[1,1,64,256]{3,2,1,0:T(8,128)(2,1)S(1)} %get-tuple-element.58), channel_id=1, source_target_pairs={{0,4},{4,8},{8,12},{1,5},{5,9},{9,13},{2,6},{6,10},{10,14},{3,7},{... | collective-permute-start | bytes 98312 | tf_op jit(solution)/shard_map/ppermute | solution.py:19
  84.6 5.7 %psum.87 = bf16[512]{0:T(512)(128)(2,1)S(1)} all-reduce(bf16[512]{0:T(512)(128)(2,1)S(1)} %convert_element_type.135), channel_id=1, replica_groups=mesh['groups'=2,'tile'=4,'image'=4] {'image'}, use_global_device_ids=true, to_apply=%region_26.27 | all-reduce | flops 512 | bytes 2048 | tf_op jit(solution)/shard_map/psum | solution.py:179
  91.1 0.9 fusion.47
  94.0 10.2 %all-reduce.4 = (f32[1,32]{1,0:T(1,128)S(1)}, f32[1,32]{1,0:T(1,128)S(1)}) all-reduce(f32[1,32]{1,0:T(1,128)S(1)} %bitcast.138, f32[1,32]{1,0:T(1,128)S(1)} %bitcast.140), channel_id=1, replica_groups=mesh['groups'=2,'tile'=4,'image'=4] {'tile'}, use_global_device_ids=true, to_apply=%region_24.25 | all-reduce | flops 64 | bytes 512 | tf_op jit(solution)/shard_map/psum | solution.py:91
  105.2 0.9 fusion.2
  106.1 0.7 fusion.23
  106.8 9.4 %all-reduce.10.cloned.1.call-done = bf16[256,512]{1,0:T(8,128)(2,1)} async-done(((bf16[256,512]{1,0:T(8,128)(2,1)}), bf16[256,512]{1,0:T(8,128)(2,1)}) %all-reduce.10.cloned.1.call-update) | async-done | bytes 262160 | tf_op jit(solution)/shard_map/psum | solution.py:178
  116.3 1.8 %convert_element_type.134 = f32[256,512]{1,0:T(8,128)} convert(bf16[256,512]{1,0:T(8,128)(2,1)} %all-reduce.10.cloned.1.call-done) | non-fusion elementwise | flops 131072 | bytes 786432 | tf_op jit(solution)/shard_map/convert_element_type | solution.py:178
  (134 shorter events, 10.7 us)
Async XLA Ops:
  7.2 37.4 %copy-start = (bf16[1000,256]{1,0:T(8,128)(2,1)S(1)}, bf16[1000,256]{1,0:T(8,128)(2,1)}, u32[]{:S(2)}) copy-start(bf16[1000,256]{1,0:T(8,128)(2,1)} %param.23) | copy-start | bytes 1536004
  7.2 109.1 %all-reduce.10.cloned.1.call-start = ((), (), s32[]{:S(2)}) async-start(), calls=%async_computation | async-start | bytes 524288 | tf_op jit(solution)/shard_map/psum | solution.py:178
  24.1 21.6 %collective-permute-start.1 = (bf16[1,1,64,256]{3,2,1,0:T(8,128)(2,1)}, bf16[1,1,64,256]{3,2,1,0:T(8,128)(2,1)S(1)}, u32[]{:S(2)}, u32[]{:S(2)}) collective-permute-start(bf16[1,1,64,256]{3,2,1,0:T(8,128)(2,1)} %get-tuple-element.65), channel_id=1, source_target_pairs={{4,0},{8,4},{12,8},{5,1},{9,5},{13,9},{6,2},{10,6},{14,10},{7,3},{... | collective-permute-start | bytes 98312 | tf_op jit(solution)/shard_map/ppermute | solution.py:22
  25.4 20.4 %collective-permute-start = (bf16[1,1,64,256]{3,2,1,0:T(8,128)(2,1)}, bf16[1,1,64,256]{3,2,1,0:T(8,128)(2,1)S(1)}, u32[]{:S(2)}, u32[]{:S(2)}) collective-permute-start(bf16[1,1,64,256]{3,2,1,0:T(8,128)(2,1)} %get-tuple-element.64), channel_id=1, source_target_pairs={{0,4},{4,8},{8,12},{1,5},{5,9},{9,13},{2,6},{6,10},{10,14},{3,7},{... | collective-permute-start | bytes 98312 | tf_op jit(solution)/shard_map/ppermute | solution.py:19
  31.3 28.4 %collective-permute-start.4 = (bf16[1,1,64,256]{3,2,1,0:T(8,128)(2,1)}, bf16[1,1,64,256]{3,2,1,0:T(8,128)(2,1)S(1)}, u32[]{:S(2)}, u32[]{:S(2)}) collective-permute-start(bf16[1,1,64,256]{3,2,1,0:T(8,128)(2,1)} %get-tuple-element.61), channel_id=1, source_target_pairs={{0,4},{4,8},{8,12},{1,5},{5,9},{9,13},{2,6},{6,10},{10,14},{3,7},{... | collective-permute-start | bytes 98312 | tf_op jit(solution)/shard_map/ppermute | solution.py:19
  33.3 3.8 %copy-start.1 = (bf16[3,3,256,256]{3,2,1,0:T(8,128)(2,1)S(1)}, bf16[3,3,256,256]{3,2,1,0:T(8,128)(2,1)}, u32[]{:S(2)}) copy-start(bf16[3,3,256,256]{3,2,1,0:T(8,128)(2,1)} %param.20) | copy-start | bytes 3538948
  33.3 26.8 %collective-permute-start.5 = (bf16[1,1,64,256]{3,2,1,0:T(8,128)(2,1)}, bf16[1,1,64,256]{3,2,1,0:T(8,128)(2,1)S(1)}, u32[]{:S(2)}, u32[]{:S(2)}) collective-permute-start(bf16[1,1,64,256]{3,2,1,0:T(8,128)(2,1)} %get-tuple-element.60), channel_id=1, source_target_pairs={{4,0},{8,4},{12,8},{5,1},{9,5},{13,9},{6,2},{10,6},{14,10},{7,3},{... | collective-permute-start | bytes 98312 | tf_op jit(solution)/shard_map/ppermute | solution.py:22
  37.1 1.6 %copy-start.2 = (bf16[3,3,256,256]{3,2,1,0:T(8,128)(2,1)S(1)}, bf16[3,3,256,256]{3,2,1,0:T(8,128)(2,1)}, u32[]{:S(2)}) copy-start(bf16[3,3,256,256]{3,2,1,0:T(8,128)(2,1)} %param.19) | copy-start | bytes 3538948
  39.7 3.0 %copy-start.3 = (bf16[3,3,256,256]{2,3,1,0:T(8,128)(2,1)S(1)}, bf16[3,3,256,256]{2,3,1,0:T(8,128)(2,1)}, u32[]{:S(2)}) copy-start(bf16[3,3,256,256]{2,3,1,0:T(8,128)(2,1)} %copy.17) | copy-start | bytes 3538948
  42.8 1.6 %copy-start.4 = (bf16[3,3,256,256]{2,3,1,0:T(8,128)(2,1)S(1)}, bf16[3,3,256,256]{2,3,1,0:T(8,128)(2,1)}, u32[]{:S(2)}) copy-start(bf16[3,3,256,256]{2,3,1,0:T(8,128)(2,1)} %copy.18) | copy-start | bytes 3538948
  44.4 0.9 copy-start.16
  44.4 1.0 copy-start.20
  44.4 1.1 copy-start.15
  45.9 1.0 copy-start.12
  46.0 1.3 %copy-start.11 = (bf16[1,3,256,256]{3,2,1,0:T(8,128)(2,1)S(1)}, bf16[1,3,256,256]{3,2,1,0:T(8,128)(2,1)}, u32[]{:S(2)}) copy-start(bf16[1,3,256,256]{3,2,1,0:T(8,128)(2,1)} %get-tuple-element.34) | copy-start | bytes 1179652
  46.9 1.0 copy-start.10
  47.2 12.5 %copy-start.19 = (f32[512]{0:T(512)S(1)}, f32[512]{0:T(512)}, u32[]{:S(2)}) copy-start(f32[512]{0:T(512)} %param.25) | copy-start | bytes 6148
  47.2 12.5 %copy-start.14 = (bf16[1,4,64,256]{3,2,1,0:T(8,128)(2,1)S(1)}, bf16[1,4,64,256]{3,2,1,0:T(8,128)(2,1)}, u32[]{:S(2)}) copy-start(bf16[1,4,64,256]{3,2,1,0:T(8,128)(2,1)} %param.14) | copy-start | bytes 393220
  60.3 1.0 copy-start.8
  61.3 1.0 copy-start.13
  72.1 18.8 %collective-permute-start.3 = (bf16[1,1,64,256]{3,2,1,0:T(8,128)(2,1)S(1)}, bf16[1,1,64,256]{3,2,1,0:T(8,128)(2,1)S(1)}, u32[]{:S(2)}, u32[]{:S(2)}) collective-permute-start(bf16[1,1,64,256]{3,2,1,0:T(8,128)(2,1)S(1)} %get-tuple-element.63), channel_id=1, source_target_pairs={{4,0},{8,4},{12,8},{5,1},{9,5},{13,9},{6,2},{10,6},{14,10},{7,3},{... | collective-permute-start | bytes 98312 | tf_op jit(solution)/shard_map/ppermute | solution.py:22
  73.4 17.5 %collective-permute-start.2 = (bf16[1,1,64,256]{3,2,1,0:T(8,128)(2,1)S(1)}, bf16[1,1,64,256]{3,2,1,0:T(8,128)(2,1)S(1)}, u32[]{:S(2)}, u32[]{:S(2)}) collective-permute-start(bf16[1,1,64,256]{3,2,1,0:T(8,128)(2,1)S(1)} %get-tuple-element.62), channel_id=1, source_target_pairs={{0,4},{4,8},{8,12},{1,5},{5,9},{9,13},{2,6},{6,10},{10,14},{3,7},{... | collective-permute-start | bytes 98312 | tf_op jit(solution)/shard_map/ppermute | solution.py:19
  78.7 13.2 %collective-permute-start.7 = (bf16[1,1,64,256]{3,2,1,0:T(8,128)(2,1)S(1)}, bf16[1,1,64,256]{3,2,1,0:T(8,128)(2,1)S(1)}, u32[]{:S(2)}, u32[]{:S(2)}) collective-permute-start(bf16[1,1,64,256]{3,2,1,0:T(8,128)(2,1)S(1)} %get-tuple-element.59), channel_id=1, source_target_pairs={{4,0},{8,4},{12,8},{5,1},{9,5},{13,9},{6,2},{10,6},{14,10},{7,3},{... | collective-permute-start | bytes 98312 | tf_op jit(solution)/shard_map/ppermute | solution.py:22
  80.0 11.9 %collective-permute-start.6 = (bf16[1,1,64,256]{3,2,1,0:T(8,128)(2,1)S(1)}, bf16[1,1,64,256]{3,2,1,0:T(8,128)(2,1)S(1)}, u32[]{:S(2)}, u32[]{:S(2)}) collective-permute-start(bf16[1,1,64,256]{3,2,1,0:T(8,128)(2,1)S(1)} %get-tuple-element.58), channel_id=1, source_target_pairs={{0,4},{4,8},{8,12},{1,5},{5,9},{9,13},{2,6},{6,10},{10,14},{3,7},{... | collective-permute-start | bytes 98312 | tf_op jit(solution)/shard_map/ppermute | solution.py:19
  92.5 0.9 copy-start.5
  92.5 0.9 copy-start.17
  92.5 0.9 copy-start.18
  92.8 11.8 %copy-start.7 = (bf16[1,3,256,256]{3,2,1,0:T(8,128)(2,1)S(1)}, bf16[1,3,256,256]{3,2,1,0:T(8,128)(2,1)}, u32[]{:S(2)}) copy-start(bf16[1,3,256,256]{3,2,1,0:T(8,128)(2,1)} %get-tuple-element.32) | copy-start | bytes 1179652
  92.8 11.8 %copy-start.9 = (bf16[1,4,64,768]{3,2,1,0:T(8,128)(2,1)S(1)}, bf16[1,4,64,768]{3,2,1,0:T(8,128)(2,1)}, u32[]{:S(2)}) copy-start(bf16[1,4,64,768]{3,2,1,0:T(8,128)(2,1)} %get-tuple-element.44) | copy-start | bytes 1179652
  93.4 11.5 %copy-start.6 = (bf16[1,3,256,256]{3,2,1,0:T(8,128)(2,1)S(1)}, bf16[1,3,256,256]{3,2,1,0:T(8,128)(2,1)}, u32[]{:S(2)}) copy-start(bf16[1,3,256,256]{3,2,1,0:T(8,128)(2,1)} %get-tuple-element.31) | copy-start | bytes 1179652
Sparse Core Ops, SparseCore 0:
  84.7 31.4 all-reduce.9
where the time goes:
time: 126 us; the launch traced here: 125 us
  blocking collectives  48.9 us (39%)
  starting transfers between devices  20.9 us (17%)
  local copies, waits for them, and re-layouts  17.4 us (14%)
  between operations  16 us (13%)
  waiting for transfers between devices  9.47 us (8%)
  other arithmetic  7.85 us (6%)
  matrix products  4.46 us (4%)
    ppermute x4, starting transfers between devices, with_halo(): lax.ppermute(lax.slice_in_dim(block, block.shape[dim] - width, None, axis...  15.6 us
    psum x1, blocking collectives, moments(): first_sum, square_sum = lax.psum((first_sum, square_sum), 'tile')  13.5 us
    psum x1, blocking collectives, body(): modulation = lax.psum(partial_terms, 'tile') + adaptive_bias  11 us
    psum x1, blocking collectives, norm_back_first(): plain_sum, paired_sum = lax.psum((plain_sum, paired_sum), 'tile')  10.2 us
    psum x1, waiting for transfers between devices, body(): lax.psum(local_weight.astype(jnp.bfloat16), 'image').astype(jnp.float32)  9.43 us
    unnamed x46, local copies, waits for them, and re-layouts  8.78 us
    psum x1, blocking collectives, body(): scale_sum, shift_sum = lax.psum((scale_sum, shift_sum), 'tile')  8.47 us
    psum x1, blocking collectives, body(): lax.psum(local_bias.astype(jnp.bfloat16), 'image').astype(jnp.float32)  5.67 us
  transfers between devices with their start and end apart: 9, of which 1 were waited for; matrix products, arithmetic and copies ran while one was open for 14% of the time, Pallas kernels for 0%

commit v1 on v0

v1 whole, which is shorter than its diff:
```python
import functools
import math

import jax
import jax.numpy as jnp
from jax import lax
from jax.experimental import pallas as pl
from jax.experimental.pallas import tpu as pltpu
from jax.sharding import PartitionSpec as P

GN_GROUPS = 32
EPSILON = 1e-05
VMEM_LIMIT = 12 * 1024 * 1024
F32, BF16 = jnp.float32, jnp.bfloat16

STAT_ROWS = 32


def terms(values):
    high = values.astype(BF16).astype(F32)
    rest = values - high
    middle = rest.astype(BF16).astype(F32)
    low = (rest - middle).astype(BF16).astype(F32)
    return jnp.concatenate([high, middle, low, jnp.zeros_like(high)], axis=0).astype(BF16)


def joined(block):
    wide = block.astype(F32)
    return wide[0:8] + (wide[8:16] + wide[16:24])


def rows8(*rows):
    width = rows[0].shape[1]
    index = lax.broadcasted_iota(jnp.int32, (8, width), 0)
    out = jnp.zeros((8, width), F32)
    for place, row in enumerate(rows):
        out = jnp.where(index == place, jnp.broadcast_to(row, (8, width)), out)
    return out


def group_matrix(channels):
    shift = (channels // GN_GROUPS).bit_length() - 1
    row = lax.shift_right_logical(lax.broadcasted_iota(jnp.int32, (channels, channels), 0), shift)
    col = lax.shift_right_logical(lax.broadcasted_iota(jnp.int32, (channels, channels), 1), shift)
    return (row == col).astype(F32).astype(BF16)


def group_sums(rows, groups):
    out = jnp.dot(terms(rows), groups, preferred_element_type=F32)
    return out[0:8] + (out[8:16] + out[16:24])


def tree_sum(parts):
    parts = list(parts)
    while len(parts) > 1:
        parts = [
            parts[i] + parts[i + 1] if i + 1 < len(parts) else parts[i]
            for i in range(0, len(parts), 2)
        ]
    return parts[0]


def local_moments(values, groups, count):
    mean = group_sums(rows8(jnp.sum(values, axis=0, keepdims=True)), groups)[0:1] / count
    centred = values - mean
    spread = group_sums(rows8(jnp.sum(centred * centred, axis=0, keepdims=True)), groups)[0:1]
    return mean, spread


def joint_moments(stats, count):
    tiles = len(stats)
    mean = tree_sum([s[0:1] for s in stats]) / tiles
    spread = tree_sum([s[1:2] + count * (s[0:1] - mean) * (s[0:1] - mean) for s in stats])
    return mean, lax.rsqrt(spread / (count * tiles) + EPSILON)


def sigmoid(values):
    return 1.0 / (1.0 + jnp.exp(-values))


def column_index(cells, cols, channels):
    index = lax.broadcasted_iota(jnp.int32, (cells, channels), 0)
    return lax.bitwise_and(index, cols - 1)


def conv(padded_ref, kernel_ref, cells, cols, flipped):
    parts = []
    for j in range(3):
        total = None
        for i in range(3):
            rows = padded_ref[(2 - i if flipped else i) * cols : (2 - i if flipped else i) * cols + cells]
            weights = kernel_ref[3 * i + j]
            product = lax.dot_general(
                rows,
                weights,
                (((1,), (1 if flipped else 0,)), ((), ())),
                preferred_element_type=F32,
            )
            total = product if total is None else total + product
        parts.append(total)
    if flipped:
        parts = parts[::-1]
    column = column_index(cells, cols, parts[0].shape[1])
    left = jnp.where(column == 0, 0.0, pltpu.roll(parts[0], 1, 0))
    right = jnp.where(column == cols - 1, 0.0, pltpu.roll(parts[2], cells - 1, 0))
    return parts[1] + (left + right)


def stat_list(refs, start, tiles):
    if len(refs) == 1:
        return [joined(refs[0][STAT_ROWS * t : STAT_ROWS * (t + 1)]) for t in range(tiles)]
    return [joined(ref[s : s + STAT_ROWS]) for ref, s in zip(refs, start, strict=True)]


def edges(place_ref, one, three):
    odd = place_ref[1] == 1
    return jnp.where(odd, one, three), jnp.where(odd, three, one)


def starts(place_ref, cells, cols):
    odd = place_ref[1]
    first = pl.multiple_of((1 - odd) * (cells - cols), cols)
    third = pl.multiple_of(odd * (cells - cols), cols)
    return first, third


def first_kernel(dims, place, images, cotangent, one, two, three):
    cells, cols, channels, tiles = dims
    start_one, start_three = starts(place, cells, cols)
    one[0:cols] = images[pl.ds(start_one, cols)]
    one[cols : 2 * cols] = cotangent[pl.ds(start_one, cols)]
    three[0:cols] = images[pl.ds(start_three, cols)]
    three[cols : 2 * cols] = cotangent[pl.ds(start_three, cols)]
    groups = group_matrix(channels)
    mean, spread = local_moments(
        images[...].astype(F32), groups, cells * (channels // GN_GROUPS)
    )
    block = terms(rows8(mean, spread))
    one[2 * cols :] = block
    two[...] = block
    three[2 * cols :] = block


def embed_kernel(sinusoid, row, time_weight, time_bias, adaptive_weight, out):
    channels = adaptive_weight.shape[1] // 2

    def times(vector, weights):
        product = jnp.dot(terms(rows8(vector)), weights, preferred_element_type=F32)
        return (product[0:8] + (product[8:16] + product[16:24]))[0:1]

    hidden = times(sinusoid[...], time_weight[...]) + time_bias[...]
    embedding = hidden * sigmoid(hidden) + row[...]
    activated = embedding * sigmoid(embedding)
    partial = times(activated, adaptive_weight[...])
    out[...] = rows8(partial[:, :channels], partial[:, channels:], activated)


def second_kernel(dims, n_stats, place, images, one, three, weights, gain, bias, embed, *rest):
    cells, cols, channels, tiles = dims
    stat_refs, (hidden, stat, out_one, out_two, out_three, padded) = rest[:n_stats], rest[n_stats:]
    count = cells * (channels // GN_GROUPS)
    mean, inverse = joint_moments(
        stat_list(stat_refs, (0, 2 * cols, 0, 2 * cols), tiles), count
    )
    stat[...] = rows8(mean, inverse)
    above, below = edges(place, one[0:cols], three[0:cols])

    def active(block):
        pre = (block.astype(F32) - mean) * inverse * gain[...] + bias[...]
        return pre * sigmoid(pre)

    padded[0:cols] = jnp.where(place[0] > 0, active(above), 0.0).astype(BF16)
    padded[cols : cols + cells] = active(images[...]).astype(BF16)
    padded[cols + cells :] = jnp.where(place[0] < tiles - 1, active(below), 0.0).astype(BF16)
    rounded = conv(padded, weights, cells, cols, False).astype(BF16)
    hidden[...] = rounded
    mean_two, spread_two = local_moments(rounded.astype(F32), group_matrix(channels), count)
    block = terms(rows8(mean_two, spread_two, embed[0:1], embed[1:2]))
    start_one, start_three = starts(place, cells, cols)
    out_one[0:cols] = hidden[pl.ds(start_one, cols)]
    out_three[0:cols] = hidden[pl.ds(start_three, cols)]
    out_one[cols:] = block
    out_two[...] = block
    out_three[cols:] = block


def grad_kernel(dims, place, cotangent, one, three, weights, out, padded):
    cells, cols, channels, tiles = dims
    above, below = edges(place, one[cols : 2 * cols], three[cols : 2 * cols])
    padded[0:cols] = jnp.where(place[0] > 0, above, jnp.zeros_like(above))
    padded[cols : cols + cells] = cotangent[...]
    padded[cols + cells :] = jnp.where(place[0] < tiles - 1, below, jnp.zeros_like(below))
    out[...] = conv(padded, weights, cells, cols, True)


def third_kernel(dims, n_stats, place, hidden, one, three, grad_active, adaptive_bias, *rest):
    cells, cols, channels, tiles = dims
    stat_refs, (active, grad_norm, stat, out_one, out_two, out_three) = rest[:n_stats], rest[n_stats:]
    count = cells * (channels // GN_GROUPS)
    stats = stat_list(stat_refs, (0, cols, 0, cols), tiles)
    mean, inverse = joint_moments(stats, count)
    modulation = tree_sum(stats)
    factor = 1.0 + (modulation[2:3] + adaptive_bias[:, :channels])
    shift = modulation[3:4] + adaptive_bias[:, channels:]
    stat[...] = rows8(mean, inverse, factor)
    above, below = edges(place, one[0:cols], three[0:cols])

    def pieces(block):
        normed = (block.astype(F32) - mean) * inverse
        pre = normed * factor + shift
        return normed, pre, sigmoid(pre)

    _, pre, gate = pieces(above)
    active[0:cols] = jnp.where(place[0] > 0, pre * gate, 0.0).astype(BF16)
    _, pre, gate = pieces(below)
    active[cols + cells :] = jnp.where(place[0] < tiles - 1, pre * gate, 0.0).astype(BF16)
    normed, pre, gate = pieces(hidden[...])
    active[cols : cols + cells] = (pre * gate).astype(BF16)
    grad_pre = grad_active[...] * (gate * (1.0 + pre * (1.0 - gate)))
    grad_norm[...] = grad_pre * factor
    block = terms(
        rows8(
            jnp.sum(grad_pre * normed, axis=0, keepdims=True),
            jnp.sum(grad_pre, axis=0, keepdims=True),
        )
    )
    start_one, start_three = starts(place, cells, cols)
    out_one[0:cols] = grad_norm[pl.ds(start_one, cols)].astype(BF16)
    out_three[0:cols] = grad_norm[pl.ds(start_three, cols)].astype(BF16)
    out_one[cols:] = block
    out_two[...] = block
    out_three[cols:] = block


def branch_kernel(dims, active, weights, out):
    cells, cols, channels, tiles = dims
    out[...] = conv(active, weights, cells, cols, False).astype(BF16)


def fourth_kernel(
    dims, n_stats, place, grad_norm, one, three, hidden, hidden_one, hidden_three, stat_two,
    weights, images, stat_one, gain, bias, embed, *rest
):
    cells, cols, channels, tiles = dims
    stat_refs, (grad_first, out, pairs, padded) = rest[:n_stats], rest[n_stats:]
    total = cells * (channels // GN_GROUPS) * tiles
    sums = tree_sum(stat_list(stat_refs, (0, cols, 0, cols), tiles))
    pairs[...] = rows8(sums[0:1], sums[1:2], embed[2:3])
    mean, inverse, factor = stat_two[0:1], stat_two[1:2], stat_two[2:3]
    groups = group_matrix(channels)
    means = group_sums(sums * factor, groups) / total
    paired, plain = means[0:1], means[1:2]
    above, below = edges(place, one[0:cols], three[0:cols])
    hidden_above, hidden_below = edges(place, hidden_one[0:cols], hidden_three[0:cols])

    def grad_hidden(grad, block):
        normed = (block.astype(F32) - mean) * inverse
        return inverse * (grad.astype(F32) - plain - normed * paired)

    padded[0:cols] = jnp.where(place[0] > 0, grad_hidden(above, hidden_above), 0.0).astype(BF16)
    padded[cols : cols + cells] = grad_hidden(grad_norm[...], hidden[...]).astype(BF16)
    padded[cols + cells :] = jnp.where(
        place[0] < tiles - 1, grad_hidden(below, hidden_below), 0.0
    ).astype(BF16)
    grad_active = conv(padded, weights, cells, cols, True)
    normed = (images[...].astype(F32) - stat_one[0:1]) * stat_one[1:2]
    pre = normed * gain[...] + bias[...]
    gate = sigmoid(pre)
    grad = grad_active * (gate * (1.0 + pre * (1.0 - gate))) * gain[...]
    grad_first[...] = grad
    sums_first = rows8(
        jnp.sum(grad, axis=0, keepdims=True), jnp.sum(grad * normed, axis=0, keepdims=True)
    )
    out[...] = terms(group_sums(sums_first, groups))


def fifth_kernel(dims, n_stats, grad_first, images, stat_one, *rest):
    cells, cols, channels, tiles = dims
    stat_refs, (out,) = rest[:n_stats], rest[n_stats:]
    total = cells * (channels // GN_GROUPS) * tiles
    means = tree_sum(stat_list(stat_refs, (0, 0, 0, 0), tiles)) / total
    inverse = stat_one[1:2]
    normed = (images[...].astype(F32) - stat_one[0:1]) * inverse
    out[...] = (inverse * (grad_first[...] - means[0:1] - normed * means[1:2])).astype(BF16)


def weight_kernel(index, *rest):
    pair_refs, (weight, bias) = rest[:-2], rest[-2:]
    if len(pair_refs) == 1:
        blocks = [pair_refs[0][8 * n : 8 * n + 8] for n in range(pair_refs[0].shape[0] // 8)]
        places = list(range(len(blocks)))
    else:
        blocks = [ref[...] for ref in pair_refs]
        places = [lax.bitwise_xor(index[0], k) for k in range(len(blocks))]
    count = -(-len(blocks) // 8) * 8
    channels = blocks[0].shape[1]
    row = lax.broadcasted_iota(jnp.int32, (count, channels), 0)

    def ordered(which):
        out = jnp.zeros((count, channels), F32)
        for block, place in zip(blocks, places, strict=True):
            out = jnp.where(row == place, jnp.broadcast_to(block[which : which + 1], out.shape), out)
        return out

    scale, shift, activated = ordered(0), ordered(1), ordered(2)
    for start, part in ((0, scale), (channels, shift)):
        weight[:, start : start + channels] = lax.dot_general(
            activated,
            part,
            (((0,), (0,)), ((), ())),
            precision=lax.Precision.HIGHEST,
            preferred_element_type=F32,
        )
        bias[:, start : start + channels] = jnp.sum(part, axis=0, keepdims=True)


def call(kernel, out_shapes, operands, scratch=(), flops=1000, smem=1, name=None):
    size = sum(o.size * o.dtype.itemsize for o in operands)
    return pl.pallas_call(
        kernel,
        out_shape=out_shapes,
        in_specs=[
            pl.BlockSpec(memory_space=pltpu.SMEM if k < smem else pltpu.VMEM)
            for k in range(len(operands))
        ],
        out_specs=jax.tree.map(lambda _: pl.BlockSpec(memory_space=pltpu.VMEM), out_shapes),
        scratch_shapes=list(scratch),
        compiler_params=pltpu.CompilerParams(vmem_limit_bytes=VMEM_LIMIT),
        cost_estimate=pl.CostEstimate(flops=flops, bytes_accessed=size, transcendentals=0),
        name=name,
    )(*operands)


def swap(values, axis, size, distance):
    return lax.ppermute(values, axis, [(i, i ^ distance) for i in range(size)])


def exchange(one, two, three, stat_start):
    tiles = lax.axis_size("tile")
    if tiles == 4:
        got = [swap(part, "tile", tiles, k + 1) for k, part in enumerate((one, two, three))]
        return got[0], got[2], [two, *got]
    ahead = [(i, (i + 1) % tiles) for i in range(tiles)]
    behind = [(target, source) for source, target in ahead]
    below, above = lax.ppermute(three, "tile", behind), lax.ppermute(one, "tile", ahead)
    return below, above, [lax.all_gather(two, "tile", axis=0, tiled=True)]


def spread_small(block):
    tiles = lax.axis_size("tile")
    if tiles == 4:
        return [block, *(swap(block, "tile", tiles, k) for k in (1, 2, 3))]
    return [lax.all_gather(block, "tile", axis=0, tiled=True)]


def body(
    images,
    cotangent,
    timesteps,
    class_ids,
    norm_gain,
    norm_bias,
    conv_first,
    conv_second,
    time_weight,
    time_bias,
    class_table,
    adaptive_weight,
    adaptive_bias,
):
    _, rows, cols, channels = images.shape
    tiles, fleet = lax.axis_size("tile"), lax.axis_size("image")
    cells = rows * cols
    dims = (cells, cols, channels, tiles)
    tile = lax.axis_index("tile").astype(jnp.int32)
    odd = tile % 2 if tiles == 4 else jnp.zeros_like(tile)
    place = jnp.stack([tile, odd])
    flat = images.reshape(cells, channels)
    flat_cot = cotangent.reshape(cells, channels)
    weights_first = conv_first.reshape(9, channels, channels)
    weights_second = conv_second.reshape(9, channels, channels)
    gain, bias = norm_gain[None], norm_bias[None]
    shape = jax.ShapeDtypeStruct
    conv_flops = 18 * cells * channels * channels
    padded = pltpu.VMEM((cells + 2 * cols, channels), BF16)
    small = shape((STAT_ROWS, channels), BF16)
    halo = shape((cols + STAT_ROWS, channels), BF16)
    halos = shape((2 * cols + STAT_ROWS, channels), BF16)
    block = shape((8, channels), F32)
    wide = shape((cells, channels), F32)
    narrow = shape((cells, channels), BF16)

    one, two, three = call(
        functools.partial(first_kernel, dims), (halos, small, halos), (place, flat, flat_cot), name="first"
    )
    image_one, image_three, stats = exchange(one, two, three, 2 * cols)

    half = time_weight.shape[0] // 2
    frequencies = jnp.exp(-math.log(10000.0) * jnp.arange(half, dtype=F32) / half)
    angles = timesteps.astype(F32)[:, None] * frequencies[None]
    sinusoid = jnp.concatenate([jnp.cos(angles), jnp.sin(angles)], axis=1)
    class_row = lax.dynamic_slice_in_dim(class_table, class_ids[0], 1, axis=0).astype(F32)
    width = adaptive_weight.shape[0]
    spare = channels - width
    time_bias, mix = time_bias[None], adaptive_weight
    if spare:
        time_weight, time_bias, class_row = (
            jnp.pad(part, ((0, 0), (0, spare))) for part in (time_weight, time_bias, class_row)
        )
        mix = jnp.pad(mix, ((0, spare), (0, 0)))
    embed = call(embed_kernel, block, (sinusoid, class_row, time_weight, time_bias, mix), smem=0, name="embed")

    hidden, stat_one, one, two, three = call(
        functools.partial(second_kernel, dims, len(stats)),
        (narrow, block, halo, small, halo),
        (place, flat, image_one, image_three, weights_first, gain, bias, embed, *stats),
        (padded,),
        conv_flops,
        name="second",
    )
    hidden_one, hidden_three, stats = exchange(one, two, three, cols)
    grad_active = call(
        functools.partial(grad_kernel, dims),
        wide,
        (place, flat_cot, image_one, image_three, weights_second),
        (padded,),
        conv_flops,
        name="grad",
    )
    active, grad_norm, stat_two, one, two, three = call(
        functools.partial(third_kernel, dims, len(stats)),
        (shape((cells + 2 * cols, channels), BF16), wide, block, halo, small, halo),
        (place, hidden, hidden_one, hidden_three, grad_active, adaptive_bias[None], *stats),
        flops=1000,
        name="third",
    )
    grad_one, grad_three, stats = exchange(one, two, three, cols)
    branch = call(
        functools.partial(branch_kernel, dims), narrow, (active, weights_second), flops=conv_flops, smem=0, name="branch"
    )
    grad_first, sums, pairs = call(
        functools.partial(fourth_kernel, dims, len(stats)),
        (wide, small, block),
        (place, grad_norm, grad_one, grad_three, hidden, hidden_one, hidden_three, stat_two,
         weights_first, flat, stat_one, gain, bias, embed, *stats),
        (padded,),
        conv_flops,
        name="fourth",
    )
    stats = spread_small(sums)
    if fleet == 4:
        pair_list = [pairs, *(swap(pairs, "image", fleet, k) for k in (1, 2, 3))]
    else:
        pair_list = [lax.all_gather(pairs, "image", axis=0, tiled=True)]
    input_grad = call(
        functools.partial(fifth_kernel, dims, len(stats)), narrow, (grad_first, flat, stat_one, *stats), smem=0, name="fifth"
    )
    image = lax.axis_index("image").astype(jnp.int32)[None]
    grad_weight, grad_bias = call(
        weight_kernel,
        (shape((channels, 2 * channels), F32), shape((1, 2 * channels), F32)),
        (image, *pair_list),
        name="weight",
    )
    return (
        branch.reshape(images.shape),
        input_grad.reshape(images.shape),
        grad_weight[:width],
        grad_bias[0],
    )


def solution(mesh):
    return jax.shard_map(
        body,
        mesh=mesh,
        in_specs=(
            P(("groups", "image"), "tile", None, None),
            P(("groups", "image"), "tile", None, None),
            P(("groups", "image")),
            P(("groups", "image")),
            P(),
            P(),
            P(),
            P(),
            P(None, "tile"),
            P("tile"),
            P(None, "tile"),
            P("tile", None),
            P(),
        ),
        out_specs=(
            P(("groups", "image"), "tile", None, None),
            P(("groups", "image"), "tile", None, None),
            P(("groups", "tile"), None),
            P("groups"),
        ),
        check_vma=False,
    )
```

time: 126 us -> 47.4 us (0.38)
  blocking collectives: 48.9 us -> 0 us
  between operations: 16 us -> 2.1 us
  local copies, waits for them, and re-layouts: 17.4 us -> 7.89 us
  Pallas kernels: 0 us -> 9.31 us
  other arithmetic: 7.85 us -> 0.83 us
  matrix products: 4.46 us -> 0 us
  starting transfers between devices: 20.9 us -> 19.1 us
  waiting for transfers between devices: 9.47 us -> 7.81 us
    psum x5 -> x0, blocking collectives: 48.9 us -> none  [the longest x1 13.5 us: moments(): first_sum, square_sum = lax.psum((first_sum, square_sum), 'tile')]
    psum x1 -> x0, waiting for transfers between devices: 9.43 us -> none  [body(): lax.psum(local_weight.astype(jnp.bfloat16), 'image').astype(jnp.float32)]
    pallas_call x0 -> x9, Pallas kernels: none -> 9.31 us  [call(): pl.pallas_call(kernel, out_shape=out_shapes, in_specs=[pl.BlockSpec(memor...]
    ppermute x8 -> x15, waiting for transfers between devices: 0.02 us -> 7.81 us  [swap(): return lax.ppermute(values, axis, [(i, i ^ distance) for i in range(size)])]
    slice x16 -> x0, local copies, waits for them, and re-layouts: 6.5 us -> none  [the longest x4 3.03 us: conv_rows(): kernel[offset].reshape(3 * channels, -1)]
    dot_general x15 -> x0, matrix products: 4.46 us -> none  [the longest x12 3.94 us: conv_rows(): jnp.dot(row_block, kernel[offset].reshape(3 * channels, -1), preferred_el...]
    convert_element_type x7 -> x1, other arithmetic: 5.14 us -> 0.7 us  [body(): lax.dynamic_slice_in_dim(class_table, class_ids[0], 1, axis=0).astype(F32)]
    reduce_sum x10 -> x0, other arithmetic: 2.16 us -> none  [the longest x1 1.01 us: moments(): first_sum = group_total(jnp.sum(values, axis=(1, 2)))]
  transfers between devices with their start and end apart: 9 -> 15, of which waited for: 1 -> 3; matrix products, arithmetic and copies ran while one was open for 14% -> 2% of each run, Pallas kernels for 0% -> 8%
where the time goes in v1:
time: 47.4 us; the launch traced here: 47 us
  starting transfers between devices  19.1 us (40%)
  Pallas kernels  9.31 us (20%)
  local copies, waits for them, and re-layouts  7.89 us (17%)
  waiting for transfers between devices  7.81 us (16%)
  between operations  2.1 us (4%)
  other arithmetic  0.83 us (2%)
    ppermute x15, starting transfers between devices, swap(): return lax.ppermute(values, axis, [(i, i ^ distance) for i in range(size)])  19.1 us
    pallas_call x9, Pallas kernels, call(): pl.pallas_call(kernel, out_shape=out_shapes, in_specs=[pl.BlockSpec(memor...  9.31 us
    unnamed x30, local copies, waits for them, and re-layouts  7.89 us
    ppermute x15, waiting for transfers between devices, swap(): return lax.ppermute(values, axis, [(i, i ^ distance) for i in range(size)])  7.81 us
  transfers between devices with their start and end apart: 15, of which 3 were waited for; matrix products, arithmetic and copies ran while one was open for 2% of the time, Pallas kernels for 8%

profile of v1, /device:TPU:0, one launch (start us, length us, event | category | flops | bytes accessed | tf_op | source)
XLA Modules:
  0.0 47.0 jit_solution(14535628032091959695)
XLA Ops:
  0.7 0.9 %copy-done.3 = bf16[1,4,64,256]{3,2,1,0:T(8,128)(2,1)S(1)} copy-done((bf16[1,4,64,256]{3,2,1,0:T(8,128)(2,1)S(1)}, bf16[1,4,64,256]{3,2,1,0:T(8,128)(2,1)}, u32[]{:S(2)}) %copy-start.3) | copy-done | bytes 131096
  1.6 0.9 %copy-done.6 = bf16[1,4,64,256]{3,2,1,0:T(8,128)(2,1)S(1)} copy-done((bf16[1,4,64,256]{3,2,1,0:T(8,128)(2,1)S(1)}, bf16[1,4,64,256]{3,2,1,0:T(8,128)(2,1)}, u32[]{:S(2)}) %copy-start.6) | copy-done | bytes 131096
  2.5 0.9 %first.1 = (bf16[160,256]{1,0:T(8,128)(2,1)S(1)}, bf16[32,256]{1,0:T(8,128)(2,1)S(1)}, bf16[160,256]{1,0:T(8,128)(2,1)S(1)}) custom-call(s32[2]{0:T(128)S(1)} %pad_add_fusion.place, bf16[256,256]{1,0:T(8,128)(2,1)S(1)} %bitcast.23, bf16[256,256]{1,0:T(8,128)(2,1)S(1)} %bitcast.27), custom_call_target="tpu_custom_call" | custom-call | flops 1000 | bytes 262152 | tf_op jit(solution)/shard_map/first/pallas_call | solution.py:319
  3.4 4.1 %collective-permute-start.2 = (bf16[32,256]{1,0:T(8,128)(2,1)S(1)}, bf16[32,256]{1,0:T(8,128)(2,1)S(1)}, u32[]{:S(2)}, u32[]{:S(2)}) collective-permute-start(bf16[32,256]{1,0:T(8,128)(2,1)S(1)} %get-tuple-element.25.rest_0_), channel_id=1, source_target_pairs={{0,8},{4,12},{8,0},{12,4},{1,9},{5,13},{9,1},{13,5},{2,10},{6,14},... | collective-permute-start | bytes 49160 | tf_op jit(solution)/shard_map/ppermute | solution.py:335
  7.5 1.6 %collective-permute-start = (bf16[160,256]{1,0:T(8,128)(2,1)S(1)}, bf16[160,256]{1,0:T(8,128)(2,1)S(1)}, u32[]{:S(2)}, u32[]{:S(2)}) collective-permute-start(bf16[160,256]{1,0:T(8,128)(2,1)S(1)} %get-tuple-element.23), channel_id=1, source_target_pairs={{0,4},{4,0},{8,12},{12,8},{1,5},{5,1},{9,13},{13,9},{2,6},{6,2},{1... | collective-permute-start | bytes 245768 | tf_op jit(solution)/shard_map/ppermute | solution.py:335
  10.5 0.7 %dynamic-slice_convert_fusion.row = f32[1,256]{1,0:T(1,128)S(1)} fusion(bf16[1000,256]{1,0:T(8,128)(2,1)} %param.23, s32[]{:T(128)S(6)} %select_n.11), kind=kLoop, calls=%fused_computation.1 | loop fusion | flops 256 | bytes 1540 | tf_op jit(solution)/shard_map/convert_element_type | solution.py:402
  11.2 0.9 %copy-done.8 = bf16[256,512]{1,0:T(8,128)(2,1)S(1)} copy-done((bf16[256,512]{1,0:T(8,128)(2,1)S(1)}, bf16[256,512]{1,0:T(8,128)(2,1)}, u32[]{:S(2)}) %copy-start.8) | copy-done | bytes 262168
  12.1 0.9 %copy-done.9 = bf16[256,256]{1,0:T(8,128)(2,1)S(1)} copy-done((bf16[256,256]{1,0:T(8,128)(2,1)S(1)}, bf16[256,256]{1,0:T(8,128)(2,1)}, u32[]{:S(2)}) %copy-start.9) | copy-done | bytes 131096
  13.0 0.7 %copy-done.14 = f32[256]{0:T(256)S(1)} copy-done((f32[256]{0:T(256)S(1)}, f32[256]{0:T(256)}, u32[]{:S(2)}) %copy-start.14) | copy-done | bytes 1048
  13.7 0.3 embed.1
  14.1 1.3 %collective-permute-done.1.three.rest_3_ = bf16[160,256]{1,0:T(8,128)(2,1)S(1)} collective-permute-done((bf16[160,256]{1,0:T(8,128)(2,1)S(1)}, bf16[160,256]{1,0:T(8,128)(2,1)S(1)}, u32[]{:S(2)}, u32[]{:S(2)}) %collective-permute-start.1) | collective-permute-done | bytes 81952 | tf_op jit(solution)/shard_map/ppermute | solution.py:335
  15.4 1.3 %copy-done.1 = bf16[3,3,256,256]{3,2,1,0:T(8,128)(2,1)S(1)} copy-done((bf16[3,3,256,256]{3,2,1,0:T(8,128)(2,1)S(1)}, bf16[3,3,256,256]{3,2,1,0:T(8,128)(2,1)}, u32[]{:S(2)}) %copy-start.1) | copy-done | bytes 1179672
  16.6 0.9 %copy-done.4 = bf16[1,4,64,256]{3,2,1,0:T(8,128)(2,1)S(1)} copy-done((bf16[1,4,64,256]{3,2,1,0:T(8,128)(2,1)S(1)}, bf16[1,4,64,256]{3,2,1,0:T(8,128)(2,1)}, u32[]{:S(2)}) %copy-start.4) | copy-done | bytes 131096
  17.5 0.7 %copy-done.10 = f32[256]{0:T(256)S(1)} copy-done((f32[256]{0:T(256)S(1)}, f32[256]{0:T(256)}, u32[]{:S(2)}) %copy-start.10) | copy-done | bytes 1048
  18.2 0.7 %copy-done.11 = f32[256]{0:T(256)S(1)} copy-done((f32[256]{0:T(256)S(1)}, f32[256]{0:T(256)}, u32[]{:S(2)}) %copy-start.11) | copy-done | bytes 1048
  18.9 1.4 %second.1 = (bf16[256,256]{1,0:T(8,128)(2,1)S(1)}, f32[8,256]{1,0:T(8,128)S(1)}, bf16[96,256]{1,0:T(8,128)(2,1)S(1)}, bf16[32,256]{1,0:T(8,128)(2,1)S(1)}, bf16[96,256]{1,0:T(8,128)(2,1)S(1)}) custom-call(s32[2]{0:T(128)S(1)} %pad_add_fusion.place, bf16[256,256]{1,0:T(8,128)(2,1)S(1)} %bitcast.24, bf16[160,256]{1,0:T(8,128)(2,1)S(1)} %collective-permute-done.one.rest_1_, ...), custom_call_target="tpu_custom_call" | custom-call | flops 301989888 | bytes 1681416 | tf_op jit(solution)/shard_map/second/pallas_call | solution.py:319
  20.4 2.6 %collective-permute-start.4 = (bf16[96,256]{1,0:T(8,128)(2,1)S(1)}, bf16[96,256]{1,0:T(8,128)(2,1)S(1)}, u32[]{:S(2)}, u32[]{:S(2)}) collective-permute-start(bf16[96,256]{1,0:T(8,128)(2,1)S(1)} %get-tuple-element.28), channel_id=1, source_target_pairs={{0,12},{4,8},{8,4},{12,0},{1,13},{5,9},{9,5},{13,1},{2,14},{6,10},... | collective-permute-start | bytes 147464 | tf_op jit(solution)/shard_map/ppermute | solution.py:335
  23.0 0.8 %collective-permute-start.5 = (bf16[32,256]{1,0:T(8,128)(2,1)S(1)}, bf16[32,256]{1,0:T(8,128)(2,1)S(1)}, u32[]{:S(2)}, u32[]{:S(2)}) collective-permute-start(bf16[32,256]{1,0:T(8,128)(2,1)S(1)} %get-tuple-element.29.rest_0_), channel_id=1, source_target_pairs={{0,8},{4,12},{8,0},{12,4},{1,9},{5,13},{9,1},{13,5},{2,10},{6,14},... | collective-permute-start | bytes 49160 | tf_op jit(solution)/shard_map/ppermute | solution.py:335
  23.9 1.1 %grad.1.grad_active = f32[256,256]{1,0:T(8,128)S(1)} custom-call(s32[2]{0:T(128)S(1)} %pad_add_fusion.place, bf16[256,256]{1,0:T(8,128)(2,1)S(1)} %bitcast.28, bf16[160,256]{1,0:T(8,128)(2,1)S(1)} %collective-permute-done.one.rest_1_, bf16[160,256]{1,0:T(8,128)(2,1)S(1)} %collective-permute-done.1.three.rest_3_, bf16[9,256,256]{2,1,0:T(8,128)(2,1)S(1)} %bitcast.19), custom_call_target="tpu_custom_call" | custom-call | flops 301989888 | bytes 1474568 | tf_op jit(solution)/shard_map/grad/pallas_call | solution.py:319
  25.0 2.7 %collective-permute-done.5.rest_2_ = bf16[32,256]{1,0:T(8,128)(2,1)S(1)} collective-permute-done((bf16[32,256]{1,0:T(8,128)(2,1)S(1)}, bf16[32,256]{1,0:T(8,128)(2,1)S(1)}, u32[]{:S(2)}, u32[]{:S(2)}) %collective-permute-start.5) | collective-permute-done | bytes 16416 | tf_op jit(solution)/shard_map/ppermute | solution.py:335
  27.7 0.9 %third.1 = (bf16[384,256]{1,0:T(8,128)(2,1)S(1)}, f32[256,256]{1,0:T(8,128)S(1)}, f32[8,256]{1,0:T(8,128)S(1)}, bf16[96,256]{1,0:T(8,128)(2,1)S(1)}, bf16[32,256...) custom-call(s32[2]{0:T(128)S(1)} %pad_add_fusion.place, bf16[256,256]{1,0:T(8,128)(2,1)S(1)} %get-tuple-element.26.hidden, ...), custom_call_target="tpu_custom_call" | custom-call | flops 1000 | bytes 624648 | tf_op jit(solution)/shard_map/third/pallas_call | solution.py:319
  28.6 1.1 %collective-permute-start.6 = (bf16[96,256]{1,0:T(8,128)(2,1)S(1)}, bf16[96,256]{1,0:T(8,128)(2,1)S(1)}, u32[]{:S(2)}, u32[]{:S(2)}) collective-permute-start(bf16[96,256]{1,0:T(8,128)(2,1)S(1)} %get-tuple-element.32), channel_id=1, source_target_pairs={{0,4},{4,0},{8,12},{12,8},{1,5},{5,1},{9,13},{13,9},{2,6},{6,2},{1... | collective-permute-start | bytes 147464 | tf_op jit(solution)/shard_map/ppermute | solution.py:335
  29.7 1.3 %collective-permute-start.7 = (bf16[96,256]{1,0:T(8,128)(2,1)S(1)}, bf16[96,256]{1,0:T(8,128)(2,1)S(1)}, u32[]{:S(2)}, u32[]{:S(2)}) collective-permute-start(bf16[96,256]{1,0:T(8,128)(2,1)S(1)} %get-tuple-element.33), channel_id=1, source_target_pairs={{0,12},{4,8},{8,4},{12,0},{1,13},{5,9},{9,5},{13,1},{2,14},{6,10},... | collective-permute-start | bytes 147464 | tf_op jit(solution)/shard_map/ppermute | solution.py:335
  30.9 1.2 %collective-permute-start.8 = (bf16[32,256]{1,0:T(8,128)(2,1)S(1)}, bf16[32,256]{1,0:T(8,128)(2,1)S(1)}, u32[]{:S(2)}, u32[]{:S(2)}) collective-permute-start(bf16[32,256]{1,0:T(8,128)(2,1)S(1)} %get-tuple-element.36.rest_0_), channel_id=1, source_target_pairs={{0,8},{4,12},{8,0},{12,4},{1,9},{5,13},{9,1},{13,5},{2,10},{6,14},... | collective-permute-start | bytes 49160 | tf_op jit(solution)/shard_map/ppermute | solution.py:335
  32.1 3.8 %collective-permute-done.8.rest_2_ = bf16[32,256]{1,0:T(8,128)(2,1)S(1)} collective-permute-done((bf16[32,256]{1,0:T(8,128)(2,1)S(1)}, bf16[32,256]{1,0:T(8,128)(2,1)S(1)}, u32[]{:S(2)}, u32[]{:S(2)}) %collective-permute-start.8) | collective-permute-done | bytes 16416 | tf_op jit(solution)/shard_map/ppermute | solution.py:335
  35.9 1.4 %fourth.1 = (f32[256,256]{1,0:T(8,128)S(1)}, bf16[32,256]{1,0:T(8,128)(2,1)S(1)}, f32[8,256]{1,0:T(8,128)S(1)}) custom-call(s32[2]{0:T(128)S(1)} %pad_add_fusion.place, f32[256,256]{1,0:T(8,128)S(1)} %get-tuple-element.31.grad_norm, bf16[96,256]{1,0:T(8,128)(2,1)S(1)} %collective-permute-done.6.one.rest_1_, ...), custom_call_target="tpu_custom_call" | custom-call | flops 301989888 | bytes 2058248 | tf_op jit(solution)/shard_map/fourth/pallas_call | solution.py:319
  37.5 1.6 %collective-permute-start.13 = (f32[8,256]{1,0:T(8,128)S(1)}, f32[8,256]{1,0:T(8,128)S(1)}, u32[]{:S(2)}, u32[]{:S(2)}) collective-permute-start(f32[8,256]{1,0:T(8,128)S(1)} %get-tuple-element.39.rest_0_), channel_id=1, source_target_pairs={{0,2},{1,3},{2,0},{3,1},{4,6},{5,7},{6,4},{7,5},{8,10},{9,11},{10,... | collective-permute-start | bytes 24584 | tf_op jit(solution)/shard_map/ppermute | solution.py:335
  39.3 2.2 %collective-permute-start.11 = (bf16[32,256]{1,0:T(8,128)(2,1)S(1)}, bf16[32,256]{1,0:T(8,128)(2,1)S(1)}, u32[]{:S(2)}, u32[]{:S(2)}) collective-permute-start(bf16[32,256]{1,0:T(8,128)(2,1)S(1)} %get-tuple-element.38.rest_0_), channel_id=1, source_target_pairs={{0,12},{4,8},{8,4},{12,0},{1,13},{5,9},{9,5},{13,1},{2,14},{6,10},... | collective-permute-start | bytes 49160 | tf_op jit(solution)/shard_map/ppermute | solution.py:335
  41.6 2.2 %collective-permute-start.9 = (bf16[32,256]{1,0:T(8,128)(2,1)S(1)}, bf16[32,256]{1,0:T(8,128)(2,1)S(1)}, u32[]{:S(2)}, u32[]{:S(2)}) collective-permute-start(bf16[32,256]{1,0:T(8,128)(2,1)S(1)} %get-tuple-element.38.rest_0_), channel_id=1, source_target_pairs={{0,4},{4,0},{8,12},{12,8},{1,5},{5,1},{9,13},{13,9},{2,6},{6,2},{1... | collective-permute-start | bytes 49160 | tf_op jit(solution)/shard_map/ppermute | solution.py:335
  43.7 1.1 %branch.1 = bf16[256,256]{1,0:T(8,128)(2,1)} custom-call(bf16[384,256]{1,0:T(8,128)(2,1)S(1)} %get-tuple-element.30.active, bf16[9,256,256]{2,1,0:T(8,128)(2,1)S(1)} %bitcast.20), custom_call_target="tpu_custom_call" | custom-call | flops 301989888 | bytes 1376256 | tf_op jit(solution)/shard_map/branch/pallas_call | solution.py:319
  44.9 1.4 %weight.1 = (f32[256,512]{1,0:T(8,128)}, f32[1,512]{1,0:T(1,128)}) custom-call(s32[1]{0:T(128)} %bitcast.14.index, f32[8,256]{1,0:T(8,128)S(1)} %get-tuple-element.39.rest_0_, f32[8,256]{1,0:T(8,128)S(1)} %collective-permute-done.12.rest_1_, f32[8,256]{1,0:T(8,128)S(1)} %collective-permute-done.13.rest_2_, f32[8,256]{1,0:T(8,128)S(1)} %collective-permute-done.14.rest_3_), custom_call_target="tpu_custom_call" | custom-call | flops 1000 | bytes 32772 | tf_op jit(solution)/shard_map/weight/pallas_call | solution.py:319
  46.3 0.7 %fifth.1 = bf16[256,256]{1,0:T(8,128)(2,1)} custom-call(f32[256,256]{1,0:T(8,128)S(1)} %get-tuple-element.37.grad_first, bf16[256,256]{1,0:T(8,128)(2,1)S(1)} %bitcast.26, f32[8,256]{1,0:T(8,128)S(1)} %get-tuple-element.35.stat_one, bf16[32,256]{1,0:T(8,128)(2,1)S(1)} %get-tuple-element.38.rest_0_, bf16[32,256]{1,0:T(8,128)(2,1)S(1)} %collective-permute-done.9.rest_1_, ...), custom_call_target="tpu_custom_call" | custom-call | flops 1000 | bytes 466944 | tf_op jit(solution)/shard_map/fifth/pallas_call | solution.py:319
  (41 shorter events, 0.7 us)
Async XLA Ops:
  0.7 0.9 %copy-start.3 = (bf16[1,4,64,256]{3,2,1,0:T(8,128)(2,1)S(1)}, bf16[1,4,64,256]{3,2,1,0:T(8,128)(2,1)}, u32[]{:S(2)}) copy-start(bf16[1,4,64,256]{3,2,1,0:T(8,128)(2,1)} %param.13) | copy-start | bytes 393220
  1.6 0.9 %copy-start.6 = (bf16[1,4,64,256]{3,2,1,0:T(8,128)(2,1)S(1)}, bf16[1,4,64,256]{3,2,1,0:T(8,128)(2,1)}, u32[]{:S(2)}) copy-start(bf16[1,4,64,256]{3,2,1,0:T(8,128)(2,1)} %param.14) | copy-start | bytes 393220
  2.5 21.4 %copy-start = (bf16[3,3,256,256]{3,2,1,0:T(8,128)(2,1)S(1)}, bf16[3,3,256,256]{3,2,1,0:T(8,128)(2,1)}, u32[]{:S(2)}) copy-start(bf16[3,3,256,256]{3,2,1,0:T(8,128)(2,1)} %param.20) | copy-start | bytes 3538948
  3.4 10.6 %collective-permute-start.2 = (bf16[32,256]{1,0:T(8,128)(2,1)S(1)}, bf16[32,256]{1,0:T(8,128)(2,1)S(1)}, u32[]{:S(2)}, u32[]{:S(2)}) collective-permute-start(bf16[32,256]{1,0:T(8,128)(2,1)S(1)} %get-tuple-element.25.rest_0_), channel_id=1, source_target_pairs={{0,8},{4,12},{8,0},{12,4},{1,9},{5,13},{9,1},{13,5},{2,10},{6,14},... | collective-permute-start | bytes 49160 | tf_op jit(solution)/shard_map/ppermute | solution.py:335
  7.5 6.5 %collective-permute-start = (bf16[160,256]{1,0:T(8,128)(2,1)S(1)}, bf16[160,256]{1,0:T(8,128)(2,1)S(1)}, u32[]{:S(2)}, u32[]{:S(2)}) collective-permute-start(bf16[160,256]{1,0:T(8,128)(2,1)S(1)} %get-tuple-element.23), channel_id=1, source_target_pairs={{0,4},{4,0},{8,12},{12,8},{1,5},{5,1},{9,13},{13,9},{2,6},{6,2},{1... | collective-permute-start | bytes 245768 | tf_op jit(solution)/shard_map/ppermute | solution.py:335
  9.1 6.2 %collective-permute-start.1 = (bf16[160,256]{1,0:T(8,128)(2,1)S(1)}, bf16[160,256]{1,0:T(8,128)(2,1)S(1)}, u32[]{:S(2)}, u32[]{:S(2)}) collective-permute-start(bf16[160,256]{1,0:T(8,128)(2,1)S(1)} %get-tuple-element.24), channel_id=1, source_target_pairs={{0,12},{4,8},{8,4},{12,0},{1,13},{5,9},{9,5},{13,1},{2,14},{6,10},... | collective-permute-start | bytes 245768 | tf_op jit(solution)/shard_map/ppermute | solution.py:335
  11.2 0.9 %copy-start.8 = (bf16[256,512]{1,0:T(8,128)(2,1)S(1)}, bf16[256,512]{1,0:T(8,128)(2,1)}, u32[]{:S(2)}) copy-start(bf16[256,512]{1,0:T(8,128)(2,1)} %adaptive_weight.1) | copy-start | bytes 786436
  12.1 0.9 %copy-start.9 = (bf16[256,256]{1,0:T(8,128)(2,1)S(1)}, bf16[256,256]{1,0:T(8,128)(2,1)}, u32[]{:S(2)}) copy-start(bf16[256,256]{1,0:T(8,128)(2,1)} %time_weight.1) | copy-start | bytes 393220
  13.0 0.7 %copy-start.14 = (f32[256]{0:T(256)S(1)}, f32[256]{0:T(256)}, u32[]{:S(2)}) copy-start(f32[256]{0:T(256)} %param.22) | copy-start | bytes 3076
  15.4 1.3 %copy-start.1 = (bf16[3,3,256,256]{3,2,1,0:T(8,128)(2,1)S(1)}, bf16[3,3,256,256]{3,2,1,0:T(8,128)(2,1)}, u32[]{:S(2)}) copy-start(bf16[3,3,256,256]{3,2,1,0:T(8,128)(2,1)} %param.19) | copy-start | bytes 3538948
  16.6 0.9 %copy-start.4 = (bf16[1,4,64,256]{3,2,1,0:T(8,128)(2,1)S(1)}, bf16[1,4,64,256]{3,2,1,0:T(8,128)(2,1)}, u32[]{:S(2)}) copy-start(bf16[1,4,64,256]{3,2,1,0:T(8,128)(2,1)} %param.13) | copy-start | bytes 393220
  17.5 0.7 %copy-start.10 = (f32[256]{0:T(256)S(1)}, f32[256]{0:T(256)}, u32[]{:S(2)}) copy-start(f32[256]{0:T(256)} %param.17) | copy-start | bytes 3076
  18.2 0.7 %copy-start.11 = (f32[256]{0:T(256)S(1)}, f32[256]{0:T(256)}, u32[]{:S(2)}) copy-start(f32[256]{0:T(256)} %param.18) | copy-start | bytes 3076
  18.9 5.0 %copy-start.7 = (bf16[1,4,64,256]{3,2,1,0:T(8,128)(2,1)S(1)}, bf16[1,4,64,256]{3,2,1,0:T(8,128)(2,1)}, u32[]{:S(2)}) copy-start(bf16[1,4,64,256]{3,2,1,0:T(8,128)(2,1)} %param.14) | copy-start | bytes 393220
  20.3 7.4 %copy-start.13 = (f32[512]{0:T(512)S(1)}, f32[512]{0:T(512)}, u32[]{:S(2)}) copy-start(f32[512]{0:T(512)} %param.25) | copy-start | bytes 6148
  20.3 7.3 %collective-permute-start.3 = (bf16[96,256]{1,0:T(8,128)(2,1)S(1)}, bf16[96,256]{1,0:T(8,128)(2,1)S(1)}, u32[]{:S(2)}, u32[]{:S(2)}) collective-permute-start(bf16[96,256]{1,0:T(8,128)(2,1)S(1)} %get-tuple-element.27), channel_id=1, source_target_pairs={{0,4},{4,0},{8,12},{12,8},{1,5},{5,1},{9,13},{13,9},{2,6},{6,2},{1... | collective-permute-start | bytes 147464 | tf_op jit(solution)/shard_map/ppermute | solution.py:335
  20.4 7.3 %collective-permute-start.4 = (bf16[96,256]{1,0:T(8,128)(2,1)S(1)}, bf16[96,256]{1,0:T(8,128)(2,1)S(1)}, u32[]{:S(2)}, u32[]{:S(2)}) collective-permute-start(bf16[96,256]{1,0:T(8,128)(2,1)S(1)} %get-tuple-element.28), channel_id=1, source_target_pairs={{0,12},{4,8},{8,4},{12,0},{1,13},{5,9},{9,5},{13,1},{2,14},{6,10},... | collective-permute-start | bytes 147464 | tf_op jit(solution)/shard_map/ppermute | solution.py:335
  23.0 4.6 %collective-permute-start.5 = (bf16[32,256]{1,0:T(8,128)(2,1)S(1)}, bf16[32,256]{1,0:T(8,128)(2,1)S(1)}, u32[]{:S(2)}, u32[]{:S(2)}) collective-permute-start(bf16[32,256]{1,0:T(8,128)(2,1)S(1)} %get-tuple-element.29.rest_0_), channel_id=1, source_target_pairs={{0,8},{4,12},{8,0},{12,4},{1,9},{5,13},{9,1},{13,5},{2,10},{6,14},... | collective-permute-start | bytes 49160 | tf_op jit(solution)/shard_map/ppermute | solution.py:335
  23.9 12.0 %copy-start.2 = (bf16[3,3,256,256]{3,2,1,0:T(8,128)(2,1)S(1)}, bf16[3,3,256,256]{3,2,1,0:T(8,128)(2,1)}, u32[]{:S(2)}) copy-start(bf16[3,3,256,256]{3,2,1,0:T(8,128)(2,1)} %param.19) | copy-start | bytes 3538948
  23.9 12.0 %copy-start.5 = (bf16[1,4,64,256]{3,2,1,0:T(8,128)(2,1)S(1)}, bf16[1,4,64,256]{3,2,1,0:T(8,128)(2,1)}, u32[]{:S(2)}) copy-start(bf16[1,4,64,256]{3,2,1,0:T(8,128)(2,1)} %param.13) | copy-start | bytes 393220
  23.9 12.0 %copy-start.12 = (f32[256]{0:T(256)S(1)}, f32[256]{0:T(256)}, u32[]{:S(2)}) copy-start(f32[256]{0:T(256)} %param.18) | copy-start | bytes 3076
  28.6 7.4 %collective-permute-start.6 = (bf16[96,256]{1,0:T(8,128)(2,1)S(1)}, bf16[96,256]{1,0:T(8,128)(2,1)S(1)}, u32[]{:S(2)}, u32[]{:S(2)}) collective-permute-start(bf16[96,256]{1,0:T(8,128)(2,1)S(1)} %get-tuple-element.32), channel_id=1, source_target_pairs={{0,4},{4,0},{8,12},{12,8},{1,5},{5,1},{9,13},{13,9},{2,6},{6,2},{1... | collective-permute-start | bytes 147464 | tf_op jit(solution)/shard_map/ppermute | solution.py:335
  29.7 6.2 %collective-permute-start.7 = (bf16[96,256]{1,0:T(8,128)(2,1)S(1)}, bf16[96,256]{1,0:T(8,128)(2,1)S(1)}, u32[]{:S(2)}, u32[]{:S(2)}) collective-permute-start(bf16[96,256]{1,0:T(8,128)(2,1)S(1)} %get-tuple-element.33), channel_id=1, source_target_pairs={{0,12},{4,8},{8,4},{12,0},{1,13},{5,9},{9,5},{13,1},{2,14},{6,10},... | collective-permute-start | bytes 147464 | tf_op jit(solution)/shard_map/ppermute | solution.py:335
  30.9 5.0 %collective-permute-start.8 = (bf16[32,256]{1,0:T(8,128)(2,1)S(1)}, bf16[32,256]{1,0:T(8,128)(2,1)S(1)}, u32[]{:S(2)}, u32[]{:S(2)}) collective-permute-start(bf16[32,256]{1,0:T(8,128)(2,1)S(1)} %get-tuple-element.36.rest_0_), channel_id=1, source_target_pairs={{0,8},{4,12},{8,0},{12,4},{1,9},{5,13},{9,1},{13,5},{2,10},{6,14},... | collective-permute-start | bytes 49160 | tf_op jit(solution)/shard_map/ppermute | solution.py:335
  37.4 4.2 %collective-permute-start.14 = (f32[8,256]{1,0:T(8,128)S(1)}, f32[8,256]{1,0:T(8,128)S(1)}, u32[]{:S(2)}, u32[]{:S(2)}) collective-permute-start(f32[8,256]{1,0:T(8,128)S(1)} %get-tuple-element.39.rest_0_), channel_id=1, source_target_pairs={{0,3},{1,2},{2,1},{3,0},{4,7},{5,6},{6,5},{7,4},{8,11},{9,10},{10,... | collective-permute-start | bytes 24584 | tf_op jit(solution)/shard_map/ppermute | solution.py:335
  37.5 7.4 %collective-permute-start.13 = (f32[8,256]{1,0:T(8,128)S(1)}, f32[8,256]{1,0:T(8,128)S(1)}, u32[]{:S(2)}, u32[]{:S(2)}) collective-permute-start(f32[8,256]{1,0:T(8,128)S(1)} %get-tuple-element.39.rest_0_), channel_id=1, source_target_pairs={{0,2},{1,3},{2,0},{3,1},{4,6},{5,7},{6,4},{7,5},{8,10},{9,11},{10,... | collective-permute-start | bytes 24584 | tf_op jit(solution)/shard_map/ppermute | solution.py:335
  39.0 5.8 %collective-permute-start.12 = (f32[8,256]{1,0:T(8,128)S(1)}, f32[8,256]{1,0:T(8,128)S(1)}, u32[]{:S(2)}, u32[]{:S(2)}) collective-permute-start(f32[8,256]{1,0:T(8,128)S(1)} %get-tuple-element.39.rest_0_), channel_id=1, source_target_pairs={{0,1},{1,0},{2,3},{3,2},{4,5},{5,4},{6,7},{7,6},{8,9},{9,8},{10,11... | collective-permute-start | bytes 24584 | tf_op jit(solution)/shard_map/ppermute | solution.py:335
  39.3 7.0 %collective-permute-start.11 = (bf16[32,256]{1,0:T(8,128)(2,1)S(1)}, bf16[32,256]{1,0:T(8,128)(2,1)S(1)}, u32[]{:S(2)}, u32[]{:S(2)}) collective-permute-start(bf16[32,256]{1,0:T(8,128)(2,1)S(1)} %get-tuple-element.38.rest_0_), channel_id=1, source_target_pairs={{0,12},{4,8},{8,4},{12,0},{1,13},{5,9},{9,5},{13,1},{2,14},{6,10},... | collective-permute-start | bytes 49160 | tf_op jit(solution)/shard_map/ppermute | solution.py:335
  41.5 4.7 %collective-permute-start.10 = (bf16[32,256]{1,0:T(8,128)(2,1)S(1)}, bf16[32,256]{1,0:T(8,128)(2,1)S(1)}, u32[]{:S(2)}, u32[]{:S(2)}) collective-permute-start(bf16[32,256]{1,0:T(8,128)(2,1)S(1)} %get-tuple-element.38.rest_0_), channel_id=1, source_target_pairs={{0,8},{4,12},{8,0},{12,4},{1,9},{5,13},{9,1},{13,5},{2,10},{6,14},... | collective-permute-start | bytes 49160 | tf_op jit(solution)/shard_map/ppermute | solution.py:335
  41.6 4.7 %collective-permute-start.9 = (bf16[32,256]{1,0:T(8,128)(2,1)S(1)}, bf16[32,256]{1,0:T(8,128)(2,1)S(1)}, u32[]{:S(2)}, u32[]{:S(2)}) collective-permute-start(bf16[32,256]{1,0:T(8,128)(2,1)S(1)} %get-tuple-element.38.rest_0_), channel_id=1, source_target_pairs={{0,4},{4,0},{8,12},{12,8},{1,5},{5,1},{9,13},{13,9},{2,6},{6,2},{1... | collective-permute-start | bytes 49160 | tf_op jit(solution)/shard_map/ppermute | solution.py:335

commit v2 on v1

--- a/solution.py
+++ b/solution.py
@@ -112,51 +112,82 @@
     return [joined(ref[s : s + STAT_ROWS]) for ref, s in zip(refs, start, strict=True)]
 
 
-def edges(place_ref, one, three):
-    odd = place_ref[1] == 1
+def standing(tiles):
+    tile = lax.axis_index("tile")
+    return tile, lax.bitwise_and(tile, 1) if tiles == 4 else 0 * tile
+
+
+def edges(place, one, three):
+    odd = place[1] == 1
     return jnp.where(odd, one, three), jnp.where(odd, three, one)
 
 
-def starts(place_ref, cells, cols):
-    odd = place_ref[1]
+def starts(place, cells, cols):
+    odd = place[1]
     first = pl.multiple_of((1 - odd) * (cells - cols), cols)
     third = pl.multiple_of(odd * (cells - cols), cols)
     return first, third
 
 
-def first_kernel(dims, place, images, cotangent, one, two, three):
-    cells, cols, channels, tiles = dims
+def first_kernel(dims, *refs):
+    cells, cols, channels, tiles = dims
+    count = (len(refs) - 7) // 2
+    sources, step, label = refs[:count], refs[count], refs[count + 1]
+    copies_to = refs[count + 2 : 2 * count + 2]
+    one, two, three, instant, sems = refs[2 * count + 2 :]
+    copies = [
+        pltpu.make_async_copy(source, target, sems.at[k])
+        for k, (source, target) in enumerate(zip(sources, copies_to, strict=True))
+    ]
+    for copy in copies:
+        copy.start()
+    images, cotangent = copies_to[:2]
+    place = standing(tiles)
     start_one, start_three = starts(place, cells, cols)
-    one[0:cols] = images[pl.ds(start_one, cols)]
-    one[cols : 2 * cols] = cotangent[pl.ds(start_one, cols)]
-    three[0:cols] = images[pl.ds(start_three, cols)]
-    three[cols : 2 * cols] = cotangent[pl.ds(start_three, cols)]
     groups = group_matrix(channels)
+    copies[0].wait()
     mean, spread = local_moments(
         images[...].astype(F32), groups, cells * (channels // GN_GROUPS)
     )
+    one[0:cols] = images[pl.ds(start_one, cols)]
+    three[0:cols] = images[pl.ds(start_three, cols)]
+    copies[1].wait()
+    one[cols : 2 * cols] = cotangent[pl.ds(start_one, cols)]
+    three[cols : 2 * cols] = cotangent[pl.ds(start_three, cols)]
     block = terms(rows8(mean, spread))
     one[2 * cols :] = block
     two[...] = block
     three[2 * cols :] = block
-
-
-def embed_kernel(sinusoid, row, time_weight, time_bias, adaptive_weight, out):
+    for copy in copies[2:]:
+        copy.wait()
+    row = lax.broadcasted_iota(jnp.int32, instant.shape, 0)
+    instant[...] = jnp.where(row == 0, step[0], label[0])
+
+
+def embed_kernel(instant, table, time_weight, time_bias, adaptive_weight, out):
     channels = adaptive_weight.shape[1] // 2
+    half = time_weight.shape[0] // 2
 
     def times(vector, weights):
         product = jnp.dot(terms(rows8(vector)), weights, preferred_element_type=F32)
         return (product[0:8] + (product[8:16] + product[16:24]))[0:1]
 
-    hidden = times(sinusoid[...], time_weight[...]) + time_bias[...]
-    embedding = hidden * sigmoid(hidden) + row[...]
+    place = lax.broadcasted_iota(jnp.int32, (8, half), 1).astype(F32)
+    angles = instant[0:1, 0:1].astype(F32) * jnp.exp(-math.log(10000.0) * place / half)
+    sinusoid = jnp.concatenate([jnp.cos(angles), jnp.sin(angles)], axis=1)[0:1]
+    classes = lax.broadcasted_iota(jnp.int32, (16, table.shape[0]), 1)
+    onehot = (classes == instant[1:2, 0:1]).astype(F32).astype(BF16)
+    row = jnp.dot(onehot, table[...], preferred_element_type=F32)[0:1]
+    hidden = times(sinusoid, time_weight[...]) + time_bias[...]
+    embedding = hidden * sigmoid(hidden) + row
     activated = embedding * sigmoid(embedding)
     partial = times(activated, adaptive_weight[...])
     out[...] = rows8(partial[:, :channels], partial[:, channels:], activated)
 
 
-def second_kernel(dims, n_stats, place, images, one, three, weights, gain, bias, embed, *rest):
-    cells, cols, channels, tiles = dims
+def second_kernel(dims, n_stats, images, one, three, weights, gain, bias, embed, *rest):
+    cells, cols, channels, tiles = dims
+    place = standing(tiles)
     stat_refs, (hidden, stat, out_one, out_two, out_three, padded) = rest[:n_stats], rest[n_stats:]
     count = cells * (channels // GN_GROUPS)
     mean, inverse = joint_moments(
@@ -184,8 +215,9 @@
     out_three[cols:] = block
 
 
-def grad_kernel(dims, place, cotangent, one, three, weights, out, padded):
-    cells, cols, channels, tiles = dims
+def grad_kernel(dims, cotangent, one, three, weights, out, padded):
+    cells, cols, channels, tiles = dims
+    place = standing(tiles)
     above, below = edges(place, one[cols : 2 * cols], three[cols : 2 * cols])
     padded[0:cols] = jnp.where(place[0] > 0, above, jnp.zeros_like(above))
     padded[cols : cols + cells] = cotangent[...]
@@ -193,8 +225,9 @@
     out[...] = conv(padded, weights, cells, cols, True)
 
 
-def third_kernel(dims, n_stats, place, hidden, one, three, grad_active, adaptive_bias, *rest):
-    cells, cols, channels, tiles = dims
+def third_kernel(dims, n_stats, hidden, one, three, grad_active, adaptive_bias, *rest):
+    cells, cols, channels, tiles = dims
+    place = standing(tiles)
     stat_refs, (active, grad_norm, stat, out_one, out_two, out_three) = rest[:n_stats], rest[n_stats:]
     count = cells * (channels // GN_GROUPS)
     stats = stat_list(stat_refs, (0, cols, 0, cols), tiles)
@@ -238,10 +271,11 @@
 
 
 def fourth_kernel(
-    dims, n_stats, place, grad_norm, one, three, hidden, hidden_one, hidden_three, stat_two,
+    dims, n_stats, branch, grad_norm, one, three, hidden, hidden_one, hidden_three, stat_two,
     weights, images, stat_one, gain, bias, embed, *rest
 ):
     cells, cols, channels, tiles = dims
+    place = standing(tiles)
     stat_refs, (grad_first, out, pairs, padded) = rest[:n_stats], rest[n_stats:]
     total = cells * (channels // GN_GROUPS) * tiles
     sums = tree_sum(stat_list(stat_refs, (0, cols, 0, cols), tiles))
@@ -284,14 +318,14 @@
     out[...] = (inverse * (grad_first[...] - means[0:1] - normed * means[1:2])).astype(BF16)
 
 
-def weight_kernel(index, *rest):
+def weight_kernel(*rest):
     pair_refs, (weight, bias) = rest[:-2], rest[-2:]
     if len(pair_refs) == 1:
         blocks = [pair_refs[0][8 * n : 8 * n + 8] for n in range(pair_refs[0].shape[0] // 8)]
         places = list(range(len(blocks)))
     else:
         blocks = [ref[...] for ref in pair_refs]
-        places = [lax.bitwise_xor(index[0], k) for k in range(len(blocks))]
+        places = [lax.bitwise_xor(lax.axis_index("image"), k) for k in range(len(blocks))]
     count = -(-len(blocks) // 8) * 8
     channels = blocks[0].shape[1]
     row = lax.broadcasted_iota(jnp.int32, (count, channels), 0)
@@ -314,14 +348,13 @@
         bias[:, start : start + channels] = jnp.sum(part, axis=0, keepdims=True)
 
 
-def call(kernel, out_shapes, operands, scratch=(), flops=1000, smem=1, name=None):
+def call(kernel, out_shapes, operands, scratch=(), flops=1000, name=None, spaces=None):
     size = sum(o.size * o.dtype.itemsize for o in operands)
     return pl.pallas_call(
         kernel,
         out_shape=out_shapes,
         in_specs=[
-            pl.BlockSpec(memory_space=pltpu.SMEM if k < smem else pltpu.VMEM)
-            for k in range(len(operands))
+            pl.BlockSpec(memory_space=(spaces or {}).get(k, pltpu.VMEM)) for k in range(len(operands))
         ],
         out_specs=jax.tree.map(lambda _: pl.BlockSpec(memory_space=pltpu.VMEM), out_shapes),
         scratch_shapes=list(scratch),
@@ -372,14 +405,6 @@
     tiles, fleet = lax.axis_size("tile"), lax.axis_size("image")
     cells = rows * cols
     dims = (cells, cols, channels, tiles)
-    tile = lax.axis_index("tile").astype(jnp.int32)
-    odd = tile % 2 if tiles == 4 else jnp.zeros_like(tile)
-    place = jnp.stack([tile, odd])
-    flat = images.reshape(cells, channels)
-    flat_cot = cotangent.reshape(cells, channels)
-    weights_first = conv_first.reshape(9, channels, channels)
-    weights_second = conv_second.reshape(9, channels, channels)
-    gain, bias = norm_gain[None], norm_bias[None]
     shape = jax.ShapeDtypeStruct
     conv_flops = 18 * cells * channels * channels
     padded = pltpu.VMEM((cells + 2 * cols, channels), BF16)
@@ -390,30 +415,45 @@
     wide = shape((cells, channels), F32)
     narrow = shape((cells, channels), BF16)
 
-    one, two, three = call(
-        functools.partial(first_kernel, dims), (halos, small, halos), (place, flat, flat_cot), name="first"
-    )
-    image_one, image_three, stats = exchange(one, two, three, 2 * cols)
-
-    half = time_weight.shape[0] // 2
-    frequencies = jnp.exp(-math.log(10000.0) * jnp.arange(half, dtype=F32) / half)
-    angles = timesteps.astype(F32)[:, None] * frequencies[None]
-    sinusoid = jnp.concatenate([jnp.cos(angles), jnp.sin(angles)], axis=1)
-    class_row = lax.dynamic_slice_in_dim(class_table, class_ids[0], 1, axis=0).astype(F32)
     width = adaptive_weight.shape[0]
     spare = channels - width
     time_bias, mix = time_bias[None], adaptive_weight
     if spare:
-        time_weight, time_bias, class_row = (
-            jnp.pad(part, ((0, 0), (0, spare))) for part in (time_weight, time_bias, class_row)
+        time_weight, time_bias, class_table = (
+            jnp.pad(part, ((0, 0), (0, spare))) for part in (time_weight, time_bias, class_table)
         )
         mix = jnp.pad(mix, ((0, spare), (0, 0)))
-    embed = call(embed_kernel, block, (sinusoid, class_row, time_weight, time_bias, mix), smem=0, name="embed")
+    loads = (
+        images.reshape(cells, channels),
+        cotangent.reshape(cells, channels),
+        time_weight,
+        mix,
+        class_table,
+        time_bias,
+        norm_gain[None],
+        norm_bias[None],
+        adaptive_bias[None],
+        conv_first.reshape(9, channels, channels),
+        conv_second.reshape(9, channels, channels),
+    )
+    spaces = {k: pltpu.HBM for k in range(len(loads))}
+    spaces[len(loads)] = spaces[len(loads) + 1] = pltpu.SMEM
+    *held, one, two, three, instant = call(
+        functools.partial(first_kernel, dims),
+        (*(shape(part.shape, part.dtype) for part in loads), halos, small, halos, shape((8, 128), jnp.int32)),
+        (*loads, timesteps, class_ids),
+        (pltpu.SemaphoreType.DMA((len(loads),)),),
+        name="first",
+        spaces=spaces,
+    )
+    flat, flat_cot, time_weight, mix, class_table, time_bias, gain, bias, adaptive_bias, weights_first, weights_second = held
+    image_one, image_three, stats = exchange(one, two, three, 2 * cols)
+    embed = call(embed_kernel, block, (instant, class_table, time_weight, time_bias, mix), name="embed")
 
     hidden, stat_one, one, two, three = call(
         functools.partial(second_kernel, dims, len(stats)),
         (narrow, block, halo, small, halo),
-        (place, flat, image_one, image_three, weights_first, gain, bias, embed, *stats),
+        (flat, image_one, image_three, weights_first, gain, bias, embed, *stats),
         (padded,),
         conv_flops,
         name="second",
@@ -422,7 +462,7 @@
     grad_active = call(
         functools.partial(grad_kernel, dims),
         wide,
-        (place, flat_cot, image_one, image_three, weights_second),
+        (flat_cot, image_one, image_three, weights_second),
         (padded,),
         conv_flops,
         name="grad",
@@ -430,22 +470,23 @@
     active, grad_norm, stat_two, one, two, three = call(
         functools.partial(third_kernel, dims, len(stats)),
         (shape((cells + 2 * cols, channels), BF16), wide, block, halo, small, halo),
-        (place, hidden, hidden_one, hidden_three, grad_active, adaptive_bias[None], *stats),
+        (hidden, hidden_one, hidden_three, grad_active, adaptive_bias, *stats),
         flops=1000,
         name="third",
     )
     grad_one, grad_three, stats = exchange(one, two, three, cols)
     branch = call(
-        functools.partial(branch_kernel, dims), narrow, (active, weights_second), flops=conv_flops, smem=0, name="branch"
+        functools.partial(branch_kernel, dims), narrow, (active, weights_second), flops=conv_flops, name="branch"
     )
     grad_first, sums, pairs = call(
         functools.partial(fourth_kernel, dims, len(stats)),
         (wide, small, block),
-        (place, grad_norm, grad_one, grad_three, hidden, hidden_one, hidden_three, stat_two,
+        (branch, grad_norm, grad_one, grad_three, hidden, hidden_one, hidden_three, stat_two,
          weights_first, flat, stat_one, gain, bias, embed, *stats),
         (padded,),
         conv_flops,
         name="fourth",
+        spaces={0: pl.ANY},
     )
     stats = spread_small(sums)
     if fleet == 4:
@@ -453,13 +494,12 @@
     else:
         pair_list = [lax.all_gather(pairs, "image", axis=0, tiled=True)]
     input_grad = call(
-        functools.partial(fifth_kernel, dims, len(stats)), narrow, (grad_first, flat, stat_one, *stats), smem=0, name="fifth"
-    )
-    image = lax.axis_index("image").astype(jnp.int32)[None]
+        functools.partial(fifth_kernel, dims, len(stats)), narrow, (grad_first, flat, stat_one, *stats), name="fifth"
+    )
     grad_weight, grad_bias = call(
         weight_kernel,
         (shape((channels, 2 * channels), F32), shape((1, 2 * channels), F32)),
-        (image, *pair_list),
+        tuple(pair_list),
         name="weight",
     )
     return (

time: 47.4 us -> 52.9 us (1.12)
  waiting for transfers between devices: 7.81 us -> 12.4 us
  local copies, waits for them, and re-layouts: 7.89 us -> 10.9 us
  Pallas kernels: 9.31 us -> 8.39 us
  other arithmetic: 0.83 us -> 0 us
    ppermute x15, waiting for transfers between devices: 7.81 us -> 12.4 us  [swap(): return lax.ppermute(values, axis, [(i, i ^ distance) for i in range(size)])]
    unnamed x30 -> x24, local copies, waits for them, and re-layouts: 7.89 us -> 10.9 us
    pallas_call x9, Pallas kernels: 9.31 us -> 8.39 us  [call(): pl.pallas_call(kernel, out_shape=out_shapes, in_specs=[pl.BlockSpec(memor...]
    convert_element_type x1 -> x0, other arithmetic: 0.7 us -> none  [body(): lax.dynamic_slice_in_dim(class_table, class_ids[0], 1, axis=0).astype(F32)]
  transfers between devices with their start and end apart: 15 -> 15, of which waited for: 3 -> 4; matrix products, arithmetic and copies ran while one was open for 2% -> 0% of each run, Pallas kernels for 8% -> 7%
where the time goes in v2:
time: 52.9 us; the launch traced here: 52.5 us
  starting transfers between devices  18.8 us (36%)
  waiting for transfers between devices  12.4 us (23%)
  local copies, waits for them, and re-layouts  10.9 us (21%)
  Pallas kernels  8.39 us (16%)
  between operations  2.02 us (4%)
    ppermute x15, starting transfers between devices, swap(): return lax.ppermute(values, axis, [(i, i ^ distance) for i in range(size)])  18.8 us
    ppermute x15, waiting for transfers between devices, swap(): return lax.ppermute(values, axis, [(i, i ^ distance) for i in range(size)])  12.4 us
    unnamed x24, local copies, waits for them, and re-layouts  10.9 us
    pallas_call x9, Pallas kernels, call(): pl.pallas_call(kernel, out_shape=out_shapes, in_specs=[pl.BlockSpec(memor...  8.39 us
  transfers between devices with their start and end apart: 15, of which 4 were waited for; matrix products, arithmetic and copies ran while one was open for 0% of the time, Pallas kernels for 7%

profile of v2, /device:TPU:0, one launch (start us, length us, event | category | flops | bytes accessed | tf_op | source)
XLA Modules:
  0.0 52.5 jit_solution(6473742451585049617)
XLA Ops:
  1.9 1.3 %copy-done = bf16[3,3,256,256]{3,2,1,0:T(8,128)(2,1)S(1)} copy-done((bf16[3,3,256,256]{3,2,1,0:T(8,128)(2,1)S(1)}, bf16[3,3,256,256]{3,2,1,0:T(8,128)(2,1)}, u32[]{:S(2)}) %copy-start) | copy-done | bytes 1179672
  3.2 1.3 %copy-done.1 = bf16[3,3,256,256]{3,2,1,0:T(8,128)(2,1)S(1)} copy-done((bf16[3,3,256,256]{3,2,1,0:T(8,128)(2,1)S(1)}, bf16[3,3,256,256]{3,2,1,0:T(8,128)(2,1)}, u32[]{:S(2)}) %copy-start.1) | copy-done | bytes 1179672
  4.5 1.0 %copy-done.3 = bf16[1000,256]{1,0:T(8,128)(2,1)S(1)} copy-done((bf16[1000,256]{1,0:T(8,128)(2,1)S(1)}, bf16[1000,256]{1,0:T(8,128)(2,1)}, u32[]{:S(2)}) %copy-start.3) | copy-done | bytes 512024
  5.5 0.9 %copy-done.4 = bf16[256,512]{1,0:T(8,128)(2,1)S(1)} copy-done((bf16[256,512]{1,0:T(8,128)(2,1)S(1)}, bf16[256,512]{1,0:T(8,128)(2,1)}, u32[]{:S(2)}) %copy-start.4) | copy-done | bytes 262168
  6.5 0.9 %copy-done.5 = bf16[1,4,64,256]{3,2,1,0:T(8,128)(2,1)S(1)} copy-done((bf16[1,4,64,256]{3,2,1,0:T(8,128)(2,1)S(1)}, bf16[1,4,64,256]{3,2,1,0:T(8,128)(2,1)}, u32[]{:S(2)}) %copy-start.5) | copy-done | bytes 131096
  7.4 0.9 %copy-done.6 = bf16[1,4,64,256]{3,2,1,0:T(8,128)(2,1)S(1)} copy-done((bf16[1,4,64,256]{3,2,1,0:T(8,128)(2,1)S(1)}, bf16[1,4,64,256]{3,2,1,0:T(8,128)(2,1)}, u32[]{:S(2)}) %copy-start.6) | copy-done | bytes 131096
  8.3 0.9 %copy-done.7 = bf16[256,256]{1,0:T(8,128)(2,1)S(1)} copy-done((bf16[256,256]{1,0:T(8,128)(2,1)S(1)}, bf16[256,256]{1,0:T(8,128)(2,1)}, u32[]{:S(2)}) %copy-start.7) | copy-done | bytes 131096
  9.2 0.7 %copy-done.8 = f32[512]{0:T(512)S(1)} copy-done((f32[512]{0:T(512)S(1)}, f32[512]{0:T(512)}, u32[]{:S(2)}) %copy-start.8) | copy-done | bytes 2072
  9.9 0.7 %copy-done.9 = f32[256]{0:T(256)S(1)} copy-done((f32[256]{0:T(256)S(1)}, f32[256]{0:T(256)}, u32[]{:S(2)}) %copy-start.9) | copy-done | bytes 1048
  10.5 0.7 %copy-done.10 = f32[256]{0:T(256)S(1)} copy-done((f32[256]{0:T(256)S(1)}, f32[256]{0:T(256)}, u32[]{:S(2)}) %copy-start.10) | copy-done | bytes 1048
  11.2 0.7 %copy-done.11 = f32[256]{0:T(256)S(1)} copy-done((f32[256]{0:T(256)S(1)}, f32[256]{0:T(256)}, u32[]{:S(2)}) %copy-start.11) | copy-done | bytes 1048
  11.9 2.0 %first.1 = (bf16[256,256]{1,0:T(8,128)(2,1)S(1)}, bf16[256,256]{1,0:T(8,128)(2,1)S(1)}, bf16[256,256]{1,0:T(8,128)(2,1)S(1)}, bf16[256,512]{1,0:T(8,128)(2,1)S(1...) custom-call(bf16[256,256]{1,0:T(8,128)(2,1)S(1)} %bitcast.14, ...), custom_call_target="tpu_custom_call" | custom-call | flops 1000 | bytes 3531784 | tf_op jit(solution)/shard_map/first/pallas_call | solution.py:353
  13.9 3.1 %collective-permute-start = (bf16[160,256]{1,0:T(8,128)(2,1)S(1)}, bf16[160,256]{1,0:T(8,128)(2,1)S(1)}, u32[]{:S(2)}, u32[]{:S(2)}) collective-permute-start(bf16[160,256]{1,0:T(8,128)(2,1)S(1)} %get-tuple-element.36), channel_id=1, source_target_pairs={{0,4},{4,0},{8,12},{12,8},{1,5},{5,1},{9,13},{13,9},{2,6},{6,2},{1... | collective-permute-start | bytes 245768 | tf_op jit(solution)/shard_map/ppermute | solution.py:368
  17.0 2.5 %collective-permute-start.1 = (bf16[160,256]{1,0:T(8,128)(2,1)S(1)}, bf16[160,256]{1,0:T(8,128)(2,1)S(1)}, u32[]{:S(2)}, u32[]{:S(2)}) collective-permute-start(bf16[160,256]{1,0:T(8,128)(2,1)S(1)} %get-tuple-element.37), channel_id=1, source_target_pairs={{0,12},{4,8},{8,4},{12,0},{1,13},{5,9},{9,5},{13,1},{2,14},{6,10},... | collective-permute-start | bytes 245768 | tf_op jit(solution)/shard_map/ppermute | solution.py:368
  20.0 4.3 %collective-permute-done.2.rest_2_ = bf16[32,256]{1,0:T(8,128)(2,1)S(1)} collective-permute-done((bf16[32,256]{1,0:T(8,128)(2,1)S(1)}, bf16[32,256]{1,0:T(8,128)(2,1)S(1)}, u32[]{:S(2)}, u32[]{:S(2)}) %collective-permute-start.2) | collective-permute-done | bytes 16416 | tf_op jit(solution)/shard_map/ppermute | solution.py:368
  24.4 0.9 %second.1 = (bf16[256,256]{1,0:T(8,128)(2,1)S(1)}, f32[8,256]{1,0:T(8,128)S(1)}, bf16[96,256]{1,0:T(8,128)(2,1)S(1)}, bf16[32,256]{1,0:T(8,128)(2,1)S(1)}, bf16[96,256]{1,0:T(8,128)(2,1)S(1)}) custom-call(bf16[256,256]{1,0:T(8,128)(2,1)S(1)} %get-tuple-element.35.images, bf16[160,256]{1,0:T(8,128)(2,1)S(1)} %collective-permute-done.one.rest_1_, ...), custom_call_target="tpu_custom_call" | custom-call | flops 301989888 | bytes 1681408 | tf_op jit(solution)/shard_map/second/pallas_call | solution.py:353
  25.8 2.4 %collective-permute-start.4 = (bf16[96,256]{1,0:T(8,128)(2,1)S(1)}, bf16[96,256]{1,0:T(8,128)(2,1)S(1)}, u32[]{:S(2)}, u32[]{:S(2)}) collective-permute-start(bf16[96,256]{1,0:T(8,128)(2,1)S(1)} %get-tuple-element.49), channel_id=1, source_target_pairs={{0,12},{4,8},{8,4},{12,0},{1,13},{5,9},{9,5},{13,1},{2,14},{6,10},... | collective-permute-start | bytes 147464 | tf_op jit(solution)/shard_map/ppermute | solution.py:368
  28.2 0.6 %collective-permute-start.5 = (bf16[32,256]{1,0:T(8,128)(2,1)S(1)}, bf16[32,256]{1,0:T(8,128)(2,1)S(1)}, u32[]{:S(2)}, u32[]{:S(2)}) collective-permute-start(bf16[32,256]{1,0:T(8,128)(2,1)S(1)} %get-tuple-element.53.rest_0_), channel_id=1, source_target_pairs={{0,8},{4,12},{8,0},{12,4},{1,9},{5,13},{9,1},{13,5},{2,10},{6,14},... | collective-permute-start | bytes 49160 | tf_op jit(solution)/shard_map/ppermute | solution.py:368
  29.3 3.5 %collective-permute-done.5.rest_2_ = bf16[32,256]{1,0:T(8,128)(2,1)S(1)} collective-permute-done((bf16[32,256]{1,0:T(8,128)(2,1)S(1)}, bf16[32,256]{1,0:T(8,128)(2,1)S(1)}, u32[]{:S(2)}, u32[]{:S(2)}) %collective-permute-start.5) | collective-permute-done | bytes 16416 | tf_op jit(solution)/shard_map/ppermute | solution.py:368
  33.2 0.8 %collective-permute-start.6 = (bf16[96,256]{1,0:T(8,128)(2,1)S(1)}, bf16[96,256]{1,0:T(8,128)(2,1)S(1)}, u32[]{:S(2)}, u32[]{:S(2)}) collective-permute-start(bf16[96,256]{1,0:T(8,128)(2,1)S(1)} %get-tuple-element.56), channel_id=1, source_target_pairs={{0,4},{4,0},{8,12},{12,8},{1,5},{5,1},{9,13},{13,9},{2,6},{6,2},{1... | collective-permute-start | bytes 147464 | tf_op jit(solution)/shard_map/ppermute | solution.py:368
  34.0 1.3 %collective-permute-start.7 = (bf16[96,256]{1,0:T(8,128)(2,1)S(1)}, bf16[96,256]{1,0:T(8,128)(2,1)S(1)}, u32[]{:S(2)}, u32[]{:S(2)}) collective-permute-start(bf16[96,256]{1,0:T(8,128)(2,1)S(1)} %get-tuple-element.57), channel_id=1, source_target_pairs={{0,12},{4,8},{8,4},{12,0},{1,13},{5,9},{9,5},{13,1},{2,14},{6,10},... | collective-permute-start | bytes 147464 | tf_op jit(solution)/shard_map/ppermute | solution.py:368
  35.4 1.4 %collective-permute-start.8 = (bf16[32,256]{1,0:T(8,128)(2,1)S(1)}, bf16[32,256]{1,0:T(8,128)(2,1)S(1)}, u32[]{:S(2)}, u32[]{:S(2)}) collective-permute-start(bf16[32,256]{1,0:T(8,128)(2,1)S(1)} %get-tuple-element.60.rest_0_), channel_id=1, source_target_pairs={{0,8},{4,12},{8,0},{12,4},{1,9},{5,13},{9,1},{13,5},{2,10},{6,14},... | collective-permute-start | bytes 49160 | tf_op jit(solution)/shard_map/ppermute | solution.py:368
  36.8 1.1 %branch.1 = bf16[256,256]{1,0:T(8,128)(2,1)} custom-call(bf16[384,256]{1,0:T(8,128)(2,1)S(1)} %get-tuple-element.54.active, bf16[9,256,256]{2,1,0:T(8,128)(2,1)S(1)} %get-tuple-element.51.weights), custom_call_target="tpu_custom_call" | custom-call | flops 301989888 | bytes 1376256 | tf_op jit(solution)/shard_map/branch/pallas_call | solution.py:353
  37.9 2.4 %collective-permute-done.8.rest_2_ = bf16[32,256]{1,0:T(8,128)(2,1)S(1)} collective-permute-done((bf16[32,256]{1,0:T(8,128)(2,1)S(1)}, bf16[32,256]{1,0:T(8,128)(2,1)S(1)}, u32[]{:S(2)}, u32[]{:S(2)}) %collective-permute-start.8) | collective-permute-done | bytes 16416 | tf_op jit(solution)/shard_map/ppermute | solution.py:368
  40.3 0.9 %copy-done.2 = bf16[256,256]{1,0:T(8,128)(2,1)S(1)} copy-done((bf16[256,256]{1,0:T(8,128)(2,1)S(1)}, bf16[256,256]{1,0:T(8,128)(2,1)}, u32[]{:S(2)}) %copy-start.2) | copy-done | bytes 131096
  41.2 0.9 %fourth.1 = (f32[256,256]{1,0:T(8,128)S(1)}, bf16[32,256]{1,0:T(8,128)(2,1)S(1)}, f32[8,256]{1,0:T(8,128)S(1)}) custom-call(bf16[256,256]{1,0:T(8,128)(2,1)S(1)} %copy-done.2, f32[256,256]{1,0:T(8,128)S(1)} %get-tuple-element.55.grad_norm, bf16[96,256]{1,0:T(8,128)(2,1)S(1)} %collective-permute-done.6.one.rest_1_, ...), custom_call_target="tpu_custom_call" | custom-call | flops 301989888 | bytes 2189312 | tf_op jit(solution)/shard_map/fourth/pallas_call | solution.py:353
  42.2 2.3 %collective-permute-start.11 = (bf16[32,256]{1,0:T(8,128)(2,1)S(1)}, bf16[32,256]{1,0:T(8,128)(2,1)S(1)}, u32[]{:S(2)}, u32[]{:S(2)}) collective-permute-start(bf16[32,256]{1,0:T(8,128)(2,1)S(1)} %get-tuple-element.62.rest_0_), channel_id=1, source_target_pairs={{0,12},{4,8},{8,4},{12,0},{1,13},{5,9},{9,5},{13,1},{2,14},{6,10},... | collective-permute-start | bytes 49160 | tf_op jit(solution)/shard_map/ppermute | solution.py:368
  44.5 2.2 %collective-permute-start.9 = (bf16[32,256]{1,0:T(8,128)(2,1)S(1)}, bf16[32,256]{1,0:T(8,128)(2,1)S(1)}, u32[]{:S(2)}, u32[]{:S(2)}) collective-permute-start(bf16[32,256]{1,0:T(8,128)(2,1)S(1)} %get-tuple-element.62.rest_0_), channel_id=1, source_target_pairs={{0,4},{4,0},{8,12},{12,8},{1,5},{5,1},{9,13},{13,9},{2,6},{6,2},{1... | collective-permute-start | bytes 49160 | tf_op jit(solution)/shard_map/ppermute | solution.py:368
  46.6 1.5 %collective-permute-start.13 = (f32[8,256]{1,0:T(8,128)S(1)}, f32[8,256]{1,0:T(8,128)S(1)}, u32[]{:S(2)}, u32[]{:S(2)}) collective-permute-start(f32[8,256]{1,0:T(8,128)S(1)} %get-tuple-element.63.rest_0_), channel_id=1, source_target_pairs={{0,2},{1,3},{2,0},{3,1},{4,6},{5,7},{6,4},{7,5},{8,10},{9,11},{10,... | collective-permute-start | bytes 24584 | tf_op jit(solution)/shard_map/ppermute | solution.py:368
  48.1 2.2 %collective-permute-done.13.rest_2_ = f32[8,256]{1,0:T(8,128)S(1)} collective-permute-done((f32[8,256]{1,0:T(8,128)S(1)}, f32[8,256]{1,0:T(8,128)S(1)}, u32[]{:S(2)}, u32[]{:S(2)}) %collective-permute-start.13) | collective-permute-done | bytes 8224 | tf_op jit(solution)/shard_map/ppermute | solution.py:368
  50.3 1.4 %weight.1 = (f32[256,512]{1,0:T(8,128)}, f32[1,512]{1,0:T(1,128)}) custom-call(f32[8,256]{1,0:T(8,128)S(1)} %get-tuple-element.63.rest_0_, f32[8,256]{1,0:T(8,128)S(1)} %collective-permute-done.12.rest_1_, f32[8,256]{1,0:T(8,128)S(1)} %collective-permute-done.13.rest_2_, f32[8,256]{1,0:T(8,128)S(1)} %collective-permute-done.14.rest_3_), custom_call_target="tpu_custom_call" | custom-call | flops 1000 | bytes 32768 | tf_op jit(solution)/shard_map/weight/pallas_call | solution.py:353
  51.7 0.7 %fifth.1 = bf16[256,256]{1,0:T(8,128)(2,1)} custom-call(f32[256,256]{1,0:T(8,128)S(1)} %get-tuple-element.61.grad_first, bf16[256,256]{1,0:T(8,128)(2,1)S(1)} %get-tuple-element.35.images, f32[8,256]{1,0:T(8,128)S(1)} %get-tuple-element.59.stat_one, bf16[32,256]{1,0:T(8,128)(2,1)S(1)} %get-tuple-element.62.rest_0_, ...), custom_call_target="tpu_custom_call" | custom-call | flops 1000 | bytes 466944 | tf_op jit(solution)/shard_map/fifth/pallas_call | solution.py:353
  (31 shorter events, 2.0 us)
Async XLA Ops:
  1.9 1.3 %copy-start = (bf16[3,3,256,256]{3,2,1,0:T(8,128)(2,1)S(1)}, bf16[3,3,256,256]{3,2,1,0:T(8,128)(2,1)}, u32[]{:S(2)}) copy-start(bf16[3,3,256,256]{3,2,1,0:T(8,128)(2,1)} %param.19) | copy-start | bytes 3538948
  3.2 1.3 %copy-start.1 = (bf16[3,3,256,256]{3,2,1,0:T(8,128)(2,1)S(1)}, bf16[3,3,256,256]{3,2,1,0:T(8,128)(2,1)}, u32[]{:S(2)}) copy-start(bf16[3,3,256,256]{3,2,1,0:T(8,128)(2,1)} %param.20) | copy-start | bytes 3538948
  4.5 1.0 %copy-start.3 = (bf16[1000,256]{1,0:T(8,128)(2,1)S(1)}, bf16[1000,256]{1,0:T(8,128)(2,1)}, u32[]{:S(2)}) copy-start(bf16[1000,256]{1,0:T(8,128)(2,1)} %refs_4_.1) | copy-start | bytes 1536004
  5.5 0.9 %copy-start.4 = (bf16[256,512]{1,0:T(8,128)(2,1)S(1)}, bf16[256,512]{1,0:T(8,128)(2,1)}, u32[]{:S(2)}) copy-start(bf16[256,512]{1,0:T(8,128)(2,1)} %refs_3_.1) | copy-start | bytes 786436
  6.5 0.9 %copy-start.5 = (bf16[1,4,64,256]{3,2,1,0:T(8,128)(2,1)S(1)}, bf16[1,4,64,256]{3,2,1,0:T(8,128)(2,1)}, u32[]{:S(2)}) copy-start(bf16[1,4,64,256]{3,2,1,0:T(8,128)(2,1)} %param.13) | copy-start | bytes 393220
  7.4 0.9 %copy-start.6 = (bf16[1,4,64,256]{3,2,1,0:T(8,128)(2,1)S(1)}, bf16[1,4,64,256]{3,2,1,0:T(8,128)(2,1)}, u32[]{:S(2)}) copy-start(bf16[1,4,64,256]{3,2,1,0:T(8,128)(2,1)} %param.14) | copy-start | bytes 393220
  8.3 0.9 %copy-start.7 = (bf16[256,256]{1,0:T(8,128)(2,1)S(1)}, bf16[256,256]{1,0:T(8,128)(2,1)}, u32[]{:S(2)}) copy-start(bf16[256,256]{1,0:T(8,128)(2,1)} %refs_2_.1) | copy-start | bytes 393220
  9.2 0.7 %copy-start.8 = (f32[512]{0:T(512)S(1)}, f32[512]{0:T(512)}, u32[]{:S(2)}) copy-start(f32[512]{0:T(512)} %param.25) | copy-start | bytes 6148
  9.9 0.7 %copy-start.9 = (f32[256]{0:T(256)S(1)}, f32[256]{0:T(256)}, u32[]{:S(2)}) copy-start(f32[256]{0:T(256)} %param.22) | copy-start | bytes 3076
  10.5 0.7 %copy-start.10 = (f32[256]{0:T(256)S(1)}, f32[256]{0:T(256)}, u32[]{:S(2)}) copy-start(f32[256]{0:T(256)} %param.17) | copy-start | bytes 3076
  11.2 0.7 %copy-start.11 = (f32[256]{0:T(256)S(1)}, f32[256]{0:T(256)}, u32[]{:S(2)}) copy-start(f32[256]{0:T(256)} %param.18) | copy-start | bytes 3076
  13.9 10.4 %collective-permute-start = (bf16[160,256]{1,0:T(8,128)(2,1)S(1)}, bf16[160,256]{1,0:T(8,128)(2,1)S(1)}, u32[]{:S(2)}, u32[]{:S(2)}) collective-permute-start(bf16[160,256]{1,0:T(8,128)(2,1)S(1)} %get-tuple-element.36), channel_id=1, source_target_pairs={{0,4},{4,0},{8,12},{12,8},{1,5},{5,1},{9,13},{13,9},{2,6},{6,2},{1... | collective-permute-start | bytes 245768 | tf_op jit(solution)/shard_map/ppermute | solution.py:368
  17.0 7.3 %collective-permute-start.1 = (bf16[160,256]{1,0:T(8,128)(2,1)S(1)}, bf16[160,256]{1,0:T(8,128)(2,1)S(1)}, u32[]{:S(2)}, u32[]{:S(2)}) collective-permute-start(bf16[160,256]{1,0:T(8,128)(2,1)S(1)} %get-tuple-element.37), channel_id=1, source_target_pairs={{0,12},{4,8},{8,4},{12,0},{1,13},{5,9},{9,5},{13,1},{2,14},{6,10},... | collective-permute-start | bytes 245768 | tf_op jit(solution)/shard_map/ppermute | solution.py:368
  19.5 4.9 %collective-permute-start.2 = (bf16[32,256]{1,0:T(8,128)(2,1)S(1)}, bf16[32,256]{1,0:T(8,128)(2,1)S(1)}, u32[]{:S(2)}, u32[]{:S(2)}) collective-permute-start(bf16[32,256]{1,0:T(8,128)(2,1)S(1)} %get-tuple-element.46.rest_0_), channel_id=1, source_target_pairs={{0,8},{4,12},{8,0},{12,4},{1,9},{5,13},{9,1},{13,5},{2,10},{6,14},... | collective-permute-start | bytes 49160 | tf_op jit(solution)/shard_map/ppermute | solution.py:368
  25.3 7.6 %collective-permute-start.3 = (bf16[96,256]{1,0:T(8,128)(2,1)S(1)}, bf16[96,256]{1,0:T(8,128)(2,1)S(1)}, u32[]{:S(2)}, u32[]{:S(2)}) collective-permute-start(bf16[96,256]{1,0:T(8,128)(2,1)S(1)} %get-tuple-element.48), channel_id=1, source_target_pairs={{0,4},{4,0},{8,12},{12,8},{1,5},{5,1},{9,13},{13,9},{2,6},{6,2},{1... | collective-permute-start | bytes 147464 | tf_op jit(solution)/shard_map/ppermute | solution.py:368
  25.8 7.1 %collective-permute-start.4 = (bf16[96,256]{1,0:T(8,128)(2,1)S(1)}, bf16[96,256]{1,0:T(8,128)(2,1)S(1)}, u32[]{:S(2)}, u32[]{:S(2)}) collective-permute-start(bf16[96,256]{1,0:T(8,128)(2,1)S(1)} %get-tuple-element.49), channel_id=1, source_target_pairs={{0,12},{4,8},{8,4},{12,0},{1,13},{5,9},{9,5},{13,1},{2,14},{6,10},... | collective-permute-start | bytes 147464 | tf_op jit(solution)/shard_map/ppermute | solution.py:368
  28.2 4.6 %collective-permute-start.5 = (bf16[32,256]{1,0:T(8,128)(2,1)S(1)}, bf16[32,256]{1,0:T(8,128)(2,1)S(1)}, u32[]{:S(2)}, u32[]{:S(2)}) collective-permute-start(bf16[32,256]{1,0:T(8,128)(2,1)S(1)} %get-tuple-element.53.rest_0_), channel_id=1, source_target_pairs={{0,8},{4,12},{8,0},{12,4},{1,9},{5,13},{9,1},{13,5},{2,10},{6,14},... | collective-permute-start | bytes 49160 | tf_op jit(solution)/shard_map/ppermute | solution.py:368
  33.2 7.1 %collective-permute-start.6 = (bf16[96,256]{1,0:T(8,128)(2,1)S(1)}, bf16[96,256]{1,0:T(8,128)(2,1)S(1)}, u32[]{:S(2)}, u32[]{:S(2)}) collective-permute-start(bf16[96,256]{1,0:T(8,128)(2,1)S(1)} %get-tuple-element.56), channel_id=1, source_target_pairs={{0,4},{4,0},{8,12},{12,8},{1,5},{5,1},{9,13},{13,9},{2,6},{6,2},{1... | collective-permute-start | bytes 147464 | tf_op jit(solution)/shard_map/ppermute | solution.py:368
  34.0 6.2 %collective-permute-start.7 = (bf16[96,256]{1,0:T(8,128)(2,1)S(1)}, bf16[96,256]{1,0:T(8,128)(2,1)S(1)}, u32[]{:S(2)}, u32[]{:S(2)}) collective-permute-start(bf16[96,256]{1,0:T(8,128)(2,1)S(1)} %get-tuple-element.57), channel_id=1, source_target_pairs={{0,12},{4,8},{8,4},{12,0},{1,13},{5,9},{9,5},{13,1},{2,14},{6,10},... | collective-permute-start | bytes 147464 | tf_op jit(solution)/shard_map/ppermute | solution.py:368
  35.4 4.9 %collective-permute-start.8 = (bf16[32,256]{1,0:T(8,128)(2,1)S(1)}, bf16[32,256]{1,0:T(8,128)(2,1)S(1)}, u32[]{:S(2)}, u32[]{:S(2)}) collective-permute-start(bf16[32,256]{1,0:T(8,128)(2,1)S(1)} %get-tuple-element.60.rest_0_), channel_id=1, source_target_pairs={{0,8},{4,12},{8,0},{12,4},{1,9},{5,13},{9,1},{13,5},{2,10},{6,14},... | collective-permute-start | bytes 49160 | tf_op jit(solution)/shard_map/ppermute | solution.py:368
  40.3 0.9 %copy-start.2 = (bf16[256,256]{1,0:T(8,128)(2,1)S(1)}, bf16[256,256]{1,0:T(8,128)(2,1)}, u32[]{:S(2)}) copy-start(bf16[256,256]{1,0:T(8,128)(2,1)} %branch.1) | copy-start | bytes 393220
  42.1 6.0 %collective-permute-start.14 = (f32[8,256]{1,0:T(8,128)S(1)}, f32[8,256]{1,0:T(8,128)S(1)}, u32[]{:S(2)}, u32[]{:S(2)}) collective-permute-start(f32[8,256]{1,0:T(8,128)S(1)} %get-tuple-element.63.rest_0_), channel_id=1, source_target_pairs={{0,3},{1,2},{2,1},{3,0},{4,7},{5,6},{6,5},{7,4},{8,11},{9,10},{10,... | collective-permute-start | bytes 24584 | tf_op jit(solution)/shard_map/ppermute | solution.py:368
  42.2 9.5 %collective-permute-start.11 = (bf16[32,256]{1,0:T(8,128)(2,1)S(1)}, bf16[32,256]{1,0:T(8,128)(2,1)S(1)}, u32[]{:S(2)}, u32[]{:S(2)}) collective-permute-start(bf16[32,256]{1,0:T(8,128)(2,1)S(1)} %get-tuple-element.62.rest_0_), channel_id=1, source_target_pairs={{0,12},{4,8},{8,4},{12,0},{1,13},{5,9},{9,5},{13,1},{2,14},{6,10},... | collective-permute-start | bytes 49160 | tf_op jit(solution)/shard_map/ppermute | solution.py:368
  44.5 7.2 %collective-permute-start.10 = (bf16[32,256]{1,0:T(8,128)(2,1)S(1)}, bf16[32,256]{1,0:T(8,128)(2,1)S(1)}, u32[]{:S(2)}, u32[]{:S(2)}) collective-permute-start(bf16[32,256]{1,0:T(8,128)(2,1)S(1)} %get-tuple-element.62.rest_0_), channel_id=1, source_target_pairs={{0,8},{4,12},{8,0},{12,4},{1,9},{5,13},{9,1},{13,5},{2,10},{6,14},... | collective-permute-start | bytes 49160 | tf_op jit(solution)/shard_map/ppermute | solution.py:368
  44.5 7.2 %collective-permute-start.9 = (bf16[32,256]{1,0:T(8,128)(2,1)S(1)}, bf16[32,256]{1,0:T(8,128)(2,1)S(1)}, u32[]{:S(2)}, u32[]{:S(2)}) collective-permute-start(bf16[32,256]{1,0:T(8,128)(2,1)S(1)} %get-tuple-element.62.rest_0_), channel_id=1, source_target_pairs={{0,4},{4,0},{8,12},{12,8},{1,5},{5,1},{9,13},{13,9},{2,6},{6,2},{1... | collective-permute-start | bytes 49160 | tf_op jit(solution)/shard_map/ppermute | solution.py:368
  46.6 3.7 %collective-permute-start.13 = (f32[8,256]{1,0:T(8,128)S(1)}, f32[8,256]{1,0:T(8,128)S(1)}, u32[]{:S(2)}, u32[]{:S(2)}) collective-permute-start(f32[8,256]{1,0:T(8,128)S(1)} %get-tuple-element.63.rest_0_), channel_id=1, source_target_pairs={{0,2},{1,3},{2,0},{3,1},{4,6},{5,7},{6,4},{7,5},{8,10},{9,11},{10,... | collective-permute-start | bytes 24584 | tf_op jit(solution)/shard_map/ppermute | solution.py:368
  48.1 2.2 %collective-permute-start.12 = (f32[8,256]{1,0:T(8,128)S(1)}, f32[8,256]{1,0:T(8,128)S(1)}, u32[]{:S(2)}, u32[]{:S(2)}) collective-permute-start(f32[8,256]{1,0:T(8,128)S(1)} %get-tuple-element.63.rest_0_), channel_id=1, source_target_pairs={{0,1},{1,0},{2,3},{3,2},{4,5},{5,4},{6,7},{7,6},{8,9},{9,8},{10,11... | collective-permute-start | bytes 24584 | tf_op jit(solution)/shard_map/ppermute | solution.py:368

commit v3 on v2

--- a/solution.py
+++ b/solution.py
@@ -131,10 +131,9 @@
 
 def first_kernel(dims, *refs):
     cells, cols, channels, tiles = dims
-    count = (len(refs) - 7) // 2
-    sources, step, label = refs[:count], refs[count], refs[count + 1]
-    copies_to = refs[count + 2 : 2 * count + 2]
-    one, two, three, instant, sems = refs[2 * count + 2 :]
+    count = (len(refs) - 4) // 2
+    sources, copies_to = refs[:count], refs[count : 2 * count]
+    one, two, three, sems = refs[2 * count :]
     copies = [
         pltpu.make_async_copy(source, target, sems.at[k])
         for k, (source, target) in enumerate(zip(sources, copies_to, strict=True))
@@ -160,11 +159,9 @@
     three[2 * cols :] = block
     for copy in copies[2:]:
         copy.wait()
-    row = lax.broadcasted_iota(jnp.int32, instant.shape, 0)
-    instant[...] = jnp.where(row == 0, step[0], label[0])
-
-
-def embed_kernel(instant, table, time_weight, time_bias, adaptive_weight, out):
+
+
+def embed_kernel(step, label, table, time_weight, time_bias, adaptive_weight, out):
     channels = adaptive_weight.shape[1] // 2
     half = time_weight.shape[0] // 2
 
@@ -173,10 +170,10 @@
         return (product[0:8] + (product[8:16] + product[16:24]))[0:1]
 
     place = lax.broadcasted_iota(jnp.int32, (8, half), 1).astype(F32)
-    angles = instant[0:1, 0:1].astype(F32) * jnp.exp(-math.log(10000.0) * place / half)
+    angles = step[0].astype(F32) * jnp.exp(-math.log(10000.0) * place / half)
     sinusoid = jnp.concatenate([jnp.cos(angles), jnp.sin(angles)], axis=1)[0:1]
     classes = lax.broadcasted_iota(jnp.int32, (16, table.shape[0]), 1)
-    onehot = (classes == instant[1:2, 0:1]).astype(F32).astype(BF16)
+    onehot = (classes == label[0]).astype(F32).astype(BF16)
     row = jnp.dot(onehot, table[...], preferred_element_type=F32)[0:1]
     hidden = times(sinusoid, time_weight[...]) + time_bias[...]
     embedding = hidden * sigmoid(hidden) + row
@@ -265,13 +262,14 @@
     out_three[cols:] = block
 
 
-def branch_kernel(dims, active, weights, out):
+def branch_kernel(dims, active, weights, out, token):
     cells, cols, channels, tiles = dims
     out[...] = conv(active, weights, cells, cols, False).astype(BF16)
+    token[...] = jnp.zeros_like(token)
 
 
 def fourth_kernel(
-    dims, n_stats, branch, grad_norm, one, three, hidden, hidden_one, hidden_three, stat_two,
+    dims, n_stats, token, grad_norm, one, three, hidden, hidden_one, hidden_three, stat_two,
     weights, images, stat_one, gain, bias, embed, *rest
 ):
     cells, cols, channels, tiles = dims
@@ -436,19 +434,24 @@
         conv_first.reshape(9, channels, channels),
         conv_second.reshape(9, channels, channels),
     )
-    spaces = {k: pltpu.HBM for k in range(len(loads))}
-    spaces[len(loads)] = spaces[len(loads) + 1] = pltpu.SMEM
-    *held, one, two, three, instant = call(
+    spaces = {k: pl.ANY for k in range(len(loads))}
+    *held, one, two, three = call(
         functools.partial(first_kernel, dims),
-        (*(shape(part.shape, part.dtype) for part in loads), halos, small, halos, shape((8, 128), jnp.int32)),
-        (*loads, timesteps, class_ids),
+        (*(shape(part.shape, part.dtype) for part in loads), halos, small, halos),
+        tuple(pltpu.with_memory_space_constraint(part, pltpu.HBM) for part in loads),
         (pltpu.SemaphoreType.DMA((len(loads),)),),
         name="first",
         spaces=spaces,
     )
     flat, flat_cot, time_weight, mix, class_table, time_bias, gain, bias, adaptive_bias, weights_first, weights_second = held
     image_one, image_three, stats = exchange(one, two, three, 2 * cols)
-    embed = call(embed_kernel, block, (instant, class_table, time_weight, time_bias, mix), name="embed")
+    embed = call(
+        embed_kernel,
+        block,
+        (timesteps, class_ids, class_table, time_weight, time_bias, mix),
+        name="embed",
+        spaces={0: pltpu.SMEM, 1: pltpu.SMEM},
+    )
 
     hidden, stat_one, one, two, three = call(
         functools.partial(second_kernel, dims, len(stats)),
@@ -475,18 +478,17 @@
         name="third",
     )
     grad_one, grad_three, stats = exchange(one, two, three, cols)
-    branch = call(
-        functools.partial(branch_kernel, dims), narrow, (active, weights_second), flops=conv_flops, name="branch"
+    branch, token = call(
+        functools.partial(branch_kernel, dims), (narrow, shape((8, 128), F32)), (active, weights_second), flops=conv_flops, name="branch"
     )
     grad_first, sums, pairs = call(
         functools.partial(fourth_kernel, dims, len(stats)),
         (wide, small, block),
-        (branch, grad_norm, grad_one, grad_three, hidden, hidden_one, hidden_three, stat_two,
+        (token, grad_norm, grad_one, grad_three, hidden, hidden_one, hidden_three, stat_two,
          weights_first, flat, stat_one, gain, bias, embed, *stats),
         (padded,),
         conv_flops,
         name="fourth",
-        spaces={0: pl.ANY},
     )
     stats = spread_small(sums)
     if fleet == 4:

time: 52.9 us -> 40.6 us (0.77)
  local copies, waits for them, and re-layouts: 10.9 us -> 0 us
  waiting for transfers between devices: 12.4 us -> 11.1 us
    unnamed x24 -> x0, local copies, waits for them, and re-layouts: 10.9 us -> none
    ppermute x15, waiting for transfers between devices: 12.4 us -> 11.1 us  [swap(): return lax.ppermute(values, axis, [(i, i ^ distance) for i in range(size)])]
  transfers between devices with their start and end apart: 15 -> 15, of which waited for: 4 -> 4; matrix products, arithmetic and copies ran while one was open for 0% -> 0% of each run, Pallas kernels for 7% -> 9%
where the time goes in v3:
time: 40.6 us; the launch traced here: 40.5 us
  starting transfers between devices  18.8 us (46%)
  waiting for transfers between devices  11.1 us (27%)
  Pallas kernels  8.57 us (21%)
  between operations  2 us (5%)
    ppermute x15, starting transfers between devices, swap(): return lax.ppermute(values, axis, [(i, i ^ distance) for i in range(size)])  18.8 us
    ppermute x15, waiting for transfers between devices, swap(): return lax.ppermute(values, axis, [(i, i ^ distance) for i in range(size)])  11.1 us
    pallas_call x9, Pallas kernels, call(): pl.pallas_call(kernel, out_shape=out_shapes, in_specs=[pl.BlockSpec(memor...  8.57 us
  transfers between devices with their start and end apart: 15, of which 4 were waited for; matrix products, arithmetic and copies ran while one was open for 0% of the time, Pallas kernels for 9%

profile of v3, /device:TPU:0, one launch (start us, length us, event | category | flops | bytes accessed | tf_op | source)
XLA Modules:
  0.0 40.5 jit_solution(9058265902905712793)
XLA Ops:
  0.6 2.2 %first.1 = (bf16[256,256]{1,0:T(8,128)(2,1)S(1)}, bf16[256,256]{1,0:T(8,128)(2,1)S(1)}, bf16[256,256]{1,0:T(8,128)(2,1)S(1)}, bf16[256,512]{1,0:T(8,128)(2,1)S(1...) custom-call(bf16[256,256]{1,0:T(8,128)(2,1)} %bitcast.14, ...), custom_call_target="tpu_custom_call" | custom-call | flops 1000 | bytes 3531776 | tf_op jit(solution)/shard_map/first/pallas_call | solution.py:351
  2.9 3.1 %collective-permute-start = (bf16[160,256]{1,0:T(8,128)(2,1)S(1)}, bf16[160,256]{1,0:T(8,128)(2,1)S(1)}, u32[]{:S(2)}, u32[]{:S(2)}) collective-permute-start(bf16[160,256]{1,0:T(8,128)(2,1)S(1)} %get-tuple-element.37), channel_id=1, source_target_pairs={{0,4},{4,0},{8,12},{12,8},{1,5},{5,1},{9,13},{13,9},{2,6},{6,2},{1... | collective-permute-start | bytes 245768 | tf_op jit(solution)/shard_map/ppermute | solution.py:366
  6.0 2.5 %collective-permute-start.1 = (bf16[160,256]{1,0:T(8,128)(2,1)S(1)}, bf16[160,256]{1,0:T(8,128)(2,1)S(1)}, u32[]{:S(2)}, u32[]{:S(2)}) collective-permute-start(bf16[160,256]{1,0:T(8,128)(2,1)S(1)} %get-tuple-element.38), channel_id=1, source_target_pairs={{0,12},{4,8},{8,4},{12,0},{1,13},{5,9},{9,5},{13,1},{2,14},{6,10},... | collective-permute-start | bytes 245768 | tf_op jit(solution)/shard_map/ppermute | solution.py:366
  8.4 0.1 collective-permute-start.2
  9.8 0.4 embed.1
  10.2 3.1 %collective-permute-done.2.rest_2_ = bf16[32,256]{1,0:T(8,128)(2,1)S(1)} collective-permute-done((bf16[32,256]{1,0:T(8,128)(2,1)S(1)}, bf16[32,256]{1,0:T(8,128)(2,1)S(1)}, u32[]{:S(2)}, u32[]{:S(2)}) %collective-permute-start.2) | collective-permute-done | bytes 16416 | tf_op jit(solution)/shard_map/ppermute | solution.py:366
  13.3 0.0 collective-permute-done.one.rest_1_
  13.3 0.0 collective-permute-done.1.three.rest_3_
  13.3 0.9 %second.1 = (bf16[256,256]{1,0:T(8,128)(2,1)S(1)}, f32[8,256]{1,0:T(8,128)S(1)}, bf16[96,256]{1,0:T(8,128)(2,1)S(1)}, bf16[32,256]{1,0:T(8,128)(2,1)S(1)}, bf16[96,256]{1,0:T(8,128)(2,1)S(1)}) custom-call(bf16[256,256]{1,0:T(8,128)(2,1)S(1)} %get-tuple-element.36.images, bf16[160,256]{1,0:T(8,128)(2,1)S(1)} %collective-permute-done.one.rest_1_, ...), custom_call_target="tpu_custom_call" | custom-call | flops 301989888 | bytes 1681408 | tf_op jit(solution)/shard_map/second/pallas_call | solution.py:351
  14.2 0.5 %collective-permute-start.3 = (bf16[96,256]{1,0:T(8,128)(2,1)S(1)}, bf16[96,256]{1,0:T(8,128)(2,1)S(1)}, u32[]{:S(2)}, u32[]{:S(2)}) collective-permute-start(bf16[96,256]{1,0:T(8,128)(2,1)S(1)} %get-tuple-element.48), channel_id=1, source_target_pairs={{0,4},{4,0},{8,12},{12,8},{1,5},{5,1},{9,13},{13,9},{2,6},{6,2},{1... | collective-permute-start | bytes 147464 | tf_op jit(solution)/shard_map/ppermute | solution.py:366
  14.7 2.4 %collective-permute-start.4 = (bf16[96,256]{1,0:T(8,128)(2,1)S(1)}, bf16[96,256]{1,0:T(8,128)(2,1)S(1)}, u32[]{:S(2)}, u32[]{:S(2)}) collective-permute-start(bf16[96,256]{1,0:T(8,128)(2,1)S(1)} %get-tuple-element.49), channel_id=1, source_target_pairs={{0,12},{4,8},{8,4},{12,0},{1,13},{5,9},{9,5},{13,1},{2,14},{6,10},... | collective-permute-start | bytes 147464 | tf_op jit(solution)/shard_map/ppermute | solution.py:366
  17.2 0.6 %collective-permute-start.5 = (bf16[32,256]{1,0:T(8,128)(2,1)S(1)}, bf16[32,256]{1,0:T(8,128)(2,1)S(1)}, u32[]{:S(2)}, u32[]{:S(2)}) collective-permute-start(bf16[32,256]{1,0:T(8,128)(2,1)S(1)} %get-tuple-element.53.rest_0_), channel_id=1, source_target_pairs={{0,8},{4,12},{8,0},{12,4},{1,9},{5,13},{9,1},{13,5},{2,10},{6,14},... | collective-permute-start | bytes 49160 | tf_op jit(solution)/shard_map/ppermute | solution.py:366
  17.8 0.5 %grad.1.grad_active = f32[256,256]{1,0:T(8,128)S(1)} custom-call(bf16[256,256]{1,0:T(8,128)(2,1)S(1)} %get-tuple-element.50.cotangent, bf16[160,256]{1,0:T(8,128)(2,1)S(1)} %collective-permute-done.one.rest_1_, bf16[160,256]{1,0:T(8,128)(2,1)S(1)} %collective-permute-done.1.three.rest_3_, bf16[9,256,256]{2,1,0:T(8,128)(2,1)S(1)} %get-tuple-element.51.weights), custom_call_target="tpu_custom_call" | custom-call | flops 301989888 | bytes 1474560 | tf_op jit(solution)/shard_map/grad/pallas_call | solution.py:351
  18.3 3.5 %collective-permute-done.5.rest_2_ = bf16[32,256]{1,0:T(8,128)(2,1)S(1)} collective-permute-done((bf16[32,256]{1,0:T(8,128)(2,1)S(1)}, bf16[32,256]{1,0:T(8,128)(2,1)S(1)}, u32[]{:S(2)}, u32[]{:S(2)}) %collective-permute-start.5) | collective-permute-done | bytes 16416 | tf_op jit(solution)/shard_map/ppermute | solution.py:366
  21.8 0.3 third.1
  22.1 0.8 %collective-permute-start.6 = (bf16[96,256]{1,0:T(8,128)(2,1)S(1)}, bf16[96,256]{1,0:T(8,128)(2,1)S(1)}, u32[]{:S(2)}, u32[]{:S(2)}) collective-permute-start(bf16[96,256]{1,0:T(8,128)(2,1)S(1)} %get-tuple-element.58), channel_id=1, source_target_pairs={{0,4},{4,0},{8,12},{12,8},{1,5},{5,1},{9,13},{13,9},{2,6},{6,2},{1... | collective-permute-start | bytes 147464 | tf_op jit(solution)/shard_map/ppermute | solution.py:366
  23.0 1.3 %collective-permute-start.7 = (bf16[96,256]{1,0:T(8,128)(2,1)S(1)}, bf16[96,256]{1,0:T(8,128)(2,1)S(1)}, u32[]{:S(2)}, u32[]{:S(2)}) collective-permute-start(bf16[96,256]{1,0:T(8,128)(2,1)S(1)} %get-tuple-element.59), channel_id=1, source_target_pairs={{0,12},{4,8},{8,4},{12,0},{1,13},{5,9},{9,5},{13,1},{2,14},{6,10},... | collective-permute-start | bytes 147464 | tf_op jit(solution)/shard_map/ppermute | solution.py:366
  24.3 1.4 %collective-permute-start.8 = (bf16[32,256]{1,0:T(8,128)(2,1)S(1)}, bf16[32,256]{1,0:T(8,128)(2,1)S(1)}, u32[]{:S(2)}, u32[]{:S(2)}) collective-permute-start(bf16[32,256]{1,0:T(8,128)(2,1)S(1)} %get-tuple-element.62.rest_0_), channel_id=1, source_target_pairs={{0,8},{4,12},{8,0},{12,4},{1,9},{5,13},{9,1},{13,5},{2,10},{6,14},... | collective-permute-start | bytes 49160 | tf_op jit(solution)/shard_map/ppermute | solution.py:366
  25.7 1.1 %branch.1 = (bf16[256,256]{1,0:T(8,128)(2,1)}, f32[8,128]{1,0:T(8,128)S(1)}) custom-call(bf16[384,256]{1,0:T(8,128)(2,1)S(1)} %get-tuple-element.54.active, bf16[9,256,256]{2,1,0:T(8,128)(2,1)S(1)} %get-tuple-element.51.weights), custom_call_target="tpu_custom_call" | custom-call | flops 301989888 | bytes 1376256 | tf_op jit(solution)/shard_map/branch/pallas_call | solution.py:351
  26.8 2.4 %collective-permute-done.8.rest_2_ = bf16[32,256]{1,0:T(8,128)(2,1)S(1)} collective-permute-done((bf16[32,256]{1,0:T(8,128)(2,1)S(1)}, bf16[32,256]{1,0:T(8,128)(2,1)S(1)}, u32[]{:S(2)}, u32[]{:S(2)}) %collective-permute-start.8) | collective-permute-done | bytes 16416 | tf_op jit(solution)/shard_map/ppermute | solution.py:366
  29.2 0.9 %fourth.1 = (f32[256,256]{1,0:T(8,128)S(1)}, bf16[32,256]{1,0:T(8,128)(2,1)S(1)}, f32[8,256]{1,0:T(8,128)S(1)}) custom-call(f32[8,128]{1,0:T(8,128)S(1)} %get-tuple-element.56.token, f32[256,256]{1,0:T(8,128)S(1)} %get-tuple-element.57.grad_norm, bf16[96,256]{1,0:T(8,128)(2,1)S(1)} %collective-permute-done.6.one.rest_1_, ...), custom_call_target="tpu_custom_call" | custom-call | flops 301989888 | bytes 2062336 | tf_op jit(solution)/shard_map/fourth/pallas_call | solution.py:351
  30.1 0.1 collective-permute-start.14
  30.2 2.3 %collective-permute-start.11 = (bf16[32,256]{1,0:T(8,128)(2,1)S(1)}, bf16[32,256]{1,0:T(8,128)(2,1)S(1)}, u32[]{:S(2)}, u32[]{:S(2)}) collective-permute-start(bf16[32,256]{1,0:T(8,128)(2,1)S(1)} %get-tuple-element.64.rest_0_), channel_id=1, source_target_pairs={{0,12},{4,8},{8,4},{12,0},{1,13},{5,9},{9,5},{13,1},{2,14},{6,10},... | collective-permute-start | bytes 49160 | tf_op jit(solution)/shard_map/ppermute | solution.py:366
  32.5 0.0 collective-permute-start.10
  32.5 2.2 %collective-permute-start.9 = (bf16[32,256]{1,0:T(8,128)(2,1)S(1)}, bf16[32,256]{1,0:T(8,128)(2,1)S(1)}, u32[]{:S(2)}, u32[]{:S(2)}) collective-permute-start(bf16[32,256]{1,0:T(8,128)(2,1)S(1)} %get-tuple-element.64.rest_0_), channel_id=1, source_target_pairs={{0,4},{4,0},{8,12},{12,8},{1,5},{5,1},{9,13},{13,9},{2,6},{6,2},{1... | collective-permute-start | bytes 49160 | tf_op jit(solution)/shard_map/ppermute | solution.py:366
  34.7 1.5 %collective-permute-start.13 = (f32[8,256]{1,0:T(8,128)S(1)}, f32[8,256]{1,0:T(8,128)S(1)}, u32[]{:S(2)}, u32[]{:S(2)}) collective-permute-start(f32[8,256]{1,0:T(8,128)S(1)} %get-tuple-element.65.rest_0_), channel_id=1, source_target_pairs={{0,2},{1,3},{2,0},{3,1},{4,6},{5,7},{6,4},{7,5},{8,10},{9,11},{10,... | collective-permute-start | bytes 24584 | tf_op jit(solution)/shard_map/ppermute | solution.py:366
  36.1 0.0 collective-permute-done.14.rest_3_
  36.2 0.0 collective-permute-start.12
  36.2 2.2 %collective-permute-done.13.rest_2_ = f32[8,256]{1,0:T(8,128)S(1)} collective-permute-done((f32[8,256]{1,0:T(8,128)S(1)}, f32[8,256]{1,0:T(8,128)S(1)}, u32[]{:S(2)}, u32[]{:S(2)}) %collective-permute-start.13) | collective-permute-done | bytes 8224 | tf_op jit(solution)/shard_map/ppermute | solution.py:366
  38.3 0.0 collective-permute-done.12.rest_1_
  38.3 1.4 %weight.1 = (f32[256,512]{1,0:T(8,128)}, f32[1,512]{1,0:T(1,128)}) custom-call(f32[8,256]{1,0:T(8,128)S(1)} %get-tuple-element.65.rest_0_, f32[8,256]{1,0:T(8,128)S(1)} %collective-permute-done.12.rest_1_, f32[8,256]{1,0:T(8,128)S(1)} %collective-permute-done.13.rest_2_, f32[8,256]{1,0:T(8,128)S(1)} %collective-permute-done.14.rest_3_), custom_call_target="tpu_custom_call" | custom-call | flops 1000 | bytes 32768 | tf_op jit(solution)/shard_map/weight/pallas_call | solution.py:351
  39.7 0.7 %fifth.1 = bf16[256,256]{1,0:T(8,128)(2,1)} custom-call(f32[256,256]{1,0:T(8,128)S(1)} %get-tuple-element.63.grad_first, bf16[256,256]{1,0:T(8,128)(2,1)S(1)} %get-tuple-element.36.images, f32[8,256]{1,0:T(8,128)S(1)} %get-tuple-element.61.stat_one, bf16[32,256]{1,0:T(8,128)(2,1)S(1)} %get-tuple-element.64.rest_0_, ...), custom_call_target="tpu_custom_call" | custom-call | flops 1000 | bytes 466944 | tf_op jit(solution)/shard_map/fifth/pallas_call | solution.py:351
  (7 shorter events, 0.0 us)
Async XLA Ops:
  2.9 10.4 %collective-permute-start = (bf16[160,256]{1,0:T(8,128)(2,1)S(1)}, bf16[160,256]{1,0:T(8,128)(2,1)S(1)}, u32[]{:S(2)}, u32[]{:S(2)}) collective-permute-start(bf16[160,256]{1,0:T(8,128)(2,1)S(1)} %get-tuple-element.37), channel_id=1, source_target_pairs={{0,4},{4,0},{8,12},{12,8},{1,5},{5,1},{9,13},{13,9},{2,6},{6,2},{1... | collective-permute-start | bytes 245768 | tf_op jit(solution)/shard_map/ppermute | solution.py:366
  6.0 7.3 %collective-permute-start.1 = (bf16[160,256]{1,0:T(8,128)(2,1)S(1)}, bf16[160,256]{1,0:T(8,128)(2,1)S(1)}, u32[]{:S(2)}, u32[]{:S(2)}) collective-permute-start(bf16[160,256]{1,0:T(8,128)(2,1)S(1)} %get-tuple-element.38), channel_id=1, source_target_pairs={{0,12},{4,8},{8,4},{12,0},{1,13},{5,9},{9,5},{13,1},{2,14},{6,10},... | collective-permute-start | bytes 245768 | tf_op jit(solution)/shard_map/ppermute | solution.py:366
  8.4 4.9 %collective-permute-start.2 = (bf16[32,256]{1,0:T(8,128)(2,1)S(1)}, bf16[32,256]{1,0:T(8,128)(2,1)S(1)}, u32[]{:S(2)}, u32[]{:S(2)}) collective-permute-start(bf16[32,256]{1,0:T(8,128)(2,1)S(1)} %get-tuple-element.46.rest_0_), channel_id=1, source_target_pairs={{0,8},{4,12},{8,0},{12,4},{1,9},{5,13},{9,1},{13,5},{2,10},{6,14},... | collective-permute-start | bytes 49160 | tf_op jit(solution)/shard_map/ppermute | solution.py:366
  14.2 7.6 %collective-permute-start.3 = (bf16[96,256]{1,0:T(8,128)(2,1)S(1)}, bf16[96,256]{1,0:T(8,128)(2,1)S(1)}, u32[]{:S(2)}, u32[]{:S(2)}) collective-permute-start(bf16[96,256]{1,0:T(8,128)(2,1)S(1)} %get-tuple-element.48), channel_id=1, source_target_pairs={{0,4},{4,0},{8,12},{12,8},{1,5},{5,1},{9,13},{13,9},{2,6},{6,2},{1... | collective-permute-start | bytes 147464 | tf_op jit(solution)/shard_map/ppermute | solution.py:366
  14.7 7.1 %collective-permute-start.4 = (bf16[96,256]{1,0:T(8,128)(2,1)S(1)}, bf16[96,256]{1,0:T(8,128)(2,1)S(1)}, u32[]{:S(2)}, u32[]{:S(2)}) collective-permute-start(bf16[96,256]{1,0:T(8,128)(2,1)S(1)} %get-tuple-element.49), channel_id=1, source_target_pairs={{0,12},{4,8},{8,4},{12,0},{1,13},{5,9},{9,5},{13,1},{2,14},{6,10},... | collective-permute-start | bytes 147464 | tf_op jit(solution)/shard_map/ppermute | solution.py:366
  17.2 4.6 %collective-permute-start.5 = (bf16[32,256]{1,0:T(8,128)(2,1)S(1)}, bf16[32,256]{1,0:T(8,128)(2,1)S(1)}, u32[]{:S(2)}, u32[]{:S(2)}) collective-permute-start(bf16[32,256]{1,0:T(8,128)(2,1)S(1)} %get-tuple-element.53.rest_0_), channel_id=1, source_target_pairs={{0,8},{4,12},{8,0},{12,4},{1,9},{5,13},{9,1},{13,5},{2,10},{6,14},... | collective-permute-start | bytes 49160 | tf_op jit(solution)/shard_map/ppermute | solution.py:366
  22.1 7.1 %collective-permute-start.6 = (bf16[96,256]{1,0:T(8,128)(2,1)S(1)}, bf16[96,256]{1,0:T(8,128)(2,1)S(1)}, u32[]{:S(2)}, u32[]{:S(2)}) collective-permute-start(bf16[96,256]{1,0:T(8,128)(2,1)S(1)} %get-tuple-element.58), channel_id=1, source_target_pairs={{0,4},{4,0},{8,12},{12,8},{1,5},{5,1},{9,13},{13,9},{2,6},{6,2},{1... | collective-permute-start | bytes 147464 | tf_op jit(solution)/shard_map/ppermute | solution.py:366
  23.0 6.2 %collective-permute-start.7 = (bf16[96,256]{1,0:T(8,128)(2,1)S(1)}, bf16[96,256]{1,0:T(8,128)(2,1)S(1)}, u32[]{:S(2)}, u32[]{:S(2)}) collective-permute-start(bf16[96,256]{1,0:T(8,128)(2,1)S(1)} %get-tuple-element.59), channel_id=1, source_target_pairs={{0,12},{4,8},{8,4},{12,0},{1,13},{5,9},{9,5},{13,1},{2,14},{6,10},... | collective-permute-start | bytes 147464 | tf_op jit(solution)/shard_map/ppermute | solution.py:366
  24.3 4.9 %collective-permute-start.8 = (bf16[32,256]{1,0:T(8,128)(2,1)S(1)}, bf16[32,256]{1,0:T(8,128)(2,1)S(1)}, u32[]{:S(2)}, u32[]{:S(2)}) collective-permute-start(bf16[32,256]{1,0:T(8,128)(2,1)S(1)} %get-tuple-element.62.rest_0_), channel_id=1, source_target_pairs={{0,8},{4,12},{8,0},{12,4},{1,9},{5,13},{9,1},{13,5},{2,10},{6,14},... | collective-permute-start | bytes 49160 | tf_op jit(solution)/shard_map/ppermute | solution.py:366
  30.1 6.0 %collective-permute-start.14 = (f32[8,256]{1,0:T(8,128)S(1)}, f32[8,256]{1,0:T(8,128)S(1)}, u32[]{:S(2)}, u32[]{:S(2)}) collective-permute-start(f32[8,256]{1,0:T(8,128)S(1)} %get-tuple-element.65.rest_0_), channel_id=1, source_target_pairs={{0,3},{1,2},{2,1},{3,0},{4,7},{5,6},{6,5},{7,4},{8,11},{9,10},{10,... | collective-permute-start | bytes 24584 | tf_op jit(solution)/shard_map/ppermute | solution.py:366
  30.2 9.5 %collective-permute-start.11 = (bf16[32,256]{1,0:T(8,128)(2,1)S(1)}, bf16[32,256]{1,0:T(8,128)(2,1)S(1)}, u32[]{:S(2)}, u32[]{:S(2)}) collective-permute-start(bf16[32,256]{1,0:T(8,128)(2,1)S(1)} %get-tuple-element.64.rest_0_), channel_id=1, source_target_pairs={{0,12},{4,8},{8,4},{12,0},{1,13},{5,9},{9,5},{13,1},{2,14},{6,10},... | collective-permute-start | bytes 49160 | tf_op jit(solution)/shard_map/ppermute | solution.py:366
  32.5 7.2 %collective-permute-start.10 = (bf16[32,256]{1,0:T(8,128)(2,1)S(1)}, bf16[32,256]{1,0:T(8,128)(2,1)S(1)}, u32[]{:S(2)}, u32[]{:S(2)}) collective-permute-start(bf16[32,256]{1,0:T(8,128)(2,1)S(1)} %get-tuple-element.64.rest_0_), channel_id=1, source_target_pairs={{0,8},{4,12},{8,0},{12,4},{1,9},{5,13},{9,1},{13,5},{2,10},{6,14},... | collective-permute-start | bytes 49160 | tf_op jit(solution)/shard_map/ppermute | solution.py:366
  32.5 7.2 %collective-permute-start.9 = (bf16[32,256]{1,0:T(8,128)(2,1)S(1)}, bf16[32,256]{1,0:T(8,128)(2,1)S(1)}, u32[]{:S(2)}, u32[]{:S(2)}) collective-permute-start(bf16[32,256]{1,0:T(8,128)(2,1)S(1)} %get-tuple-element.64.rest_0_), channel_id=1, source_target_pairs={{0,4},{4,0},{8,12},{12,8},{1,5},{5,1},{9,13},{13,9},{2,6},{6,2},{1... | collective-permute-start | bytes 49160 | tf_op jit(solution)/shard_map/ppermute | solution.py:366
  34.7 3.7 %collective-permute-start.13 = (f32[8,256]{1,0:T(8,128)S(1)}, f32[8,256]{1,0:T(8,128)S(1)}, u32[]{:S(2)}, u32[]{:S(2)}) collective-permute-start(f32[8,256]{1,0:T(8,128)S(1)} %get-tuple-element.65.rest_0_), channel_id=1, source_target_pairs={{0,2},{1,3},{2,0},{3,1},{4,6},{5,7},{6,4},{7,5},{8,10},{9,11},{10,... | collective-permute-start | bytes 24584 | tf_op jit(solution)/shard_map/ppermute | solution.py:366
  36.2 2.2 %collective-permute-start.12 = (f32[8,256]{1,0:T(8,128)S(1)}, f32[8,256]{1,0:T(8,128)S(1)}, u32[]{:S(2)}, u32[]{:S(2)}) collective-permute-start(f32[8,256]{1,0:T(8,128)S(1)} %get-tuple-element.65.rest_0_), channel_id=1, source_target_pairs={{0,1},{1,0},{2,3},{3,2},{4,5},{5,4},{6,7},{7,6},{8,9},{9,8},{10,11... | collective-permute-start | bytes 24584 | tf_op jit(solution)/shard_map/ppermute | solution.py:366

commit v4 on v3

--- a/solution.py
+++ b/solution.py
@@ -83,32 +83,37 @@
     return lax.bitwise_and(index, cols - 1)
 
 
-def conv(padded_ref, kernel_ref, cells, cols, flipped):
+def conv(padded_ref, kernel_ref, cells, cols, flipped, turned=False):
     parts = []
     for j in range(3):
         total = None
         for i in range(3):
-            rows = padded_ref[(2 - i if flipped else i) * cols : (2 - i if flipped else i) * cols + cells]
-            weights = kernel_ref[3 * i + j]
+            start = (2 - i if flipped else i) * cols
             product = lax.dot_general(
-                rows,
-                weights,
-                (((1,), (1 if flipped else 0,)), ((), ())),
+                padded_ref[start : start + cells],
+                kernel_ref[3 * i + j],
+                (((1,), (1 if flipped and not turned else 0,)), ((), ())),
                 preferred_element_type=F32,
             )
             total = product if total is None else total + product
         parts.append(total)
     if flipped:
         parts = parts[::-1]
-    column = column_index(cells, cols, parts[0].shape[1])
-    left = jnp.where(column == 0, 0.0, pltpu.roll(parts[0], 1, 0))
-    right = jnp.where(column == cols - 1, 0.0, pltpu.roll(parts[2], cells - 1, 0))
-    return parts[1] + (left + right)
+    return parts[1] + (shifted(parts[0], cols, 1) + shifted(parts[2], cols, -1))
+
+
+def shifted(values, cols, step):
+    cells = values.shape[0]
+    column = column_index(cells, cols, values.shape[1])
+    if step == 1:
+        return jnp.where(column == 0, 0.0, pltpu.roll(values, 1, 0))
+    return jnp.where(column == cols - 1, 0.0, pltpu.roll(values, cells - 1, 0))
 
 
 def stat_list(refs, start, tiles):
     if len(refs) == 1:
-        return [joined(refs[0][STAT_ROWS * t : STAT_ROWS * (t + 1)]) for t in range(tiles)]
+        size = refs[0].shape[0] // tiles
+        return [joined(refs[0][size * t : size * t + STAT_ROWS]) for t in range(tiles)]
     return [joined(ref[s : s + STAT_ROWS]) for ref, s in zip(refs, start, strict=True)]
 
 
@@ -151,12 +156,14 @@
     one[0:cols] = images[pl.ds(start_one, cols)]
     three[0:cols] = images[pl.ds(start_three, cols)]
     copies[1].wait()
-    one[cols : 2 * cols] = cotangent[pl.ds(start_one, cols)]
-    three[cols : 2 * cols] = cotangent[pl.ds(start_three, cols)]
+    odd = place[1]
+    near, far = (1 - odd) * (cells - 2 * cols), odd * (cells - 2 * cols)
+    one[cols : 3 * cols] = cotangent[pl.ds(pl.multiple_of(near, cols), 2 * cols)]
+    three[cols : 3 * cols] = cotangent[pl.ds(pl.multiple_of(far, cols), 2 * cols)]
     block = terms(rows8(mean, spread))
-    one[2 * cols :] = block
+    one[3 * cols :] = block
     two[...] = block
-    three[2 * cols :] = block
+    three[3 * cols :] = block
     for copy in copies[2:]:
         copy.wait()
 
@@ -188,7 +195,7 @@
     stat_refs, (hidden, stat, out_one, out_two, out_three, padded) = rest[:n_stats], rest[n_stats:]
     count = cells * (channels // GN_GROUPS)
     mean, inverse = joint_moments(
-        stat_list(stat_refs, (0, 2 * cols, 0, 2 * cols), tiles), count
+        stat_list(stat_refs, (0, 3 * cols, 0, 3 * cols), tiles), count
     )
     stat[...] = rows8(mean, inverse)
     above, below = edges(place, one[0:cols], three[0:cols])
@@ -212,20 +219,106 @@
     out_three[cols:] = block
 
 
+def turn_kernel(weights, turned, grouped):
+    channels = weights.shape[1]
+    unit = 1.0 * (lax.broadcasted_iota(jnp.int32, (channels, channels), 0) == lax.broadcasted_iota(jnp.int32, (channels, channels), 1))
+    unit = unit.astype(BF16)
+    picks = group_columns(channels, 0, GN_GROUPS, 0)
+    for tap in range(weights.shape[0]):
+        matrix = lax.dot_general(
+            unit, weights[tap], (((1,), (1,)), ((), ())), preferred_element_type=F32
+        ).astype(BF16)
+        turned[tap] = matrix
+        grouped[tap] = jnp.dot(picks, matrix, preferred_element_type=F32)
+
+
+def group_columns(channels, offset, length, axis):
+    size = (channels, length) if axis else (length, channels)
+    shift = (channels // GN_GROUPS).bit_length() - 1
+    channel = lax.broadcasted_iota(jnp.int32, size, 1 - axis)
+    short = lax.broadcasted_iota(jnp.int32, size, axis)
+    hit = lax.shift_right_logical(channel, shift) + offset == short
+    return (1.0 * hit).astype(BF16)
+
+
 def grad_kernel(dims, cotangent, one, three, weights, out, padded):
     cells, cols, channels, tiles = dims
     place = standing(tiles)
-    above, below = edges(place, one[cols : 2 * cols], three[cols : 2 * cols])
-    padded[0:cols] = jnp.where(place[0] > 0, above, jnp.zeros_like(above))
-    padded[cols : cols + cells] = cotangent[...]
-    padded[cols + cells :] = jnp.where(place[0] < tiles - 1, below, jnp.zeros_like(below))
-    out[...] = conv(padded, weights, cells, cols, True)
-
-
-def third_kernel(dims, n_stats, hidden, one, three, grad_active, adaptive_bias, *rest):
+    above, below = edges(place, one[cols : 3 * cols], three[cols : 3 * cols])
+    padded[0 : 2 * cols] = jnp.where(place[0] > 0, above, jnp.zeros_like(above))
+    padded[2 * cols : 2 * cols + cells] = cotangent[...]
+    padded[2 * cols + cells :] = jnp.where(place[0] < tiles - 1, below, jnp.zeros_like(below))
+    out[...] = conv(padded, weights, cells + 2 * cols, cols, True)
+
+
+def halves(values):
+    high = values.astype(BF16)
+    return high, (values - high.astype(F32)).astype(BF16)
+
+
+def cross_kernel(
+    dims, images, one, three, stat_one, gain, bias, hidden, turned, grouped, slope, moved, matrix, shifts
+):
     cells, cols, channels, tiles = dims
     place = standing(tiles)
-    stat_refs, (active, grad_norm, stat, out_one, out_two, out_three) = rest[:n_stats], rest[n_stats:]
+    above, below = edges(place, one[0:cols], three[0:cols])
+
+    def pieces(block):
+        normed = (block.astype(F32) - stat_one[0:1]) * stat_one[1:2]
+        pre = normed * gain[...] + bias[...]
+        gate = sigmoid(pre)
+        grade = gate * (1.0 + pre * (1.0 - gate)) * gain[...]
+        return grade, grade * normed
+
+    own = pieces(images[...])
+    slope[...], moved[...] = own
+    top = [jnp.where(place[0] > 0, part, 0.0) for part in pieces(above)]
+    bottom = [jnp.where(place[0] < tiles - 1, part, 0.0) for part in pieces(below)]
+    for which in range(2):
+        whole = jnp.concatenate([top[which], own[which], bottom[which]], axis=0)
+        shifts[which, 0] = shifted(whole, cols, 1).astype(BF16)
+        shifts[which, 1] = whole.astype(BF16)
+        shifts[which, 2] = shifted(whole, cols, -1).astype(BF16)
+    unit = 1.0 * (lax.broadcasted_iota(jnp.int32, (channels, channels), 0) == lax.broadcasted_iota(jnp.int32, (channels, channels), 1))
+    hidden_turned = lax.dot_general(
+        unit.astype(BF16), hidden[...], (((1,), (1,)), ((), ())), preferred_element_type=F32
+    ).astype(BF16)
+    spread = jnp.zeros((channels, 4 * GN_GROUPS), F32)
+    flat = jnp.zeros((GN_GROUPS, 4 * GN_GROUPS), F32)
+    for which in range(2):
+        total, plain = None, None
+        for j in range(3):
+            lines = [
+                jnp.sum(shifts[which, j, r * cols : (r + 1) * cols].astype(F32), axis=0, keepdims=True)
+                for r in range(cells // cols + 2)
+            ]
+            for i in range(3):
+                product = jnp.dot(
+                    hidden_turned,
+                    shifts[which, j, i * cols : i * cols + cells],
+                    preferred_element_type=F32,
+                ) * turned[3 * i + j].astype(F32)
+                total = product if total is None else total + product
+                line = grouped[3 * i + j] * tree_sum(lines[i : i + cells // cols])
+                plain = line if plain is None else plain + line
+        for part in halves(total):
+            spread += jnp.dot(
+                part, group_columns(channels, which * GN_GROUPS, 4 * GN_GROUPS, 1), preferred_element_type=F32
+            )
+        for part in halves(plain):
+            flat += jnp.dot(
+                part, group_columns(channels, (2 + which) * GN_GROUPS, 4 * GN_GROUPS, 1), preferred_element_type=F32
+            )
+    summed = jnp.sum(spread.reshape(GN_GROUPS, channels // GN_GROUPS, 4 * GN_GROUPS), axis=1)
+    matrix[...] = jnp.concatenate(halves(summed + flat), axis=1)
+
+
+def third_kernel(
+    dims, n_stats, hidden, one, three, grad_active, adaptive_bias, turned, slope, moved, matrix, *rest
+):
+    cells, cols, channels, tiles = dims
+    place = standing(tiles)
+    stat_refs, (active, grad_norm, stat, out, padded) = rest[:n_stats], rest[n_stats:]
     count = cells * (channels // GN_GROUPS)
     stats = stat_list(stat_refs, (0, cols, 0, cols), tiles)
     mean, inverse = joint_moments(stats, count)
@@ -235,31 +328,40 @@
     stat[...] = rows8(mean, inverse, factor)
     above, below = edges(place, one[0:cols], three[0:cols])
 
-    def pieces(block):
+    def piece(block, start, inside):
+        stop = start + block.shape[0]
         normed = (block.astype(F32) - mean) * inverse
         pre = normed * factor + shift
-        return normed, pre, sigmoid(pre)
-
-    _, pre, gate = pieces(above)
-    active[0:cols] = jnp.where(place[0] > 0, pre * gate, 0.0).astype(BF16)
-    _, pre, gate = pieces(below)
-    active[cols + cells :] = jnp.where(place[0] < tiles - 1, pre * gate, 0.0).astype(BF16)
-    normed, pre, gate = pieces(hidden[...])
-    active[cols : cols + cells] = (pre * gate).astype(BF16)
-    grad_pre = grad_active[...] * (gate * (1.0 + pre * (1.0 - gate)))
-    grad_norm[...] = grad_pre * factor
-    block = terms(
+        gate = sigmoid(pre)
+        grad_pre = grad_active[start:stop] * (gate * (1.0 + pre * (1.0 - gate)))
+        grad = grad_pre * factor
+        grad_norm[start:stop] = grad
+        result, scaled = pre * gate, grad * inverse
+        if inside is not None:
+            result, scaled = jnp.where(inside, result, 0.0), jnp.where(inside, scaled, 0.0)
+        active[start:stop] = result.astype(BF16)
+        padded[start:stop] = scaled.astype(BF16)
+        return normed, grad_pre
+
+    piece(above, 0, place[0] > 0)
+    normed, grad_pre = piece(hidden[...], cols, None)
+    piece(below, cols + cells, place[0] < tiles - 1)
+    base = conv(padded, turned, cells, cols, True, True)
+    out[0:STAT_ROWS] = terms(
         rows8(
             jnp.sum(grad_pre * normed, axis=0, keepdims=True),
             jnp.sum(grad_pre, axis=0, keepdims=True),
+            jnp.sum(base * slope[...], axis=0, keepdims=True),
+            jnp.sum(base * moved[...], axis=0, keepdims=True),
         )
     )
-    start_one, start_three = starts(place, cells, cols)
-    out_one[0:cols] = grad_norm[pl.ds(start_one, cols)].astype(BF16)
-    out_three[0:cols] = grad_norm[pl.ds(start_three, cols)].astype(BF16)
-    out_one[cols:] = block
-    out_two[...] = block
-    out_three[cols:] = block
+    out[STAT_ROWS:] = matrix[...]
+
+
+def pairs_kernel(dims, n_stats, embed, *rest):
+    cells, cols, channels, tiles = dims
+    sums = tree_sum(stat_list(rest[:n_stats], (0, 0, 0, 0), tiles))
+    rest[n_stats][...] = rows8(sums[0:1], sums[1:2], embed[2:3])
 
 
 def branch_kernel(dims, active, weights, out, token):
@@ -269,51 +371,53 @@
 
 
 def fourth_kernel(
-    dims, n_stats, token, grad_norm, one, three, hidden, hidden_one, hidden_three, stat_two,
-    weights, images, stat_one, gain, bias, embed, *rest
+    dims, n_stats, token, grad_norm, hidden, one, three, stat_two, turned, images, stat_one, slope, *rest
 ):
     cells, cols, channels, tiles = dims
     place = standing(tiles)
-    stat_refs, (grad_first, out, pairs, padded) = rest[:n_stats], rest[n_stats:]
+    stat_refs, (out, padded) = rest[:n_stats], rest[n_stats:]
     total = cells * (channels // GN_GROUPS) * tiles
-    sums = tree_sum(stat_list(stat_refs, (0, cols, 0, cols), tiles))
-    pairs[...] = rows8(sums[0:1], sums[1:2], embed[2:3])
+    if len(stat_refs) == 1:
+        size = stat_refs[0].shape[0] // tiles
+        blocks = [stat_refs[0][size * t + STAT_ROWS : size * (t + 1)] for t in range(tiles)]
+    else:
+        blocks = [ref[STAT_ROWS:] for ref in stat_refs]
+    width = 4 * GN_GROUPS
+    matrix = tree_sum([b[:, :width].astype(F32) + b[:, width:].astype(F32) for b in blocks])
+    sums = tree_sum(stat_list(stat_refs, (0, 0, 0, 0), tiles))
     mean, inverse, factor = stat_two[0:1], stat_two[1:2], stat_two[2:3]
-    groups = group_matrix(channels)
-    means = group_sums(sums * factor, groups) / total
-    paired, plain = means[0:1], means[1:2]
+    row = lax.broadcasted_iota(jnp.int32, (8, channels), 0)
+    reduced = group_sums(jnp.where(row < 2, sums * factor, sums), group_matrix(channels))
+    paired, plain = reduced[0:1] / total, reduced[1:2] / total
     above, below = edges(place, one[0:cols], three[0:cols])
-    hidden_above, hidden_below = edges(place, hidden_one[0:cols], hidden_three[0:cols])
 
     def grad_hidden(grad, block):
         normed = (block.astype(F32) - mean) * inverse
-        return inverse * (grad.astype(F32) - plain - normed * paired)
-
-    padded[0:cols] = jnp.where(place[0] > 0, grad_hidden(above, hidden_above), 0.0).astype(BF16)
-    padded[cols : cols + cells] = grad_hidden(grad_norm[...], hidden[...]).astype(BF16)
+        return inverse * (grad - plain - normed * paired)
+
+    padded[0:cols] = jnp.where(place[0] > 0, grad_hidden(grad_norm[0:cols], above), 0.0).astype(BF16)
+    padded[cols : cols + cells] = grad_hidden(grad_norm[cols : cols + cells], hidden[...]).astype(BF16)
     padded[cols + cells :] = jnp.where(
-        place[0] < tiles - 1, grad_hidden(below, hidden_below), 0.0
+        place[0] < tiles - 1, grad_hidden(grad_norm[cols + cells :], below), 0.0
     ).astype(BF16)
-    grad_active = conv(padded, weights, cells, cols, True)
+    grad = conv(padded, turned, cells, cols, True, True) * slope[...]
+    beta = paired * inverse * inverse
+    alpha = plain * inverse - beta * mean
+    per = channels // GN_GROUPS
+    weights = terms(rows8(alpha / per, beta / per))
+    picked = jnp.dot(weights, group_columns(channels, 0, GN_GROUPS, 1), preferred_element_type=F32)
+    picked = picked[0:8] + (picked[8:16] + picked[16:24])
+    found = jnp.dot(picked, matrix, precision=lax.Precision.HIGHEST, preferred_element_type=F32)
+    found = terms(rows8(pltpu.roll(found, width // 2, 1)[0:1] + found[1:2]))
+    means = []
+    for which in range(2):
+        back = jnp.dot(
+            found, group_columns(channels, which * GN_GROUPS, width, 0), preferred_element_type=F32
+        )
+        back = back[0:8] + (back[8:16] + back[16:24])
+        means.append((reduced[2 + which : 3 + which] - back[0:1]) / total)
     normed = (images[...].astype(F32) - stat_one[0:1]) * stat_one[1:2]
-    pre = normed * gain[...] + bias[...]
-    gate = sigmoid(pre)
-    grad = grad_active * (gate * (1.0 + pre * (1.0 - gate))) * gain[...]
-    grad_first[...] = grad
-    sums_first = rows8(
-        jnp.sum(grad, axis=0, keepdims=True), jnp.sum(grad * normed, axis=0, keepdims=True)
-    )
-    out[...] = terms(group_sums(sums_first, groups))
-
-
-def fifth_kernel(dims, n_stats, grad_first, images, stat_one, *rest):
-    cells, cols, channels, tiles = dims
-    stat_refs, (out,) = rest[:n_stats], rest[n_stats:]
-    total = cells * (channels // GN_GROUPS) * tiles
-    means = tree_sum(stat_list(stat_refs, (0, 0, 0, 0), tiles)) / total
-    inverse = stat_one[1:2]
-    normed = (images[...].astype(F32) - stat_one[0:1]) * inverse
-    out[...] = (inverse * (grad_first[...] - means[0:1] - normed * means[1:2])).astype(BF16)
+    out[...] = (stat_one[1:2] * (grad - means[0] - normed * means[1])).astype(BF16)
 
 
 def weight_kernel(*rest):
@@ -366,7 +470,7 @@
     return lax.ppermute(values, axis, [(i, i ^ distance) for i in range(size)])
 
 
-def exchange(one, two, three, stat_start):
+def exchange(one, two, three):
     tiles = lax.axis_size("tile")
     if tiles == 4:
         got = [swap(part, "tile", tiles, k + 1) for k, part in enumerate((one, two, three))]
@@ -408,7 +512,7 @@
     padded = pltpu.VMEM((cells + 2 * cols, channels), BF16)
     small = shape((STAT_ROWS, channels), BF16)
     halo = shape((cols + STAT_ROWS, channels), BF16)
-    halos = shape((2 * cols + STAT_ROWS, channels), BF16)
+    halos = shape((3 * cols + STAT_ROWS, channels), BF16)
     block = shape((8, channels), F32)
     wide = shape((cells, channels), F32)
     narrow = shape((cells, channels), BF16)
@@ -444,7 +548,14 @@
         spaces=spaces,
     )
     flat, flat_cot, time_weight, mix, class_table, time_bias, gain, bias, adaptive_bias, weights_first, weights_second = held
-    image_one, image_three, stats = exchange(one, two, three, 2 * cols)
+    image_one, image_three, stats = exchange(one, two, three)
+    turned, grouped = call(
+        turn_kernel,
+        (shape((9, channels, channels), BF16), shape((9, GN_GROUPS, channels), F32)),
+        (weights_first,),
+        flops=conv_flops,
+        name="turn",
+    )
     embed = call(
         embed_kernel,
         block,
@@ -461,42 +572,58 @@
         conv_flops,
         name="second",
     )
-    hidden_one, hidden_three, stats = exchange(one, two, three, cols)
+    hidden_one, hidden_three, stats = exchange(one, two, three)
     grad_active = call(
         functools.partial(grad_kernel, dims),
-        wide,
+        shape((cells + 2 * cols, channels), F32),
         (flat_cot, image_one, image_three, weights_second),
+        (pltpu.VMEM((cells + 4 * cols, channels), BF16),),
+        conv_flops,
+        name="grad",
+    )
+    slope, moved, matrix = call(
+        functools.partial(cross_kernel, dims),
+        (wide, wide, shape((GN_GROUPS, 8 * GN_GROUPS), BF16)),
+        (flat, image_one, image_three, stat_one, gain, bias, hidden, turned, grouped),
+        (pltpu.VMEM((2, 3, cells + 2 * cols, channels), BF16),),
+        conv_flops,
+        name="cross",
+    )
+    active, grad_norm, stat_two, message = call(
+        functools.partial(third_kernel, dims, len(stats)),
+        (
+            shape((cells + 2 * cols, channels), BF16),
+            shape((cells + 2 * cols, channels), F32),
+            block,
+            shape((STAT_ROWS + GN_GROUPS, channels), BF16),
+        ),
+        (hidden, hidden_one, hidden_three, grad_active, adaptive_bias, turned, slope, moved, matrix, *stats),
         (padded,),
         conv_flops,
-        name="grad",
-    )
-    active, grad_norm, stat_two, one, two, three = call(
-        functools.partial(third_kernel, dims, len(stats)),
-        (shape((cells + 2 * cols, channels), BF16), wide, block, halo, small, halo),
-        (hidden, hidden_one, hidden_three, grad_active, adaptive_bias, *stats),
-        flops=1000,
         name="third",
     )
-    grad_one, grad_three, stats = exchange(one, two, three, cols)
+    stats = spread_small(message)
     branch, token = call(
-        functools.partial(branch_kernel, dims), (narrow, shape((8, 128), F32)), (active, weights_second), flops=conv_flops, name="branch"
-    )
-    grad_first, sums, pairs = call(
-        functools.partial(fourth_kernel, dims, len(stats)),
-        (wide, small, block),
-        (token, grad_norm, grad_one, grad_three, hidden, hidden_one, hidden_three, stat_two,
-         weights_first, flat, stat_one, gain, bias, embed, *stats),
-        (padded,),
-        conv_flops,
-        name="fourth",
-    )
-    stats = spread_small(sums)
+        functools.partial(branch_kernel, dims),
+        (narrow, shape((8, 128), F32)),
+        (active, weights_second),
+        flops=conv_flops,
+        name="branch",
+    )
+    pairs = call(
+        functools.partial(pairs_kernel, dims, len(stats)), block, (embed, *stats), name="pairs"
+    )
     if fleet == 4:
         pair_list = [pairs, *(swap(pairs, "image", fleet, k) for k in (1, 2, 3))]
     else:
         pair_list = [lax.all_gather(pairs, "image", axis=0, tiled=True)]
     input_grad = call(
-        functools.partial(fifth_kernel, dims, len(stats)), narrow, (grad_first, flat, stat_one, *stats), name="fifth"
+        functools.partial(fourth_kernel, dims, len(stats)),
+        narrow,
+        (token, grad_norm, hidden, hidden_one, hidden_three, stat_two, turned, flat, stat_one, slope, *stats),
+        (padded,),
+        conv_flops,
+        name="fourth",
     )
     grad_weight, grad_bias = call(
         weight_kernel,

time: 40.6 us -> 38.1 us (0.938)
  Pallas kernels: 8.57 us -> 12.5 us
  waiting for transfers between devices: 11.1 us -> 7.5 us
  starting transfers between devices: 18.8 us -> 15.9 us
    pallas_call x9 -> x11, Pallas kernels: 8.57 us -> 12.5 us  [call(): pl.pallas_call(kernel, out_shape=out_shapes, in_specs=[pl.BlockSpec(memor...]
    ppermute x15 -> x12, waiting for transfers between devices: 11.1 us -> 7.5 us  [swap(): return lax.ppermute(values, axis, [(i, i ^ distance) for i in range(size)])]
    ppermute x15 -> x12, starting transfers between devices: 18.8 us -> 15.9 us  [swap(): return lax.ppermute(values, axis, [(i, i ^ distance) for i in range(size)])]
  transfers between devices with their start and end apart: 15 -> 12, of which waited for: 4 -> 4; matrix products, arithmetic and copies ran while one was open for 0% -> 0% of each run, Pallas kernels for 9% -> 19%
where the time goes in v4:
time: 38.1 us; the launch traced here: 37.9 us
  starting transfers between devices  15.9 us (42%)
  Pallas kernels  12.5 us (33%)
  waiting for transfers between devices  7.5 us (20%)
  between operations  1.98 us (5%)
    ppermute x12, starting transfers between devices, swap(): return lax.ppermute(values, axis, [(i, i ^ distance) for i in range(size)])  15.9 us
    pallas_call x11, Pallas kernels, call(): pl.pallas_call(kernel, out_shape=out_shapes, in_specs=[pl.BlockSpec(memor...  12.5 us
    ppermute x12, waiting for transfers between devices, swap(): return lax.ppermute(values, axis, [(i, i ^ distance) for i in range(size)])  7.5 us
  transfers between devices with their start and end apart: 12, of which 4 were waited for; matrix products, arithmetic and copies ran while one was open for 0% of the time, Pallas kernels for 19%

profile of v4, /device:TPU:0, one launch (start us, length us, event | category | flops | bytes accessed | tf_op | source)
XLA Modules:
  0.0 37.9 jit_solution(12966358995353038860)
XLA Ops:
  0.6 2.2 %first.1 = (bf16[256,256]{1,0:T(8,128)(2,1)S(1)}, bf16[256,256]{1,0:T(8,128)(2,1)S(1)}, bf16[256,256]{1,0:T(8,128)(2,1)S(1)}, bf16[256,512]{1,0:T(8,128)(2,1)S(1...) custom-call(bf16[256,256]{1,0:T(8,128)(2,1)} %bitcast.14, ...), custom_call_target="tpu_custom_call" | custom-call | flops 1000 | bytes 3531776 | tf_op jit(solution)/shard_map/first/pallas_call | solution.py:455
  2.9 3.1 %collective-permute-start = (bf16[224,256]{1,0:T(8,128)(2,1)S(1)}, bf16[224,256]{1,0:T(8,128)(2,1)S(1)}, u32[]{:S(2)}, u32[]{:S(2)}) collective-permute-start(bf16[224,256]{1,0:T(8,128)(2,1)S(1)} %get-tuple-element.37), channel_id=1, source_target_pairs={{0,4},{4,0},{8,12},{12,8},{1,5},{5,1},{9,13},{13,9},{2,6},{6,2},{1... | collective-permute-start | bytes 344072 | tf_op jit(solution)/shard_map/ppermute | solution.py:470
  6.0 2.5 %collective-permute-start.1 = (bf16[224,256]{1,0:T(8,128)(2,1)S(1)}, bf16[224,256]{1,0:T(8,128)(2,1)S(1)}, u32[]{:S(2)}, u32[]{:S(2)}) collective-permute-start(bf16[224,256]{1,0:T(8,128)(2,1)S(1)} %get-tuple-element.38), channel_id=1, source_target_pairs={{0,12},{4,8},{8,4},{12,0},{1,13},{5,9},{9,5},{13,1},{2,14},{6,10},... | collective-permute-start | bytes 344072 | tf_op jit(solution)/shard_map/ppermute | solution.py:470
  8.4 0.1 collective-permute-start.2
  9.8 0.4 %embed.1 = f32[8,256]{1,0:T(8,128)S(1)} custom-call(s32[1]{0:T(128)S(6)} %copy.17.step, s32[1]{0:T(128)S(6)} %copy.18.label, bf16[1000,256]{1,0:T(8,128)(2,1)S(1)} %get-tuple-element.42.table, bf16[256,256]{1,0:T(8,128)(2,1)S(1)} %get-tuple-element.43.time_weight, f32[1,256]{1,0:T(1,128)S(1)} %get-tuple-element.44.time_bias, ...), custom_call_target="tpu_custom_call" | custom-call | flops 1000 | bytes 906248 | tf_op jit(solution)/shard_map/embed/pallas_call | solution.py:455
  10.2 1.6 %turn.1 = (bf16[9,256,256]{2,1,0:T(8,128)(2,1)S(1)}, f32[9,32,256]{2,1,0:T(8,128)S(1)}) custom-call(bf16[9,256,256]{2,1,0:T(8,128)(2,1)S(1)} %get-tuple-element.39.weights), custom_call_target="tpu_custom_call" | custom-call | flops 301989888 | bytes 1179648 | tf_op jit(solution)/shard_map/turn/pallas_call | solution.py:455
  11.9 2.7 %collective-permute-done.2.rest_2_ = bf16[32,256]{1,0:T(8,128)(2,1)S(1)} collective-permute-done((bf16[32,256]{1,0:T(8,128)(2,1)S(1)}, bf16[32,256]{1,0:T(8,128)(2,1)S(1)}, u32[]{:S(2)}, u32[]{:S(2)}) %collective-permute-start.2) | collective-permute-done | bytes 16416 | tf_op jit(solution)/shard_map/ppermute | solution.py:470
  14.6 0.0 collective-permute-done.one.rest_1_
  14.6 0.0 collective-permute-done.1.three.rest_3_
  14.6 0.9 %second.1 = (bf16[256,256]{1,0:T(8,128)(2,1)S(1)}, f32[8,256]{1,0:T(8,128)S(1)}, bf16[96,256]{1,0:T(8,128)(2,1)S(1)}, bf16[32,256]{1,0:T(8,128)(2,1)S(1)}, bf16[96,256]{1,0:T(8,128)(2,1)S(1)}) custom-call(bf16[256,256]{1,0:T(8,128)(2,1)S(1)} %get-tuple-element.36.images, bf16[224,256]{1,0:T(8,128)(2,1)S(1)} %collective-permute-done.one.rest_1_, ...), custom_call_target="tpu_custom_call" | custom-call | flops 301989888 | bytes 1812480 | tf_op jit(solution)/shard_map/second/pallas_call | solution.py:455
  15.5 0.4 %collective-permute-start.3 = (bf16[96,256]{1,0:T(8,128)(2,1)S(1)}, bf16[96,256]{1,0:T(8,128)(2,1)S(1)}, u32[]{:S(2)}, u32[]{:S(2)}) collective-permute-start(bf16[96,256]{1,0:T(8,128)(2,1)S(1)} %get-tuple-element.48), channel_id=1, source_target_pairs={{0,4},{4,0},{8,12},{12,8},{1,5},{5,1},{9,13},{13,9},{2,6},{6,2},{1... | collective-permute-start | bytes 147464 | tf_op jit(solution)/shard_map/ppermute | solution.py:470
  15.9 2.6 %collective-permute-start.4 = (bf16[96,256]{1,0:T(8,128)(2,1)S(1)}, bf16[96,256]{1,0:T(8,128)(2,1)S(1)}, u32[]{:S(2)}, u32[]{:S(2)}) collective-permute-start(bf16[96,256]{1,0:T(8,128)(2,1)S(1)} %get-tuple-element.49), channel_id=1, source_target_pairs={{0,12},{4,8},{8,4},{12,0},{1,13},{5,9},{9,5},{13,1},{2,14},{6,10},... | collective-permute-start | bytes 147464 | tf_op jit(solution)/shard_map/ppermute | solution.py:470
  18.6 0.5 %collective-permute-start.5 = (bf16[32,256]{1,0:T(8,128)(2,1)S(1)}, bf16[32,256]{1,0:T(8,128)(2,1)S(1)}, u32[]{:S(2)}, u32[]{:S(2)}) collective-permute-start(bf16[32,256]{1,0:T(8,128)(2,1)S(1)} %get-tuple-element.59.rest_0_), channel_id=1, source_target_pairs={{0,8},{4,12},{8,0},{12,4},{1,9},{5,13},{9,1},{13,5},{2,10},{6,14},... | collective-permute-start | bytes 49160 | tf_op jit(solution)/shard_map/ppermute | solution.py:470
  19.0 0.7 %grad.1.grad_active = f32[384,256]{1,0:T(8,128)S(1)} custom-call(bf16[256,256]{1,0:T(8,128)(2,1)S(1)} %get-tuple-element.50.cotangent, bf16[224,256]{1,0:T(8,128)(2,1)S(1)} %collective-permute-done.one.rest_1_, bf16[224,256]{1,0:T(8,128)(2,1)S(1)} %collective-permute-done.1.three.rest_3_, bf16[9,256,256]{2,1,0:T(8,128)(2,1)S(1)} %get-tuple-element.51.weights), custom_call_target="tpu_custom_call" | custom-call | flops 301989888 | bytes 1540096 | tf_op jit(solution)/shard_map/grad/pallas_call | solution.py:455
  19.7 1.8 %cross.1 = (f32[256,256]{1,0:T(8,128)S(1)}, f32[256,256]{1,0:T(8,128)S(1)}, bf16[32,256]{1,0:T(8,128)(2,1)S(1)}) custom-call(bf16[256,256]{1,0:T(8,128)(2,1)S(1)} %get-tuple-element.36.images, bf16[224,256]{1,0:T(8,128)(2,1)S(1)} %collective-permute-done.one.rest_1_, bf16[224,256]{1,0:T(8,128)(2,1)S(1)} %collective-permute-done.1.three.rest_3_, ...), custom_call_target="tpu_custom_call" | custom-call | flops 301989888 | bytes 1976320 | tf_op jit(solution)/shard_map/cross/pallas_call | solution.py:455
  21.5 1.7 %collective-permute-done.5.rest_2_ = bf16[32,256]{1,0:T(8,128)(2,1)S(1)} collective-permute-done((bf16[32,256]{1,0:T(8,128)(2,1)S(1)}, bf16[32,256]{1,0:T(8,128)(2,1)S(1)}, u32[]{:S(2)}, u32[]{:S(2)}) %collective-permute-start.5) | collective-permute-done | bytes 16416 | tf_op jit(solution)/shard_map/ppermute | solution.py:470
  23.2 0.0 collective-permute-done.3.one.rest_1_
  23.2 0.0 collective-permute-done.4.three.rest_3_
  23.2 0.7 %third.1 = (bf16[384,256]{1,0:T(8,128)(2,1)S(1)}, f32[384,256]{1,0:T(8,128)S(1)}, f32[8,256]{1,0:T(8,128)S(1)}, bf16[64,256]{1,0:T(8,128)(2,1)S(1)}) custom-call(bf16[256,256]{1,0:T(8,128)(2,1)S(1)} %get-tuple-element.47.hidden, bf16[96,256]{1,0:T(8,128)(2,1)S(1)} %collective-permute-done.3.one.rest_1_, ...), custom_call_target="tpu_custom_call" | custom-call | flops 301989888 | bytes 2476032 | tf_op jit(solution)/shard_map/third/pallas_call | solution.py:455
  23.9 0.8 %collective-permute-start.6 = (bf16[64,256]{1,0:T(8,128)(2,1)S(1)}, bf16[64,256]{1,0:T(8,128)(2,1)S(1)}, u32[]{:S(2)}, u32[]{:S(2)}) collective-permute-start(bf16[64,256]{1,0:T(8,128)(2,1)S(1)} %get-tuple-element.65.rest_0_), channel_id=1, source_target_pairs={{0,4},{4,0},{8,12},{12,8},{1,5},{5,1},{9,13},{13,9},{2,6},{6,2},{1... | collective-permute-start | bytes 98312 | tf_op jit(solution)/shard_map/ppermute | solution.py:470
  24.7 1.4 %collective-permute-start.7 = (bf16[64,256]{1,0:T(8,128)(2,1)S(1)}, bf16[64,256]{1,0:T(8,128)(2,1)S(1)}, u32[]{:S(2)}, u32[]{:S(2)}) collective-permute-start(bf16[64,256]{1,0:T(8,128)(2,1)S(1)} %get-tuple-element.65.rest_0_), channel_id=1, source_target_pairs={{0,8},{4,12},{8,0},{12,4},{1,9},{5,13},{9,1},{13,5},{2,10},{6,14},... | collective-permute-start | bytes 98312 | tf_op jit(solution)/shard_map/ppermute | solution.py:470
  26.1 2.2 %collective-permute-start.8 = (bf16[64,256]{1,0:T(8,128)(2,1)S(1)}, bf16[64,256]{1,0:T(8,128)(2,1)S(1)}, u32[]{:S(2)}, u32[]{:S(2)}) collective-permute-start(bf16[64,256]{1,0:T(8,128)(2,1)S(1)} %get-tuple-element.65.rest_0_), channel_id=1, source_target_pairs={{0,12},{4,8},{8,4},{12,0},{1,13},{5,9},{9,5},{13,1},{2,14},{6,10},... | collective-permute-start | bytes 98312 | tf_op jit(solution)/shard_map/ppermute | solution.py:470
  28.4 1.1 %branch.1 = (bf16[256,256]{1,0:T(8,128)(2,1)}, f32[8,128]{1,0:T(8,128)S(1)}) custom-call(bf16[384,256]{1,0:T(8,128)(2,1)S(1)} %get-tuple-element.60.active, bf16[9,256,256]{2,1,0:T(8,128)(2,1)S(1)} %get-tuple-element.51.weights), custom_call_target="tpu_custom_call" | custom-call | flops 301989888 | bytes 1376256 | tf_op jit(solution)/shard_map/branch/pallas_call | solution.py:455
  29.5 0.0 collective-permute-done.6.rest_1_
  29.5 0.0 collective-permute-done.7.rest_2_
  29.5 2.3 %collective-permute-done.8.rest_3_ = bf16[64,256]{1,0:T(8,128)(2,1)S(1)} collective-permute-done((bf16[64,256]{1,0:T(8,128)(2,1)S(1)}, bf16[64,256]{1,0:T(8,128)(2,1)S(1)}, u32[]{:S(2)}, u32[]{:S(2)}) %collective-permute-start.8) | collective-permute-done | bytes 32800 | tf_op jit(solution)/shard_map/ppermute | solution.py:470
  31.9 1.6 %collective-permute-start.10 = (f32[8,256]{1,0:T(8,128)S(1)}, f32[8,256]{1,0:T(8,128)S(1)}, u32[]{:S(2)}, u32[]{:S(2)}) collective-permute-start(f32[8,256]{1,0:T(8,128)S(1)} %pairs.1.rest_0_), channel_id=1, source_target_pairs={{0,2},{1,3},{2,0},{3,1},{4,6},{5,7},{6,4},{7,5},{8,10},{9,11},{10,... | collective-permute-start | bytes 24584 | tf_op jit(solution)/shard_map/ppermute | solution.py:470
  33.4 0.0 collective-permute-start.11
  33.4 0.6 %collective-permute-start.9 = (f32[8,256]{1,0:T(8,128)S(1)}, f32[8,256]{1,0:T(8,128)S(1)}, u32[]{:S(2)}, u32[]{:S(2)}) collective-permute-start(f32[8,256]{1,0:T(8,128)S(1)} %pairs.1.rest_0_), channel_id=1, source_target_pairs={{0,1},{1,0},{2,3},{3,2},{4,5},{5,4},{6,7},{7,6},{8,9},{9,8},{10,11... | collective-permute-start | bytes 24584 | tf_op jit(solution)/shard_map/ppermute | solution.py:470
  34.1 1.7 %fourth.1 = bf16[256,256]{1,0:T(8,128)(2,1)} custom-call(f32[8,128]{1,0:T(8,128)S(1)} %get-tuple-element.62.token, f32[384,256]{1,0:T(8,128)S(1)} %get-tuple-element.63.grad_norm, bf16[256,256]{1,0:T(8,128)(2,1)S(1)} %get-tuple-element.47.hidden, bf16[96,256]{1,0:T(8,128)(2,1)S(1)} %collective-permute-done.3.one.rest_1_, ...), custom_call_target="tpu_custom_call" | custom-call | flops 301989888 | bytes 2347008 | tf_op jit(solution)/shard_map/fourth/pallas_call | solution.py:455
  35.7 0.8 %collective-permute-done.11.rest_3_ = f32[8,256]{1,0:T(8,128)S(1)} collective-permute-done((f32[8,256]{1,0:T(8,128)S(1)}, f32[8,256]{1,0:T(8,128)S(1)}, u32[]{:S(2)}, u32[]{:S(2)}) %collective-permute-start.11) | collective-permute-done | bytes 8224 | tf_op jit(solution)/shard_map/ppermute | solution.py:470
  36.5 1.4 %weight.1 = (f32[256,512]{1,0:T(8,128)}, f32[1,512]{1,0:T(1,128)}) custom-call(f32[8,256]{1,0:T(8,128)S(1)} %pairs.1.rest_0_, f32[8,256]{1,0:T(8,128)S(1)} %collective-permute-done.9.rest_1_, f32[8,256]{1,0:T(8,128)S(1)} %collective-permute-done.10.rest_2_, f32[8,256]{1,0:T(8,128)S(1)} %collective-permute-done.11.rest_3_), custom_call_target="tpu_custom_call" | custom-call | flops 1000 | bytes 32768 | tf_op jit(solution)/shard_map/weight/pallas_call | solution.py:455
  (3 shorter events, 0.0 us)
Async XLA Ops:
  2.9 11.7 %collective-permute-start = (bf16[224,256]{1,0:T(8,128)(2,1)S(1)}, bf16[224,256]{1,0:T(8,128)(2,1)S(1)}, u32[]{:S(2)}, u32[]{:S(2)}) collective-permute-start(bf16[224,256]{1,0:T(8,128)(2,1)S(1)} %get-tuple-element.37), channel_id=1, source_target_pairs={{0,4},{4,0},{8,12},{12,8},{1,5},{5,1},{9,13},{13,9},{2,6},{6,2},{1... | collective-permute-start | bytes 344072 | tf_op jit(solution)/shard_map/ppermute | solution.py:470
  6.0 8.6 %collective-permute-start.1 = (bf16[224,256]{1,0:T(8,128)(2,1)S(1)}, bf16[224,256]{1,0:T(8,128)(2,1)S(1)}, u32[]{:S(2)}, u32[]{:S(2)}) collective-permute-start(bf16[224,256]{1,0:T(8,128)(2,1)S(1)} %get-tuple-element.38), channel_id=1, source_target_pairs={{0,12},{4,8},{8,4},{12,0},{1,13},{5,9},{9,5},{13,1},{2,14},{6,10},... | collective-permute-start | bytes 344072 | tf_op jit(solution)/shard_map/ppermute | solution.py:470
  8.4 6.1 %collective-permute-start.2 = (bf16[32,256]{1,0:T(8,128)(2,1)S(1)}, bf16[32,256]{1,0:T(8,128)(2,1)S(1)}, u32[]{:S(2)}, u32[]{:S(2)}) collective-permute-start(bf16[32,256]{1,0:T(8,128)(2,1)S(1)} %get-tuple-element.46.rest_0_), channel_id=1, source_target_pairs={{0,8},{4,12},{8,0},{12,4},{1,9},{5,13},{9,1},{13,5},{2,10},{6,14},... | collective-permute-start | bytes 49160 | tf_op jit(solution)/shard_map/ppermute | solution.py:470
  15.5 7.7 %collective-permute-start.3 = (bf16[96,256]{1,0:T(8,128)(2,1)S(1)}, bf16[96,256]{1,0:T(8,128)(2,1)S(1)}, u32[]{:S(2)}, u32[]{:S(2)}) collective-permute-start(bf16[96,256]{1,0:T(8,128)(2,1)S(1)} %get-tuple-element.48), channel_id=1, source_target_pairs={{0,4},{4,0},{8,12},{12,8},{1,5},{5,1},{9,13},{13,9},{2,6},{6,2},{1... | collective-permute-start | bytes 147464 | tf_op jit(solution)/shard_map/ppermute | solution.py:470
  15.9 7.3 %collective-permute-start.4 = (bf16[96,256]{1,0:T(8,128)(2,1)S(1)}, bf16[96,256]{1,0:T(8,128)(2,1)S(1)}, u32[]{:S(2)}, u32[]{:S(2)}) collective-permute-start(bf16[96,256]{1,0:T(8,128)(2,1)S(1)} %get-tuple-element.49), channel_id=1, source_target_pairs={{0,12},{4,8},{8,4},{12,0},{1,13},{5,9},{9,5},{13,1},{2,14},{6,10},... | collective-permute-start | bytes 147464 | tf_op jit(solution)/shard_map/ppermute | solution.py:470
  18.6 4.6 %collective-permute-start.5 = (bf16[32,256]{1,0:T(8,128)(2,1)S(1)}, bf16[32,256]{1,0:T(8,128)(2,1)S(1)}, u32[]{:S(2)}, u32[]{:S(2)}) collective-permute-start(bf16[32,256]{1,0:T(8,128)(2,1)S(1)} %get-tuple-element.59.rest_0_), channel_id=1, source_target_pairs={{0,8},{4,12},{8,0},{12,4},{1,9},{5,13},{9,1},{13,5},{2,10},{6,14},... | collective-permute-start | bytes 49160 | tf_op jit(solution)/shard_map/ppermute | solution.py:470
  23.9 5.6 %collective-permute-start.6 = (bf16[64,256]{1,0:T(8,128)(2,1)S(1)}, bf16[64,256]{1,0:T(8,128)(2,1)S(1)}, u32[]{:S(2)}, u32[]{:S(2)}) collective-permute-start(bf16[64,256]{1,0:T(8,128)(2,1)S(1)} %get-tuple-element.65.rest_0_), channel_id=1, source_target_pairs={{0,4},{4,0},{8,12},{12,8},{1,5},{5,1},{9,13},{13,9},{2,6},{6,2},{1... | collective-permute-start | bytes 98312 | tf_op jit(solution)/shard_map/ppermute | solution.py:470
  24.7 4.8 %collective-permute-start.7 = (bf16[64,256]{1,0:T(8,128)(2,1)S(1)}, bf16[64,256]{1,0:T(8,128)(2,1)S(1)}, u32[]{:S(2)}, u32[]{:S(2)}) collective-permute-start(bf16[64,256]{1,0:T(8,128)(2,1)S(1)} %get-tuple-element.65.rest_0_), channel_id=1, source_target_pairs={{0,8},{4,12},{8,0},{12,4},{1,9},{5,13},{9,1},{13,5},{2,10},{6,14},... | collective-permute-start | bytes 98312 | tf_op jit(solution)/shard_map/ppermute | solution.py:470
  26.1 5.7 %collective-permute-start.8 = (bf16[64,256]{1,0:T(8,128)(2,1)S(1)}, bf16[64,256]{1,0:T(8,128)(2,1)S(1)}, u32[]{:S(2)}, u32[]{:S(2)}) collective-permute-start(bf16[64,256]{1,0:T(8,128)(2,1)S(1)} %get-tuple-element.65.rest_0_), channel_id=1, source_target_pairs={{0,12},{4,8},{8,4},{12,0},{1,13},{5,9},{9,5},{13,1},{2,14},{6,10},... | collective-permute-start | bytes 98312 | tf_op jit(solution)/shard_map/ppermute | solution.py:470
  31.9 3.9 %collective-permute-start.10 = (f32[8,256]{1,0:T(8,128)S(1)}, f32[8,256]{1,0:T(8,128)S(1)}, u32[]{:S(2)}, u32[]{:S(2)}) collective-permute-start(f32[8,256]{1,0:T(8,128)S(1)} %pairs.1.rest_0_), channel_id=1, source_target_pairs={{0,2},{1,3},{2,0},{3,1},{4,6},{5,7},{6,4},{7,5},{8,10},{9,11},{10,... | collective-permute-start | bytes 24584 | tf_op jit(solution)/shard_map/ppermute | solution.py:470
  33.4 3.1 %collective-permute-start.11 = (f32[8,256]{1,0:T(8,128)S(1)}, f32[8,256]{1,0:T(8,128)S(1)}, u32[]{:S(2)}, u32[]{:S(2)}) collective-permute-start(f32[8,256]{1,0:T(8,128)S(1)} %pairs.1.rest_0_), channel_id=1, source_target_pairs={{0,3},{1,2},{2,1},{3,0},{4,7},{5,6},{6,5},{7,4},{8,11},{9,10},{10,... | collective-permute-start | bytes 24584 | tf_op jit(solution)/shard_map/ppermute | solution.py:470
  33.4 3.1 %collective-permute-start.9 = (f32[8,256]{1,0:T(8,128)S(1)}, f32[8,256]{1,0:T(8,128)S(1)}, u32[]{:S(2)}, u32[]{:S(2)}) collective-permute-start(f32[8,256]{1,0:T(8,128)S(1)} %pairs.1.rest_0_), channel_id=1, source_target_pairs={{0,1},{1,0},{2,3},{3,2},{4,5},{5,4},{6,7},{7,6},{8,9},{9,8},{10,11... | collective-permute-start | bytes 24584 | tf_op jit(solution)/shard_map/ppermute | solution.py:470

commit v5 on v4

--- a/solution.py
+++ b/solution.py
@@ -13,20 +13,25 @@
 VMEM_LIMIT = 12 * 1024 * 1024
 F32, BF16 = jnp.float32, jnp.bfloat16
 
-STAT_ROWS = 32
-
-
-def terms(values):
+STAT_ROWS = 16
+
+
+def split(values):
     high = values.astype(BF16).astype(F32)
     rest = values - high
     middle = rest.astype(BF16).astype(F32)
-    low = (rest - middle).astype(BF16).astype(F32)
-    return jnp.concatenate([high, middle, low, jnp.zeros_like(high)], axis=0).astype(BF16)
+    return high, middle, (rest - middle).astype(BF16).astype(F32)
+
+
+def terms(values):
+    high, middle, low = split(values)
+    return jnp.concatenate([high + pltpu.roll(middle, 4, 0), low], axis=0).astype(BF16)
 
 
 def joined(block):
     wide = block.astype(F32)
-    return wide[0:8] + (wide[8:16] + wide[16:24])
+    total = wide[0:8] + (pltpu.roll(wide[0:8], 4, 0) + wide[8:16])
+    return jnp.where(lax.broadcasted_iota(jnp.int32, total.shape, 0) < 4, total, 0.0)
 
 
 def rows8(*rows):
@@ -46,8 +51,7 @@
 
 
 def group_sums(rows, groups):
-    out = jnp.dot(terms(rows), groups, preferred_element_type=F32)
-    return out[0:8] + (out[8:16] + out[16:24])
+    return joined(jnp.dot(terms(rows), groups, preferred_element_type=F32))
 
 
 def tree_sum(parts):
@@ -168,19 +172,18 @@
         copy.wait()
 
 
-def embed_kernel(step, label, table, time_weight, time_bias, adaptive_weight, out):
+def embed_kernel(instant, table, time_weight, time_bias, adaptive_weight, out):
     channels = adaptive_weight.shape[1] // 2
     half = time_weight.shape[0] // 2
 
     def times(vector, weights):
-        product = jnp.dot(terms(rows8(vector)), weights, preferred_element_type=F32)
-        return (product[0:8] + (product[8:16] + product[16:24]))[0:1]
+        return joined(jnp.dot(terms(rows8(vector)), weights, preferred_element_type=F32))[0:1]
 
     place = lax.broadcasted_iota(jnp.int32, (8, half), 1).astype(F32)
-    angles = step[0].astype(F32) * jnp.exp(-math.log(10000.0) * place / half)
+    angles = instant[0:1, 0:1].astype(F32) * jnp.exp(-math.log(10000.0) * place / half)
     sinusoid = jnp.concatenate([jnp.cos(angles), jnp.sin(angles)], axis=1)[0:1]
     classes = lax.broadcasted_iota(jnp.int32, (16, table.shape[0]), 1)
-    onehot = (classes == label[0]).astype(F32).astype(BF16)
+    onehot = (classes == instant[1:2, 0:1]).astype(F32).astype(BF16)
     row = jnp.dot(onehot, table[...], preferred_element_type=F32)[0:1]
     hidden = times(sinusoid, time_weight[...]) + time_bias[...]
     embedding = hidden * sigmoid(hidden) + row
@@ -219,17 +222,32 @@
     out_three[cols:] = block
 
 
-def turn_kernel(weights, turned, grouped):
+def identity(size):
+    row = lax.broadcasted_iota(jnp.int32, (size, size), 0)
+    return (1.0 * (row == lax.broadcasted_iota(jnp.int32, (size, size), 1))).astype(BF16)
+
+
+def turn_kernel(count, source, *refs):
+    sources, weights, copies_to = refs[:count], refs[count], refs[count + 1 : 2 * count + 1]
+    turned, grouped, sems = refs[2 * count + 1 :]
+    main = pltpu.make_async_copy(source, weights, sems.at[count])
+    copies = [
+        pltpu.make_async_copy(start, end, sems.at[k])
+        for k, (start, end) in enumerate(zip(sources, copies_to, strict=True))
+    ]
+    for copy in (main, *copies):
+        copy.start()
     channels = weights.shape[1]
-    unit = 1.0 * (lax.broadcasted_iota(jnp.int32, (channels, channels), 0) == lax.broadcasted_iota(jnp.int32, (channels, channels), 1))
-    unit = unit.astype(BF16)
-    picks = group_columns(channels, 0, GN_GROUPS, 0)
-    for tap in range(weights.shape[0]):
-        matrix = lax.dot_general(
-            unit, weights[tap], (((1,), (1,)), ((), ())), preferred_element_type=F32
-        ).astype(BF16)
-        turned[tap] = matrix
-        grouped[tap] = jnp.dot(picks, matrix, preferred_element_type=F32)
+    rows = jnp.concatenate([identity(channels), group_columns(channels, 0, GN_GROUPS, 0)], axis=0)
+    main.wait()
+    for k in range(source.shape[0]):
+        product = lax.dot_general(
+            rows, weights[k], (((1,), (1,)), ((), ())), preferred_element_type=F32
+        )
+        turned[k] = product[:channels].astype(BF16)
+        grouped[k] = product[channels:]
+    for copy in copies:
+        copy.wait()
 
 
 def group_columns(channels, offset, length, axis):
@@ -257,7 +275,7 @@
 
 
 def cross_kernel(
-    dims, images, one, three, stat_one, gain, bias, hidden, turned, grouped, slope, moved, matrix, shifts
+    dims, images, one, three, stat_one, gain, bias, hidden, turned, grouped, slope, moved, matrix, factors, left, products
 ):
     cells, cols, channels, tiles = dims
     place = standing(tiles)
@@ -272,35 +290,46 @@
 
     own = pieces(images[...])
     slope[...], moved[...] = own
-    top = [jnp.where(place[0] > 0, part, 0.0) for part in pieces(above)]
-    bottom = [jnp.where(place[0] < tiles - 1, part, 0.0) for part in pieces(below)]
-    for which in range(2):
-        whole = jnp.concatenate([top[which], own[which], bottom[which]], axis=0)
-        shifts[which, 0] = shifted(whole, cols, 1).astype(BF16)
-        shifts[which, 1] = whole.astype(BF16)
-        shifts[which, 2] = shifted(whole, cols, -1).astype(BF16)
-    unit = 1.0 * (lax.broadcasted_iota(jnp.int32, (channels, channels), 0) == lax.broadcasted_iota(jnp.int32, (channels, channels), 1))
-    hidden_turned = lax.dot_general(
-        unit.astype(BF16), hidden[...], (((1,), (1,)), ((), ())), preferred_element_type=F32
-    ).astype(BF16)
+    for which, (top, bottom) in enumerate(zip(pieces(above), pieces(below), strict=True)):
+        factors[which, 0:cols] = jnp.where(place[0] > 0, top, 0.0).astype(BF16)
+        factors[which, cols : cols + cells] = own[which].astype(BF16)
+        factors[which, cols + cells :] = jnp.where(place[0] < tiles - 1, bottom, 0.0).astype(BF16)
+    wide = hidden[...].astype(F32)
+    unit = identity(channels)
+    for j, line in enumerate((shifted(wide, cols, -1).astype(BF16), hidden[...], shifted(wide, cols, 1).astype(BF16))):
+        left[j * channels : (j + 1) * channels] = lax.dot_general(
+            unit, line, (((1,), (1,)), ((), ())), preferred_element_type=F32
+        ).astype(BF16)
+    row = lax.broadcasted_iota(jnp.int32, (16, cells), 0)
+    column = lax.bitwise_and(lax.broadcasted_iota(jnp.int32, (16, cells), 1), cols - 1)
+    inside = jnp.where(row == 0, 1.0 * (column < cols - 1), jnp.where(row == 2, 1.0 * (column > 0), 1.0))
+    left[3 * channels :] = inside.astype(BF16)
+    for i in range(3):
+        for which in range(2):
+            products[which, i] = jnp.dot(
+                left[...], factors[which, i * cols : i * cols + cells], preferred_element_type=F32
+            )
+    step = channels // 8
+    totals = ([], [])
+    for start in range(0, channels, step):
+        parts = ([], [])
+        for k in range(9):
+            matrix_rows = turned[k, start : start + step].astype(F32)
+            for which in range(2):
+                begin = (k % 3) * channels + start
+                parts[which].append(products[which, k // 3, begin : begin + step] * matrix_rows)
+        for which in range(2):
+            totals[which].append(tree_sum(parts[which]))
     spread = jnp.zeros((channels, 4 * GN_GROUPS), F32)
     flat = jnp.zeros((GN_GROUPS, 4 * GN_GROUPS), F32)
     for which in range(2):
-        total, plain = None, None
-        for j in range(3):
-            lines = [
-                jnp.sum(shifts[which, j, r * cols : (r + 1) * cols].astype(F32), axis=0, keepdims=True)
-                for r in range(cells // cols + 2)
+        total = jnp.concatenate(totals[which], axis=0)
+        plain = tree_sum(
+            [
+                grouped[k] * products[which, k // 3, 3 * channels + k % 3 : 3 * channels + k % 3 + 1]
+                for k in range(9)
             ]
-            for i in range(3):
-                product = jnp.dot(
-                    hidden_turned,
-                    shifts[which, j, i * cols : i * cols + cells],
-                    preferred_element_type=F32,
-                ) * turned[3 * i + j].astype(F32)
-                total = product if total is None else total + product
-                line = grouped[3 * i + j] * tree_sum(lines[i : i + cells // cols])
-                plain = line if plain is None else plain + line
+        )
         for part in halves(total):
             spread += jnp.dot(
                 part, group_columns(channels, which * GN_GROUPS, 4 * GN_GROUPS, 1), preferred_element_type=F32
@@ -405,16 +434,16 @@
     alpha = plain * inverse - beta * mean
     per = channels // GN_GROUPS
     weights = terms(rows8(alpha / per, beta / per))
-    picked = jnp.dot(weights, group_columns(channels, 0, GN_GROUPS, 1), preferred_element_type=F32)
-    picked = picked[0:8] + (picked[8:16] + picked[16:24])
+    picked = joined(
+        jnp.dot(weights, group_columns(channels, 0, GN_GROUPS, 1), preferred_element_type=F32)
+    )
     found = jnp.dot(picked, matrix, precision=lax.Precision.HIGHEST, preferred_element_type=F32)
     found = terms(rows8(pltpu.roll(found, width // 2, 1)[0:1] + found[1:2]))
     means = []
     for which in range(2):
-        back = jnp.dot(
-            found, group_columns(channels, which * GN_GROUPS, width, 0), preferred_element_type=F32
+        back = joined(
+            jnp.dot(found, group_columns(channels, which * GN_GROUPS, width, 0), preferred_element_type=F32)
         )
-        back = back[0:8] + (back[8:16] + back[16:24])
         means.append((reduced[2 + which : 3 + which] - back[0:1]) / total)
     normed = (images[...].astype(F32) - stat_one[0:1]) * stat_one[1:2]
     out[...] = (stat_one[1:2] * (grad - means[0] - normed * means[1])).astype(BF16)
@@ -438,14 +467,14 @@
             out = jnp.where(row == place, jnp.broadcast_to(block[which : which + 1], out.shape), out)
         return out
 
-    scale, shift, activated = ordered(0), ordered(1), ordered(2)
-    for start, part in ((0, scale), (channels, shift)):
+    activated = split(ordered(2))
+    left = jnp.concatenate([activated[k] for k in (0, 0, 1, 0, 2, 1)], axis=0).astype(BF16)
+    for start, which in ((0, 0), (channels, 1)):
+        part = ordered(which)
+        pieces = split(part)
+        right = jnp.concatenate([pieces[k] for k in (0, 1, 0, 2, 0, 1)], axis=0).astype(BF16)
         weight[:, start : start + channels] = lax.dot_general(
-            activated,
-            part,
-            (((0,), (0,)), ((), ())),
-            precision=lax.Precision.HIGHEST,
-            preferred_element_type=F32,
+            left, right, (((0,), (0,)), ((), ())), preferred_element_type=F32
         )
         bias[:, start : start + channels] = jnp.sum(part, axis=0, keepdims=True)
 
@@ -525,43 +554,41 @@
             jnp.pad(part, ((0, 0), (0, spare))) for part in (time_weight, time_bias, class_table)
         )
         mix = jnp.pad(mix, ((0, spare), (0, 0)))
+    pin = lambda part: pltpu.with_memory_space_constraint(part, pltpu.HBM)
+    like = lambda parts: tuple(shape(part.shape, part.dtype) for part in parts)
     loads = (
         images.reshape(cells, channels),
         cotangent.reshape(cells, channels),
-        time_weight,
-        mix,
-        class_table,
-        time_bias,
         norm_gain[None],
         norm_bias[None],
-        adaptive_bias[None],
-        conv_first.reshape(9, channels, channels),
-        conv_second.reshape(9, channels, channels),
-    )
-    spaces = {k: pl.ANY for k in range(len(loads))}
-    *held, one, two, three = call(
+    )
+    flat, flat_cot, gain, bias, one, two, three = call(
         functools.partial(first_kernel, dims),
-        (*(shape(part.shape, part.dtype) for part in loads), halos, small, halos),
-        tuple(pltpu.with_memory_space_constraint(part, pltpu.HBM) for part in loads),
+        (*like(loads), halos, small, halos),
+        tuple(pin(part) for part in loads),
         (pltpu.SemaphoreType.DMA((len(loads),)),),
         name="first",
-        spaces=spaces,
-    )
-    flat, flat_cot, time_weight, mix, class_table, time_bias, gain, bias, adaptive_bias, weights_first, weights_second = held
+        spaces={k: pl.ANY for k in range(len(loads))},
+    )
     image_one, image_three, stats = exchange(one, two, three)
-    turned, grouped = call(
-        turn_kernel,
-        (shape((9, channels, channels), BF16), shape((9, GN_GROUPS, channels), F32)),
-        (weights_first,),
+    taps = conv_first.reshape(9, channels, channels)
+    weights_second = conv_second.reshape(9, channels, channels)
+    loads = (time_weight, mix, class_table, time_bias, adaptive_bias[None])
+    weights_first, time_weight, mix, class_table, time_bias, adaptive_bias, turned, grouped = call(
+        functools.partial(turn_kernel, len(loads)),
+        (*like((taps, *loads)), shape(taps.shape, BF16), shape((9, GN_GROUPS, channels), F32)),
+        tuple(pin(part) for part in (taps, *loads)),
+        (pltpu.SemaphoreType.DMA((len(loads) + 1,)),),
         flops=conv_flops,
         name="turn",
-    )
+        spaces={k: pl.ANY for k in range(len(loads) + 1)},
+    )
+    instant = jnp.broadcast_to(jnp.concatenate([timesteps[:1], class_ids[:1]])[:, None], (2, 128))
     embed = call(
         embed_kernel,
         block,
-        (timesteps, class_ids, class_table, time_weight, time_bias, mix),
+        (instant, class_table, time_weight, time_bias, mix),
         name="embed",
-        spaces={0: pltpu.SMEM, 1: pltpu.SMEM},
     )
 
     hidden, stat_one, one, two, three = call(
@@ -585,7 +612,11 @@
         functools.partial(cross_kernel, dims),
         (wide, wide, shape((GN_GROUPS, 8 * GN_GROUPS), BF16)),
         (flat, image_one, image_three, stat_one, gain, bias, hidden, turned, grouped),
-        (pltpu.VMEM((2, 3, cells + 2 * cols, channels), BF16),),
+        (
+            pltpu.VMEM((2, cells + 2 * cols, channels), BF16),
+            pltpu.VMEM((3 * channels + 16, cells), BF16),
+            pltpu.VMEM((2, 3, 3 * channels + 16, channels), F32),
+        ),
         conv_flops,
         name="cross",
     )

time: 38.1 us -> 35.9 us (0.942)
  waiting for transfers between devices: 7.5 us -> 6.25 us
  Pallas kernels: 12.5 us -> 11.4 us
    ppermute x12, waiting for transfers between devices: 7.5 us -> 6.25 us  [swap(): return lax.ppermute(values, axis, [(i, i ^ distance) for i in range(size)])]
    pallas_call x11, Pallas kernels: 12.5 us -> 11.4 us  [call(): pl.pallas_call(kernel, out_shape=out_shapes, in_specs=[pl.BlockSpec(memor...]
  transfers between devices with their start and end apart: 12 -> 12, of which waited for: 4 -> 4; matrix products, arithmetic and copies ran while one was open for 0% -> 0% of each run, Pallas kernels for 19% -> 21%
where the time goes in v5:
time: 35.9 us; the launch traced here: 35.7 us
  starting transfers between devices  15.9 us (44%)
  Pallas kernels  11.4 us (32%)
  waiting for transfers between devices  6.25 us (17%)
  between operations  1.99 us (6%)
    ppermute x12, starting transfers between devices, swap(): return lax.ppermute(values, axis, [(i, i ^ distance) for i in range(size)])  15.9 us
    pallas_call x11, Pallas kernels, call(): pl.pallas_call(kernel, out_shape=out_shapes, in_specs=[pl.BlockSpec(memor...  11.4 us
    ppermute x12, waiting for transfers between devices, swap(): return lax.ppermute(values, axis, [(i, i ^ distance) for i in range(size)])  6.25 us
  transfers between devices with their start and end apart: 12, of which 4 were waited for; matrix products, arithmetic and copies ran while one was open for 0% of the time, Pallas kernels for 21%

profile of v5, /device:TPU:0, one launch (start us, length us, event | category | flops | bytes accessed | tf_op | source)
XLA Modules:
  0.0 35.7 jit_solution(6676906515713178842)
XLA Ops:
  0.6 1.3 %first.1 = (bf16[256,256]{1,0:T(8,128)(2,1)S(1)}, bf16[256,256]{1,0:T(8,128)(2,1)S(1)}, f32[1,256]{1,0:T(1,128)S(1)}, f32[1,256]{1,0:T(1,128)S(1)}, bf16[208,256...) custom-call(bf16[256,256]{1,0:T(8,128)(2,1)} %bitcast.15, bf16[256,256]{1,0:T(8,128)(2,1)} %bitcast.16, ...), custom_call_target="tpu_custom_call" | custom-call | flops 1000 | bytes 264192 | tf_op jit(solution)/shard_map/first/pallas_call | solution.py:484
  1.9 3.1 %collective-permute-start = (bf16[208,256]{1,0:T(8,128)(2,1)S(1)}, bf16[208,256]{1,0:T(8,128)(2,1)S(1)}, u32[]{:S(2)}, u32[]{:S(2)}) collective-permute-start(bf16[208,256]{1,0:T(8,128)(2,1)S(1)} %get-tuple-element.36), channel_id=1, source_target_pairs={{0,4},{4,0},{8,12},{12,8},{1,5},{5,1},{9,13},{13,9},{2,6},{6,2},{1... | collective-permute-start | bytes 319496 | tf_op jit(solution)/shard_map/ppermute | solution.py:499
  5.0 2.5 %collective-permute-start.1 = (bf16[208,256]{1,0:T(8,128)(2,1)S(1)}, bf16[208,256]{1,0:T(8,128)(2,1)S(1)}, u32[]{:S(2)}, u32[]{:S(2)}) collective-permute-start(bf16[208,256]{1,0:T(8,128)(2,1)S(1)} %get-tuple-element.37), channel_id=1, source_target_pairs={{0,12},{4,8},{8,4},{12,0},{1,13},{5,9},{9,5},{13,1},{2,14},{6,10},... | collective-permute-start | bytes 319496 | tf_op jit(solution)/shard_map/ppermute | solution.py:499
  7.5 0.1 collective-permute-start.2
  8.9 0.1 pad_add_fusion
  9.0 1.9 %turn.1 = (bf16[9,256,256]{2,1,0:T(8,128)(2,1)S(1)}, bf16[256,256]{1,0:T(8,128)(2,1)S(1)}, bf16[256,512]{1,0:T(8,128)(2,1)S(1)}, bf16[1000,256]{1,0:T(8,128)(2,1...) custom-call(bf16[9,256,256]{2,1,0:T(8,128)(2,1)} %bitcast.13, ...), custom_call_target="tpu_custom_call" | custom-call | flops 301989888 | bytes 2087936 | tf_op jit(solution)/shard_map/turn/pallas_call | solution.py:484
  10.9 0.1 broadcast_in_dim.22.instant
  11.0 0.4 %embed.1 = f32[8,256]{1,0:T(8,128)S(1)} custom-call(s32[2,128]{1,0:T(2,128)S(1)} %broadcast_in_dim.22.instant, bf16[1000,256]{1,0:T(8,128)(2,1)S(1)} %get-tuple-element.41.table, bf16[256,256]{1,0:T(8,128)(2,1)S(1)} %get-tuple-element.42.time_weight, f32[1,256]{1,0:T(1,128)S(1)} %get-tuple-element.43.time_bias, ...), custom_call_target="tpu_custom_call" | custom-call | flops 1000 | bytes 907264 | tf_op jit(solution)/shard_map/embed/pallas_call | solution.py:484
  11.3 1.6 %collective-permute-done.2.rest_2_ = bf16[16,256]{1,0:T(8,128)(2,1)S(1)} collective-permute-done((bf16[16,256]{1,0:T(8,128)(2,1)S(1)}, bf16[16,256]{1,0:T(8,128)(2,1)S(1)}, u32[]{:S(2)}, u32[]{:S(2)}) %collective-permute-start.2) | collective-permute-done | bytes 8224 | tf_op jit(solution)/shard_map/ppermute | solution.py:499
  12.9 0.0 collective-permute-done.one.rest_1_
  12.9 0.0 collective-permute-done.1.three.rest_3_
  13.0 0.9 %second.1 = (bf16[256,256]{1,0:T(8,128)(2,1)S(1)}, f32[8,256]{1,0:T(8,128)S(1)}, bf16[80,256]{1,0:T(8,128)(2,1)S(1)}, bf16[16,256]{1,0:T(8,128)(2,1)S(1)}, bf16[80,256]{1,0:T(8,128)(2,1)S(1)}) custom-call(bf16[256,256]{1,0:T(8,128)(2,1)S(1)} %get-tuple-element.35.images, bf16[208,256]{1,0:T(8,128)(2,1)S(1)} %collective-permute-done.one.rest_1_, ...), custom_call_target="tpu_custom_call" | custom-call | flops 301989888 | bytes 1763328 | tf_op jit(solution)/shard_map/second/pallas_call | solution.py:484
  13.9 0.5 %collective-permute-start.3 = (bf16[80,256]{1,0:T(8,128)(2,1)S(1)}, bf16[80,256]{1,0:T(8,128)(2,1)S(1)}, u32[]{:S(2)}, u32[]{:S(2)}) collective-permute-start(bf16[80,256]{1,0:T(8,128)(2,1)S(1)} %get-tuple-element.47), channel_id=1, source_target_pairs={{0,4},{4,0},{8,12},{12,8},{1,5},{5,1},{9,13},{13,9},{2,6},{6,2},{1... | collective-permute-start | bytes 122888 | tf_op jit(solution)/shard_map/ppermute | solution.py:499
  14.4 2.6 %collective-permute-start.4 = (bf16[80,256]{1,0:T(8,128)(2,1)S(1)}, bf16[80,256]{1,0:T(8,128)(2,1)S(1)}, u32[]{:S(2)}, u32[]{:S(2)}) collective-permute-start(bf16[80,256]{1,0:T(8,128)(2,1)S(1)} %get-tuple-element.48), channel_id=1, source_target_pairs={{0,12},{4,8},{8,4},{12,0},{1,13},{5,9},{9,5},{13,1},{2,14},{6,10},... | collective-permute-start | bytes 122888 | tf_op jit(solution)/shard_map/ppermute | solution.py:499
  17.0 0.4 %collective-permute-start.5 = (bf16[16,256]{1,0:T(8,128)(2,1)S(1)}, bf16[16,256]{1,0:T(8,128)(2,1)S(1)}, u32[]{:S(2)}, u32[]{:S(2)}) collective-permute-start(bf16[16,256]{1,0:T(8,128)(2,1)S(1)} %get-tuple-element.57.rest_0_), channel_id=1, source_target_pairs={{0,8},{4,12},{8,0},{12,4},{1,9},{5,13},{9,1},{13,5},{2,10},{6,14},... | collective-permute-start | bytes 24584 | tf_op jit(solution)/shard_map/ppermute | solution.py:499
  17.4 0.7 %grad.1.grad_active = f32[384,256]{1,0:T(8,128)S(1)} custom-call(bf16[256,256]{1,0:T(8,128)(2,1)S(1)} %get-tuple-element.49.cotangent, bf16[208,256]{1,0:T(8,128)(2,1)S(1)} %collective-permute-done.one.rest_1_, bf16[208,256]{1,0:T(8,128)(2,1)S(1)} %collective-permute-done.1.three.rest_3_, bf16[9,256,256]{2,1,0:T(8,128)(2,1)S(1)} %bitcast.11), custom_call_target="tpu_custom_call" | custom-call | flops 301989888 | bytes 1523712 | tf_op jit(solution)/shard_map/grad/pallas_call | solution.py:484
  18.1 1.7 %cross.1 = (f32[256,256]{1,0:T(8,128)S(1)}, f32[256,256]{1,0:T(8,128)S(1)}, bf16[32,256]{1,0:T(8,128)(2,1)S(1)}) custom-call(bf16[256,256]{1,0:T(8,128)(2,1)S(1)} %get-tuple-element.35.images, bf16[208,256]{1,0:T(8,128)(2,1)S(1)} %collective-permute-done.one.rest_1_, bf16[208,256]{1,0:T(8,128)(2,1)S(1)} %collective-permute-done.1.three.rest_3_, ...), custom_call_target="tpu_custom_call" | custom-call | flops 301989888 | bytes 1959936 | tf_op jit(solution)/shard_map/cross/pallas_call | solution.py:484
  19.8 1.8 %collective-permute-done.5.rest_2_ = bf16[16,256]{1,0:T(8,128)(2,1)S(1)} collective-permute-done((bf16[16,256]{1,0:T(8,128)(2,1)S(1)}, bf16[16,256]{1,0:T(8,128)(2,1)S(1)}, u32[]{:S(2)}, u32[]{:S(2)}) %collective-permute-start.5) | collective-permute-done | bytes 8224 | tf_op jit(solution)/shard_map/ppermute | solution.py:499
  21.6 0.0 collective-permute-done.3.one.rest_1_
  21.6 0.0 collective-permute-done.4.three.rest_3_
  21.6 0.7 %third.1 = (bf16[384,256]{1,0:T(8,128)(2,1)S(1)}, f32[384,256]{1,0:T(8,128)S(1)}, f32[8,256]{1,0:T(8,128)S(1)}, bf16[48,256]{1,0:T(8,128)(2,1)S(1)}) custom-call(bf16[256,256]{1,0:T(8,128)(2,1)S(1)} %get-tuple-element.46.hidden, bf16[80,256]{1,0:T(8,128)(2,1)S(1)} %collective-permute-done.3.one.rest_1_, ...), custom_call_target="tpu_custom_call" | custom-call | flops 301989888 | bytes 2426880 | tf_op jit(solution)/shard_map/third/pallas_call | solution.py:484
  22.3 0.7 %collective-permute-start.6 = (bf16[48,256]{1,0:T(8,128)(2,1)S(1)}, bf16[48,256]{1,0:T(8,128)(2,1)S(1)}, u32[]{:S(2)}, u32[]{:S(2)}) collective-permute-start(bf16[48,256]{1,0:T(8,128)(2,1)S(1)} %get-tuple-element.63.rest_0_), channel_id=1, source_target_pairs={{0,4},{4,0},{8,12},{12,8},{1,5},{5,1},{9,13},{13,9},{2,6},{6,2},{1... | collective-permute-start | bytes 73736 | tf_op jit(solution)/shard_map/ppermute | solution.py:499
  23.0 1.3 %collective-permute-start.7 = (bf16[48,256]{1,0:T(8,128)(2,1)S(1)}, bf16[48,256]{1,0:T(8,128)(2,1)S(1)}, u32[]{:S(2)}, u32[]{:S(2)}) collective-permute-start(bf16[48,256]{1,0:T(8,128)(2,1)S(1)} %get-tuple-element.63.rest_0_), channel_id=1, source_target_pairs={{0,8},{4,12},{8,0},{12,4},{1,9},{5,13},{9,1},{13,5},{2,10},{6,14},... | collective-permute-start | bytes 73736 | tf_op jit(solution)/shard_map/ppermute | solution.py:499
  24.3 2.4 %collective-permute-start.8 = (bf16[48,256]{1,0:T(8,128)(2,1)S(1)}, bf16[48,256]{1,0:T(8,128)(2,1)S(1)}, u32[]{:S(2)}, u32[]{:S(2)}) collective-permute-start(bf16[48,256]{1,0:T(8,128)(2,1)S(1)} %get-tuple-element.63.rest_0_), channel_id=1, source_target_pairs={{0,12},{4,8},{8,4},{12,0},{1,13},{5,9},{9,5},{13,1},{2,14},{6,10},... | collective-permute-start | bytes 73736 | tf_op jit(solution)/shard_map/ppermute | solution.py:499
  26.7 1.1 %branch.1 = (bf16[256,256]{1,0:T(8,128)(2,1)}, f32[8,128]{1,0:T(8,128)S(1)}) custom-call(bf16[384,256]{1,0:T(8,128)(2,1)S(1)} %get-tuple-element.58.active, bf16[9,256,256]{2,1,0:T(8,128)(2,1)S(1)} %bitcast.12), custom_call_target="tpu_custom_call" | custom-call | flops 301989888 | bytes 1376256 | tf_op jit(solution)/shard_map/branch/pallas_call | solution.py:484
  27.9 2.1 %collective-permute-done.8.rest_3_ = bf16[48,256]{1,0:T(8,128)(2,1)S(1)} collective-permute-done((bf16[48,256]{1,0:T(8,128)(2,1)S(1)}, bf16[48,256]{1,0:T(8,128)(2,1)S(1)}, u32[]{:S(2)}, u32[]{:S(2)}) %collective-permute-start.8) | collective-permute-done | bytes 24608 | tf_op jit(solution)/shard_map/ppermute | solution.py:499
  30.0 1.6 %collective-permute-start.10 = (f32[8,256]{1,0:T(8,128)S(1)}, f32[8,256]{1,0:T(8,128)S(1)}, u32[]{:S(2)}, u32[]{:S(2)}) collective-permute-start(f32[8,256]{1,0:T(8,128)S(1)} %pairs.1.rest_0_), channel_id=1, source_target_pairs={{0,2},{1,3},{2,0},{3,1},{4,6},{5,7},{6,4},{7,5},{8,10},{9,11},{10,... | collective-permute-start | bytes 24584 | tf_op jit(solution)/shard_map/ppermute | solution.py:499
  31.5 0.0 collective-permute-start.11
  31.6 0.6 %collective-permute-start.9 = (f32[8,256]{1,0:T(8,128)S(1)}, f32[8,256]{1,0:T(8,128)S(1)}, u32[]{:S(2)}, u32[]{:S(2)}) collective-permute-start(f32[8,256]{1,0:T(8,128)S(1)} %pairs.1.rest_0_), channel_id=1, source_target_pairs={{0,1},{1,0},{2,3},{3,2},{4,5},{5,4},{6,7},{7,6},{8,9},{9,8},{10,11... | collective-permute-start | bytes 24584 | tf_op jit(solution)/shard_map/ppermute | solution.py:499
  32.2 1.7 %fourth.1 = bf16[256,256]{1,0:T(8,128)(2,1)} custom-call(f32[8,128]{1,0:T(8,128)S(1)} %get-tuple-element.60.token, f32[384,256]{1,0:T(8,128)S(1)} %get-tuple-element.61.grad_norm, bf16[256,256]{1,0:T(8,128)(2,1)S(1)} %get-tuple-element.46.hidden, bf16[80,256]{1,0:T(8,128)(2,1)S(1)} %collective-permute-done.3.one.rest_1_, ...), custom_call_target="tpu_custom_call" | custom-call | flops 301989888 | bytes 2297856 | tf_op jit(solution)/shard_map/fourth/pallas_call | solution.py:484
  33.9 0.8 %collective-permute-done.11.rest_3_ = f32[8,256]{1,0:T(8,128)S(1)} collective-permute-done((f32[8,256]{1,0:T(8,128)S(1)}, f32[8,256]{1,0:T(8,128)S(1)}, u32[]{:S(2)}, u32[]{:S(2)}) %collective-permute-start.11) | collective-permute-done | bytes 8224 | tf_op jit(solution)/shard_map/ppermute | solution.py:499
  34.6 1.0 %weight.1 = (f32[256,512]{1,0:T(8,128)}, f32[1,512]{1,0:T(1,128)}) custom-call(f32[8,256]{1,0:T(8,128)S(1)} %pairs.1.rest_0_, f32[8,256]{1,0:T(8,128)S(1)} %collective-permute-done.9.rest_1_, f32[8,256]{1,0:T(8,128)S(1)} %collective-permute-done.10.rest_2_, f32[8,256]{1,0:T(8,128)S(1)} %collective-permute-done.11.rest_3_), custom_call_target="tpu_custom_call" | custom-call | flops 1000 | bytes 32768 | tf_op jit(solution)/shard_map/weight/pallas_call | solution.py:484
  (7 shorter events, 0.0 us)
Async XLA Ops:
  1.9 11.0 %collective-permute-start = (bf16[208,256]{1,0:T(8,128)(2,1)S(1)}, bf16[208,256]{1,0:T(8,128)(2,1)S(1)}, u32[]{:S(2)}, u32[]{:S(2)}) collective-permute-start(bf16[208,256]{1,0:T(8,128)(2,1)S(1)} %get-tuple-element.36), channel_id=1, source_target_pairs={{0,4},{4,0},{8,12},{12,8},{1,5},{5,1},{9,13},{13,9},{2,6},{6,2},{1... | collective-permute-start | bytes 319496 | tf_op jit(solution)/shard_map/ppermute | solution.py:499
  5.0 7.9 %collective-permute-start.1 = (bf16[208,256]{1,0:T(8,128)(2,1)S(1)}, bf16[208,256]{1,0:T(8,128)(2,1)S(1)}, u32[]{:S(2)}, u32[]{:S(2)}) collective-permute-start(bf16[208,256]{1,0:T(8,128)(2,1)S(1)} %get-tuple-element.37), channel_id=1, source_target_pairs={{0,12},{4,8},{8,4},{12,0},{1,13},{5,9},{9,5},{13,1},{2,14},{6,10},... | collective-permute-start | bytes 319496 | tf_op jit(solution)/shard_map/ppermute | solution.py:499
  7.5 5.4 %collective-permute-start.2 = (bf16[16,256]{1,0:T(8,128)(2,1)S(1)}, bf16[16,256]{1,0:T(8,128)(2,1)S(1)}, u32[]{:S(2)}, u32[]{:S(2)}) collective-permute-start(bf16[16,256]{1,0:T(8,128)(2,1)S(1)} %get-tuple-element.45.rest_0_), channel_id=1, source_target_pairs={{0,8},{4,12},{8,0},{12,4},{1,9},{5,13},{9,1},{13,5},{2,10},{6,14},... | collective-permute-start | bytes 24584 | tf_op jit(solution)/shard_map/ppermute | solution.py:499
  11.0 6.5 %copy-start = (bf16[3,3,256,256]{3,2,1,0:T(8,128)(2,1)S(1)}, bf16[3,3,256,256]{3,2,1,0:T(8,128)(2,1)}, u32[]{:S(2)}) copy-start(bf16[3,3,256,256]{3,2,1,0:T(8,128)(2,1)} %param.20) | copy-start | bytes 3538948
  13.9 7.7 %collective-permute-start.3 = (bf16[80,256]{1,0:T(8,128)(2,1)S(1)}, bf16[80,256]{1,0:T(8,128)(2,1)S(1)}, u32[]{:S(2)}, u32[]{:S(2)}) collective-permute-start(bf16[80,256]{1,0:T(8,128)(2,1)S(1)} %get-tuple-element.47), channel_id=1, source_target_pairs={{0,4},{4,0},{8,12},{12,8},{1,5},{5,1},{9,13},{13,9},{2,6},{6,2},{1... | collective-permute-start | bytes 122888 | tf_op jit(solution)/shard_map/ppermute | solution.py:499
  14.4 7.2 %collective-permute-start.4 = (bf16[80,256]{1,0:T(8,128)(2,1)S(1)}, bf16[80,256]{1,0:T(8,128)(2,1)S(1)}, u32[]{:S(2)}, u32[]{:S(2)}) collective-permute-start(bf16[80,256]{1,0:T(8,128)(2,1)S(1)} %get-tuple-element.48), channel_id=1, source_target_pairs={{0,12},{4,8},{8,4},{12,0},{1,13},{5,9},{9,5},{13,1},{2,14},{6,10},... | collective-permute-start | bytes 122888 | tf_op jit(solution)/shard_map/ppermute | solution.py:499
  17.0 4.5 %collective-permute-start.5 = (bf16[16,256]{1,0:T(8,128)(2,1)S(1)}, bf16[16,256]{1,0:T(8,128)(2,1)S(1)}, u32[]{:S(2)}, u32[]{:S(2)}) collective-permute-start(bf16[16,256]{1,0:T(8,128)(2,1)S(1)} %get-tuple-element.57.rest_0_), channel_id=1, source_target_pairs={{0,8},{4,12},{8,0},{12,4},{1,9},{5,13},{9,1},{13,5},{2,10},{6,14},... | collective-permute-start | bytes 24584 | tf_op jit(solution)/shard_map/ppermute | solution.py:499
  22.3 5.6 %collective-permute-start.6 = (bf16[48,256]{1,0:T(8,128)(2,1)S(1)}, bf16[48,256]{1,0:T(8,128)(2,1)S(1)}, u32[]{:S(2)}, u32[]{:S(2)}) collective-permute-start(bf16[48,256]{1,0:T(8,128)(2,1)S(1)} %get-tuple-element.63.rest_0_), channel_id=1, source_target_pairs={{0,4},{4,0},{8,12},{12,8},{1,5},{5,1},{9,13},{13,9},{2,6},{6,2},{1... | collective-permute-start | bytes 73736 | tf_op jit(solution)/shard_map/ppermute | solution.py:499
  23.0 4.9 %collective-permute-start.7 = (bf16[48,256]{1,0:T(8,128)(2,1)S(1)}, bf16[48,256]{1,0:T(8,128)(2,1)S(1)}, u32[]{:S(2)}, u32[]{:S(2)}) collective-permute-start(bf16[48,256]{1,0:T(8,128)(2,1)S(1)} %get-tuple-element.63.rest_0_), channel_id=1, source_target_pairs={{0,8},{4,12},{8,0},{12,4},{1,9},{5,13},{9,1},{13,5},{2,10},{6,14},... | collective-permute-start | bytes 73736 | tf_op jit(solution)/shard_map/ppermute | solution.py:499
  24.3 5.6 %collective-permute-start.8 = (bf16[48,256]{1,0:T(8,128)(2,1)S(1)}, bf16[48,256]{1,0:T(8,128)(2,1)S(1)}, u32[]{:S(2)}, u32[]{:S(2)}) collective-permute-start(bf16[48,256]{1,0:T(8,128)(2,1)S(1)} %get-tuple-element.63.rest_0_), channel_id=1, source_target_pairs={{0,12},{4,8},{8,4},{12,0},{1,13},{5,9},{9,5},{13,1},{2,14},{6,10},... | collective-permute-start | bytes 73736 | tf_op jit(solution)/shard_map/ppermute | solution.py:499
  30.0 3.9 %collective-permute-start.10 = (f32[8,256]{1,0:T(8,128)S(1)}, f32[8,256]{1,0:T(8,128)S(1)}, u32[]{:S(2)}, u32[]{:S(2)}) collective-permute-start(f32[8,256]{1,0:T(8,128)S(1)} %pairs.1.rest_0_), channel_id=1, source_target_pairs={{0,2},{1,3},{2,0},{3,1},{4,6},{5,7},{6,4},{7,5},{8,10},{9,11},{10,... | collective-permute-start | bytes 24584 | tf_op jit(solution)/shard_map/ppermute | solution.py:499
  31.5 3.1 %collective-permute-start.11 = (f32[8,256]{1,0:T(8,128)S(1)}, f32[8,256]{1,0:T(8,128)S(1)}, u32[]{:S(2)}, u32[]{:S(2)}) collective-permute-start(f32[8,256]{1,0:T(8,128)S(1)} %pairs.1.rest_0_), channel_id=1, source_target_pairs={{0,3},{1,2},{2,1},{3,0},{4,7},{5,6},{6,5},{7,4},{8,11},{9,10},{10,... | collective-permute-start | bytes 24584 | tf_op jit(solution)/shard_map/ppermute | solution.py:499
  31.6 3.1 %collective-permute-start.9 = (f32[8,256]{1,0:T(8,128)S(1)}, f32[8,256]{1,0:T(8,128)S(1)}, u32[]{:S(2)}, u32[]{:S(2)}) collective-permute-start(f32[8,256]{1,0:T(8,128)S(1)} %pairs.1.rest_0_), channel_id=1, source_target_pairs={{0,1},{1,0},{2,3},{3,2},{4,5},{5,4},{6,7},{7,6},{8,9},{9,8},{10,11... | collective-permute-start | bytes 24584 | tf_op jit(solution)/shard_map/ppermute | solution.py:499

commit v6 on v5

--- a/solution.py
+++ b/solution.py
@@ -160,14 +160,12 @@
     one[0:cols] = images[pl.ds(start_one, cols)]
     three[0:cols] = images[pl.ds(start_three, cols)]
     copies[1].wait()
-    odd = place[1]
-    near, far = (1 - odd) * (cells - 2 * cols), odd * (cells - 2 * cols)
-    one[cols : 3 * cols] = cotangent[pl.ds(pl.multiple_of(near, cols), 2 * cols)]
-    three[cols : 3 * cols] = cotangent[pl.ds(pl.multiple_of(far, cols), 2 * cols)]
+    one[cols : 2 * cols] = cotangent[pl.ds(start_one, cols)]
+    three[cols : 2 * cols] = cotangent[pl.ds(start_three, cols)]
     block = terms(rows8(mean, spread))
-    one[3 * cols :] = block
+    one[2 * cols :] = block
     two[...] = block
-    three[3 * cols :] = block
+    three[2 * cols :] = block
     for copy in copies[2:]:
         copy.wait()
 
@@ -198,7 +196,7 @@
     stat_refs, (hidden, stat, out_one, out_two, out_three, padded) = rest[:n_stats], rest[n_stats:]
     count = cells * (channels // GN_GROUPS)
     mean, inverse = joint_moments(
-        stat_list(stat_refs, (0, 3 * cols, 0, 3 * cols), tiles), count
+        stat_list(stat_refs, (0, 2 * cols, 0, 2 * cols), tiles), count
     )
     stat[...] = rows8(mean, inverse)
     above, below = edges(place, one[0:cols], three[0:cols])
@@ -262,11 +260,11 @@
 def grad_kernel(dims, cotangent, one, three, weights, out, padded):
     cells, cols, channels, tiles = dims
     place = standing(tiles)
-    above, below = edges(place, one[cols : 3 * cols], three[cols : 3 * cols])
-    padded[0 : 2 * cols] = jnp.where(place[0] > 0, above, jnp.zeros_like(above))
-    padded[2 * cols : 2 * cols + cells] = cotangent[...]
-    padded[2 * cols + cells :] = jnp.where(place[0] < tiles - 1, below, jnp.zeros_like(below))
-    out[...] = conv(padded, weights, cells + 2 * cols, cols, True)
+    above, below = edges(place, one[cols : 2 * cols], three[cols : 2 * cols])
+    padded[0:cols] = jnp.where(place[0] > 0, above, jnp.zeros_like(above))
+    padded[cols : cols + cells] = cotangent[...]
+    padded[cols + cells :] = jnp.where(place[0] < tiles - 1, below, jnp.zeros_like(below))
+    out[...] = conv(padded, weights, cells, cols, True)
 
 
 def halves(values):
@@ -275,7 +273,7 @@
 
 
 def cross_kernel(
-    dims, images, one, three, stat_one, gain, bias, hidden, turned, grouped, slope, moved, matrix, factors, left, products
+    dims, images, one, three, stat_one, gain, bias, hidden, turned, grouped, slope, factors, matrix, left, products
 ):
     cells, cols, channels, tiles = dims
     place = standing(tiles)
@@ -289,7 +287,7 @@
         return grade, grade * normed
 
     own = pieces(images[...])
-    slope[...], moved[...] = own
+    slope[...] = own[0]
     for which, (top, bottom) in enumerate(zip(pieces(above), pieces(below), strict=True)):
         factors[which, 0:cols] = jnp.where(place[0] > 0, top, 0.0).astype(BF16)
         factors[which, cols : cols + cells] = own[which].astype(BF16)
@@ -343,11 +341,11 @@
 
 
 def third_kernel(
-    dims, n_stats, hidden, one, three, grad_active, adaptive_bias, turned, slope, moved, matrix, *rest
+    dims, n_stats, hidden, one, three, grad_active, adaptive_bias, turned, factors, matrix, *rest
 ):
     cells, cols, channels, tiles = dims
     place = standing(tiles)
-    stat_refs, (active, grad_norm, stat, out, padded) = rest[:n_stats], rest[n_stats:]
+    stat_refs, (active, grad_norm, stat, out_one, out_two, out_three, padded) = rest[:n_stats], rest[n_stats:]
     count = cells * (channels // GN_GROUPS)
     stats = stat_list(stat_refs, (0, cols, 0, cols), tiles)
     mean, inverse = joint_moments(stats, count)
@@ -357,39 +355,44 @@
     stat[...] = rows8(mean, inverse, factor)
     above, below = edges(place, one[0:cols], three[0:cols])
 
-    def piece(block, start, inside):
-        stop = start + block.shape[0]
+    def pieces(block):
         normed = (block.astype(F32) - mean) * inverse
         pre = normed * factor + shift
-        gate = sigmoid(pre)
-        grad_pre = grad_active[start:stop] * (gate * (1.0 + pre * (1.0 - gate)))
-        grad = grad_pre * factor
-        grad_norm[start:stop] = grad
-        result, scaled = pre * gate, grad * inverse
-        if inside is not None:
-            result, scaled = jnp.where(inside, result, 0.0), jnp.where(inside, scaled, 0.0)
-        active[start:stop] = result.astype(BF16)
-        padded[start:stop] = scaled.astype(BF16)
-        return normed, grad_pre
-
-    piece(above, 0, place[0] > 0)
-    normed, grad_pre = piece(hidden[...], cols, None)
-    piece(below, cols + cells, place[0] < tiles - 1)
-    base = conv(padded, turned, cells, cols, True, True)
-    out[0:STAT_ROWS] = terms(
+        return normed, pre, sigmoid(pre)
+
+    normed, pre, gate = pieces(hidden[...])
+    active[cols : cols + cells] = (pre * gate).astype(BF16)
+    grad_pre = grad_active[...] * (gate * (1.0 + pre * (1.0 - gate)))
+    grad = grad_pre * factor
+    grad_norm[...] = grad
+    edge = jnp.zeros((2 * cols, channels), BF16)
+    padded[0 : 2 * cols] = edge
+    padded[2 * cols : 2 * cols + cells] = (grad * inverse).astype(BF16)
+    padded[2 * cols + cells :] = edge
+    base = conv(padded, turned, cells + 2 * cols, cols, True, True)
+    _, pre, gate = pieces(above)
+    active[0:cols] = jnp.where(place[0] > 0, pre * gate, 0.0).astype(BF16)
+    _, pre, gate = pieces(below)
+    active[cols + cells :] = jnp.where(place[0] < tiles - 1, pre * gate, 0.0).astype(BF16)
+    block = terms(
         rows8(
             jnp.sum(grad_pre * normed, axis=0, keepdims=True),
             jnp.sum(grad_pre, axis=0, keepdims=True),
-            jnp.sum(base * slope[...], axis=0, keepdims=True),
-            jnp.sum(base * moved[...], axis=0, keepdims=True),
+            jnp.sum(base * factors[0].astype(F32), axis=0, keepdims=True),
+            jnp.sum(base * factors[1].astype(F32), axis=0, keepdims=True),
         )
     )
-    out[STAT_ROWS:] = matrix[...]
+    start_one, start_three = starts(place, cells, cols)
+    out_one[0:cols] = grad_norm[pl.ds(start_one, cols)].astype(BF16)
+    out_three[0:cols] = grad_norm[pl.ds(start_three, cols)].astype(BF16)
+    for out, start in ((out_one, cols), (out_two, 0), (out_three, cols)):
+        out[start : start + STAT_ROWS] = block
+        out[start + STAT_ROWS :] = matrix[...]
 
 
 def pairs_kernel(dims, n_stats, embed, *rest):
     cells, cols, channels, tiles = dims
-    sums = tree_sum(stat_list(rest[:n_stats], (0, 0, 0, 0), tiles))
+    sums = tree_sum(stat_list(rest[:n_stats], (0, cols, 0, cols), tiles))
     rest[n_stats][...] = rows8(sums[0:1], sums[1:2], embed[2:3])
 
 
@@ -400,7 +403,7 @@
 
 
 def fourth_kernel(
-    dims, n_stats, token, grad_norm, hidden, one, three, stat_two, turned, images, stat_one, slope, *rest
+    dims, n_stats, token, grad_norm, grad_one, grad_three, hidden, one, three, stat_two, turned, images, stat_one, slope, *rest
 ):
     cells, cols, channels, tiles = dims
     place = standing(tiles)
@@ -410,24 +413,25 @@
         size = stat_refs[0].shape[0] // tiles
         blocks = [stat_refs[0][size * t + STAT_ROWS : size * (t + 1)] for t in range(tiles)]
     else:
-        blocks = [ref[STAT_ROWS:] for ref in stat_refs]
+        blocks = [ref[ref.shape[0] - GN_GROUPS :] for ref in stat_refs]
     width = 4 * GN_GROUPS
     matrix = tree_sum([b[:, :width].astype(F32) + b[:, width:].astype(F32) for b in blocks])
-    sums = tree_sum(stat_list(stat_refs, (0, 0, 0, 0), tiles))
+    sums = tree_sum(stat_list(stat_refs, (0, cols, 0, cols), tiles))
     mean, inverse, factor = stat_two[0:1], stat_two[1:2], stat_two[2:3]
     row = lax.broadcasted_iota(jnp.int32, (8, channels), 0)
     reduced = group_sums(jnp.where(row < 2, sums * factor, sums), group_matrix(channels))
     paired, plain = reduced[0:1] / total, reduced[1:2] / total
     above, below = edges(place, one[0:cols], three[0:cols])
+    grad_above, grad_below = edges(place, grad_one[0:cols], grad_three[0:cols])
 
     def grad_hidden(grad, block):
         normed = (block.astype(F32) - mean) * inverse
-        return inverse * (grad - plain - normed * paired)
-
-    padded[0:cols] = jnp.where(place[0] > 0, grad_hidden(grad_norm[0:cols], above), 0.0).astype(BF16)
-    padded[cols : cols + cells] = grad_hidden(grad_norm[cols : cols + cells], hidden[...]).astype(BF16)
+        return inverse * (grad.astype(F32) - plain - normed * paired)
+
+    padded[0:cols] = jnp.where(place[0] > 0, grad_hidden(grad_above, above), 0.0).astype(BF16)
+    padded[cols : cols + cells] = grad_hidden(grad_norm[...], hidden[...]).astype(BF16)
     padded[cols + cells :] = jnp.where(
-        place[0] < tiles - 1, grad_hidden(grad_norm[cols + cells :], below), 0.0
+        place[0] < tiles - 1, grad_hidden(grad_below, below), 0.0
     ).astype(BF16)
     grad = conv(padded, turned, cells, cols, True, True) * slope[...]
     beta = paired * inverse * inverse
@@ -508,13 +512,6 @@
     behind = [(target, source) for source, target in ahead]
     below, above = lax.ppermute(three, "tile", behind), lax.ppermute(one, "tile", ahead)
     return below, above, [lax.all_gather(two, "tile", axis=0, tiled=True)]
-
-
-def spread_small(block):
-    tiles = lax.axis_size("tile")
-    if tiles == 4:
-        return [block, *(swap(block, "tile", tiles, k) for k in (1, 2, 3))]
-    return [lax.all_gather(block, "tile", axis=0, tiled=True)]
 
 
 def body(
@@ -541,7 +538,7 @@
     padded = pltpu.VMEM((cells + 2 * cols, channels), BF16)
     small = shape((STAT_ROWS, channels), BF16)
     halo = shape((cols + STAT_ROWS, channels), BF16)
-    halos = shape((3 * cols + STAT_ROWS, channels), BF16)
+    halos = shape((2 * cols + STAT_ROWS, channels), BF16)
     block = shape((8, channels), F32)
     wide = shape((cells, channels), F32)
     narrow = shape((cells, channels), BF16)
@@ -602,41 +599,37 @@
     hidden_one, hidden_three, stats = exchange(one, two, three)
     grad_active = call(
         functools.partial(grad_kernel, dims),
-        shape((cells + 2 * cols, channels), F32),
+        wide,
         (flat_cot, image_one, image_three, weights_second),
-        (pltpu.VMEM((cells + 4 * cols, channels), BF16),),
+        (padded,),
         conv_flops,
         name="grad",
     )
-    slope, moved, matrix = call(
+    slope, factors, matrix = call(
         functools.partial(cross_kernel, dims),
-        (wide, wide, shape((GN_GROUPS, 8 * GN_GROUPS), BF16)),
+        (wide, shape((2, cells + 2 * cols, channels), BF16), shape((GN_GROUPS, 8 * GN_GROUPS), BF16)),
         (flat, image_one, image_three, stat_one, gain, bias, hidden, turned, grouped),
         (
-            pltpu.VMEM((2, cells + 2 * cols, channels), BF16),
             pltpu.VMEM((3 * channels + 16, cells), BF16),
             pltpu.VMEM((2, 3, 3 * channels + 16, channels), F32),
         ),
         conv_flops,
         name="cross",
     )
-    active, grad_norm, stat_two, message = call(
+    mail = shape((STAT_ROWS + GN_GROUPS, channels), BF16)
+    mail_halo = shape((cols + STAT_ROWS + GN_GROUPS, channels), BF16)
+    active, grad_norm, stat_two, one, two, three = call(
         functools.partial(third_kernel, dims, len(stats)),
-        (
-            shape((cells + 2 * cols, channels), BF16),
-            shape((cells + 2 * cols, channels), F32),
-            block,
-            shape((STAT_ROWS + GN_GROUPS, channels), BF16),
-        ),
-        (hidden, hidden_one, hidden_three, grad_active, adaptive_bias, turned, slope, moved, matrix, *stats),
-        (padded,),
+        (shape((cells + 2 * cols, channels), BF16), wide, block, mail_halo, mail, mail_halo),
+        (hidden, hidden_one, hidden_three, grad_active, adaptive_bias, turned, factors, matrix, *stats),
+        (pltpu.VMEM((cells + 4 * cols, channels), BF16),),
         conv_flops,
         name="third",
     )
-    stats = spread_small(message)
+    grad_one, grad_three, stats = exchange(one, two, three)
     branch, token = call(
         functools.partial(branch_kernel, dims),
-        (narrow, shape((8, 128), F32)),
+        (pltpu.VMEM((cells, channels), BF16), shape((8, 128), F32)),
         (active, weights_second),
         flops=conv_flops,
         name="branch",
@@ -650,8 +643,8 @@
         pair_list = [lax.all_gather(pairs, "image", axis=0, tiled=True)]
     input_grad = call(
         functools.partial(fourth_kernel, dims, len(stats)),
-        narrow,
-        (token, grad_norm, hidden, hidden_one, hidden_three, stat_two, turned, flat, stat_one, slope, *stats),
+        pltpu.VMEM((cells, channels), BF16),
+        (token, grad_norm, grad_one, grad_three, hidden, hidden_one, hidden_three, stat_two, turned, flat, stat_one, slope, *stats),
         (padded,),
         conv_flops,
         name="fourth",

time: 35.9 us -> 35 us (0.975)
  local copies, waits for them, and re-layouts: 0.07 us -> 1.39 us
  Pallas kernels: 11.4 us -> 10.1 us
  starting transfers between devices: 15.9 us -> 15.1 us
    unnamed x2 -> x4, local copies, waits for them, and re-layouts: 0.01 us -> 1.32 us
    pallas_call x11, Pallas kernels: 11.4 us -> 10.1 us  [call(): pl.pallas_call(kernel, out_shape=out_shapes, in_specs=[pl.BlockSpec(memor...]
    ppermute x12, starting transfers between devices: 15.9 us -> 15.1 us  [swap(): return lax.ppermute(values, axis, [(i, i ^ distance) for i in range(size)])]
  transfers between devices with their start and end apart: 12 -> 12, of which waited for: 4 -> 4; matrix products, arithmetic and copies ran while one was open for 0% -> 4% of each run, Pallas kernels for 21% -> 17%
where the time goes in v6:
time: 35 us; the launch traced here: 34.8 us
  starting transfers between devices  15.1 us (43%)
  Pallas kernels  10.1 us (29%)
  waiting for transfers between devices  6.16 us (18%)
  between operations  2 us (6%)
  local copies, waits for them, and re-layouts  1.39 us (4%)
    ppermute x12, starting transfers between devices, swap(): return lax.ppermute(values, axis, [(i, i ^ distance) for i in range(size)])  15.1 us
    pallas_call x11, Pallas kernels, call(): pl.pallas_call(kernel, out_shape=out_shapes, in_specs=[pl.BlockSpec(memor...  10.1 us
    ppermute x12, waiting for transfers between devices, swap(): return lax.ppermute(values, axis, [(i, i ^ distance) for i in range(size)])  6.16 us
    unnamed x4, local copies, waits for them, and re-layouts  1.32 us
  transfers between devices with their start and end apart: 12, of which 4 were waited for; matrix products, arithmetic and copies ran while one was open for 4% of the time, Pallas kernels for 17%

profile of v6, /device:TPU:0, one launch (start us, length us, event | category | flops | bytes accessed | tf_op | source)
XLA Modules:
  0.0 34.8 jit_solution(15290910655138791717)
XLA Ops:
  0.6 1.3 %first.1 = (bf16[256,256]{1,0:T(8,128)(2,1)S(1)}, bf16[256,256]{1,0:T(8,128)(2,1)S(1)}, f32[1,256]{1,0:T(1,128)S(1)}, f32[1,256]{1,0:T(1,128)S(1)}, bf16[144,256...) custom-call(bf16[256,256]{1,0:T(8,128)(2,1)} %bitcast.16, bf16[256,256]{1,0:T(8,128)(2,1)} %bitcast.17, ...), custom_call_target="tpu_custom_call" | custom-call | flops 1000 | bytes 264192 | tf_op jit(solution)/shard_map/first/pallas_call | solution.py:488
  1.9 3.1 %collective-permute-start = (bf16[144,256]{1,0:T(8,128)(2,1)S(1)}, bf16[144,256]{1,0:T(8,128)(2,1)S(1)}, u32[]{:S(2)}, u32[]{:S(2)}) collective-permute-start(bf16[144,256]{1,0:T(8,128)(2,1)S(1)} %get-tuple-element.38), channel_id=1, source_target_pairs={{0,4},{4,0},{8,12},{12,8},{1,5},{5,1},{9,13},{13,9},{2,6},{6,2},{1... | collective-permute-start | bytes 221192 | tf_op jit(solution)/shard_map/ppermute | solution.py:503
  5.0 2.5 %collective-permute-start.1 = (bf16[144,256]{1,0:T(8,128)(2,1)S(1)}, bf16[144,256]{1,0:T(8,128)(2,1)S(1)}, u32[]{:S(2)}, u32[]{:S(2)}) collective-permute-start(bf16[144,256]{1,0:T(8,128)(2,1)S(1)} %get-tuple-element.39), channel_id=1, source_target_pairs={{0,12},{4,8},{8,4},{12,0},{1,13},{5,9},{9,5},{13,1},{2,14},{6,10},... | collective-permute-start | bytes 221192 | tf_op jit(solution)/shard_map/ppermute | solution.py:503
  7.5 0.1 collective-permute-start.2
  8.9 0.1 pad_add_fusion
  9.0 1.9 %turn.1 = (bf16[9,256,256]{2,1,0:T(8,128)(2,1)S(1)}, bf16[256,256]{1,0:T(8,128)(2,1)S(1)}, bf16[256,512]{1,0:T(8,128)(2,1)S(1)}, bf16[1000,256]{1,0:T(8,128)(2,1...) custom-call(bf16[9,256,256]{2,1,0:T(8,128)(2,1)} %bitcast.15, ...), custom_call_target="tpu_custom_call" | custom-call | flops 301989888 | bytes 2087936 | tf_op jit(solution)/shard_map/turn/pallas_call | solution.py:488
  10.9 0.1 broadcast_in_dim.22.instant
  11.0 0.4 %embed.1 = f32[8,256]{1,0:T(8,128)S(1)} custom-call(s32[2,128]{1,0:T(2,128)S(1)} %broadcast_in_dim.22.instant, bf16[1000,256]{1,0:T(8,128)(2,1)S(1)} %get-tuple-element.43.table, bf16[256,256]{1,0:T(8,128)(2,1)S(1)} %get-tuple-element.44.time_weight, f32[1,256]{1,0:T(1,128)S(1)} %get-tuple-element.45.time_bias, ...), custom_call_target="tpu_custom_call" | custom-call | flops 1000 | bytes 907264 | tf_op jit(solution)/shard_map/embed/pallas_call | solution.py:488
  11.3 0.7 %collective-permute-done.2.rest_2_ = bf16[16,256]{1,0:T(8,128)(2,1)S(1)} collective-permute-done((bf16[16,256]{1,0:T(8,128)(2,1)S(1)}, bf16[16,256]{1,0:T(8,128)(2,1)S(1)}, u32[]{:S(2)}, u32[]{:S(2)}) %collective-permute-start.2) | collective-permute-done | bytes 8224 | tf_op jit(solution)/shard_map/ppermute | solution.py:503
  12.1 0.0 collective-permute-done.one.rest_1_
  12.1 0.9 %second.1 = (bf16[256,256]{1,0:T(8,128)(2,1)S(1)}, f32[8,256]{1,0:T(8,128)S(1)}, bf16[80,256]{1,0:T(8,128)(2,1)S(1)}, bf16[16,256]{1,0:T(8,128)(2,1)S(1)}, bf16[80,256]{1,0:T(8,128)(2,1)S(1)}) custom-call(bf16[256,256]{1,0:T(8,128)(2,1)S(1)} %get-tuple-element.37.images, bf16[144,256]{1,0:T(8,128)(2,1)S(1)} %collective-permute-done.one.rest_1_, ...), custom_call_target="tpu_custom_call" | custom-call | flops 301989888 | bytes 1632256 | tf_op jit(solution)/shard_map/second/pallas_call | solution.py:488
  13.0 1.2 %collective-permute-start.3 = (bf16[80,256]{1,0:T(8,128)(2,1)S(1)}, bf16[80,256]{1,0:T(8,128)(2,1)S(1)}, u32[]{:S(2)}, u32[]{:S(2)}) collective-permute-start(bf16[80,256]{1,0:T(8,128)(2,1)S(1)} %get-tuple-element.49), channel_id=1, source_target_pairs={{0,4},{4,0},{8,12},{12,8},{1,5},{5,1},{9,13},{13,9},{2,6},{6,2},{1... | collective-permute-start | bytes 122888 | tf_op jit(solution)/shard_map/ppermute | solution.py:503
  14.1 2.5 %collective-permute-start.4 = (bf16[80,256]{1,0:T(8,128)(2,1)S(1)}, bf16[80,256]{1,0:T(8,128)(2,1)S(1)}, u32[]{:S(2)}, u32[]{:S(2)}) collective-permute-start(bf16[80,256]{1,0:T(8,128)(2,1)S(1)} %get-tuple-element.50), channel_id=1, source_target_pairs={{0,12},{4,8},{8,4},{12,0},{1,13},{5,9},{9,5},{13,1},{2,14},{6,10},... | collective-permute-start | bytes 122888 | tf_op jit(solution)/shard_map/ppermute | solution.py:503
  16.6 0.0 collective-permute-start.5
  16.6 0.5 %grad.1.grad_active = f32[256,256]{1,0:T(8,128)S(1)} custom-call(bf16[256,256]{1,0:T(8,128)(2,1)S(1)} %get-tuple-element.51.cotangent, bf16[144,256]{1,0:T(8,128)(2,1)S(1)} %collective-permute-done.one.rest_1_, bf16[144,256]{1,0:T(8,128)(2,1)S(1)} %collective-permute-done.1.three.rest_3_, bf16[9,256,256]{2,1,0:T(8,128)(2,1)S(1)} %bitcast.13), custom_call_target="tpu_custom_call" | custom-call | flops 301989888 | bytes 1458176 | tf_op jit(solution)/shard_map/grad/pallas_call | solution.py:488
  17.1 1.7 %cross.1 = (f32[256,256]{1,0:T(8,128)S(1)}, bf16[2,384,256]{2,1,0:T(8,128)(2,1)S(1)}, bf16[32,256]{1,0:T(8,128)(2,1)S(1)}) custom-call(bf16[256,256]{1,0:T(8,128)(2,1)S(1)} %get-tuple-element.37.images, bf16[144,256]{1,0:T(8,128)(2,1)S(1)} %collective-permute-done.one.rest_1_, bf16[144,256]{1,0:T(8,128)(2,1)S(1)} %collective-permute-done.1.three.rest_3_, ...), custom_call_target="tpu_custom_call" | custom-call | flops 301989888 | bytes 1894400 | tf_op jit(solution)/shard_map/cross/pallas_call | solution.py:488
  18.8 2.3 %collective-permute-done.5.rest_2_ = bf16[16,256]{1,0:T(8,128)(2,1)S(1)} collective-permute-done((bf16[16,256]{1,0:T(8,128)(2,1)S(1)}, bf16[16,256]{1,0:T(8,128)(2,1)S(1)}, u32[]{:S(2)}, u32[]{:S(2)}) %collective-permute-start.5) | collective-permute-done | bytes 8224 | tf_op jit(solution)/shard_map/ppermute | solution.py:503
  21.2 0.0 collective-permute-done.3.one.rest_1_
  21.2 0.0 collective-permute-done.4.three.rest_3_
  21.2 0.9 %third.1 = (bf16[384,256]{1,0:T(8,128)(2,1)S(1)}, f32[256,256]{1,0:T(8,128)S(1)}, f32[8,256]{1,0:T(8,128)S(1)}, bf16[112,256]{1,0:T(8,128)(2,1)S(1)}, bf16[48,25...) custom-call(bf16[256,256]{1,0:T(8,128)(2,1)S(1)} %get-tuple-element.48.hidden, ...), custom_call_target="tpu_custom_call" | custom-call | flops 301989888 | bytes 2164736 | tf_op jit(solution)/shard_map/third/pallas_call | solution.py:488
  22.1 0.1 collective-permute-start.6
  22.1 2.1 %collective-permute-start.7 = (bf16[112,256]{1,0:T(8,128)(2,1)S(1)}, bf16[112,256]{1,0:T(8,128)(2,1)S(1)}, u32[]{:S(2)}, u32[]{:S(2)}) collective-permute-start(bf16[112,256]{1,0:T(8,128)(2,1)S(1)} %get-tuple-element.64), channel_id=1, source_target_pairs={{0,12},{4,8},{8,4},{12,0},{1,13},{5,9},{9,5},{13,1},{2,14},{6,10},... | collective-permute-start | bytes 172040 | tf_op jit(solution)/shard_map/ppermute | solution.py:503
  24.2 1.4 %collective-permute-start.8 = (bf16[48,256]{1,0:T(8,128)(2,1)S(1)}, bf16[48,256]{1,0:T(8,128)(2,1)S(1)}, u32[]{:S(2)}, u32[]{:S(2)}) collective-permute-start(bf16[48,256]{1,0:T(8,128)(2,1)S(1)} %get-tuple-element.67.rest_0_), channel_id=1, source_target_pairs={{0,8},{4,12},{8,0},{12,4},{1,9},{5,13},{9,1},{13,5},{2,10},{6,14},... | collective-permute-start | bytes 73736 | tf_op jit(solution)/shard_map/ppermute | solution.py:503
  25.6 0.5 %branch.1 = (bf16[256,256]{1,0:T(8,128)(2,1)S(1)}, f32[8,128]{1,0:T(8,128)S(1)}) custom-call(bf16[384,256]{1,0:T(8,128)(2,1)S(1)} %get-tuple-element.59.active, bf16[9,256,256]{2,1,0:T(8,128)(2,1)S(1)} %bitcast.14), custom_call_target="tpu_custom_call" | custom-call | flops 301989888 | bytes 1376256 | tf_op jit(solution)/shard_map/branch/pallas_call | solution.py:488
  26.1 0.7 %copy.17 = bf16[1,4,64,256]{3,2,1,0:T(8,128)(2,1)} copy(bf16[1,4,64,256]{3,2,1,0:T(8,128)(2,1)S(1)} %bitcast.12) | data formatting | bytes 262144
  26.8 2.3 %collective-permute-done.8.rest_2_ = bf16[48,256]{1,0:T(8,128)(2,1)S(1)} collective-permute-done((bf16[48,256]{1,0:T(8,128)(2,1)S(1)}, bf16[48,256]{1,0:T(8,128)(2,1)S(1)}, u32[]{:S(2)}, u32[]{:S(2)}) %collective-permute-start.8) | collective-permute-done | bytes 24608 | tf_op jit(solution)/shard_map/ppermute | solution.py:503
  29.1 1.6 %collective-permute-start.10 = (f32[8,256]{1,0:T(8,128)S(1)}, f32[8,256]{1,0:T(8,128)S(1)}, u32[]{:S(2)}, u32[]{:S(2)}) collective-permute-start(f32[8,256]{1,0:T(8,128)S(1)} %pairs.1.rest_0_), channel_id=1, source_target_pairs={{0,2},{1,3},{2,0},{3,1},{4,6},{5,7},{6,4},{7,5},{8,10},{9,11},{10,... | collective-permute-start | bytes 24584 | tf_op jit(solution)/shard_map/ppermute | solution.py:503
  30.7 0.7 %collective-permute-start.9 = (f32[8,256]{1,0:T(8,128)S(1)}, f32[8,256]{1,0:T(8,128)S(1)}, u32[]{:S(2)}, u32[]{:S(2)}) collective-permute-start(f32[8,256]{1,0:T(8,128)S(1)} %pairs.1.rest_0_), channel_id=1, source_target_pairs={{0,1},{1,0},{2,3},{3,2},{4,5},{5,4},{6,7},{7,6},{8,9},{9,8},{10,11... | collective-permute-start | bytes 24584 | tf_op jit(solution)/shard_map/ppermute | solution.py:503
  31.3 1.0 %fourth.1 = bf16[256,256]{1,0:T(8,128)(2,1)S(1)} custom-call(f32[8,128]{1,0:T(8,128)S(1)} %get-tuple-element.61.token, f32[256,256]{1,0:T(8,128)S(1)} %get-tuple-element.62.grad_norm, bf16[112,256]{1,0:T(8,128)(2,1)S(1)} %collective-permute-done.6.grad_one.rest_1_, bf16[112,256]{1,0:T(8,128)(2,1)S(1)} %collective-permute-done.7.grad_three.rest_3_, ...), custom_call_target="tpu_custom_call" | custom-call | flops 301989888 | bytes 2347008 | tf_op jit(solution)/shard_map/fourth/pallas_call | solution.py:488
  32.4 0.7 %copy.18 = bf16[1,4,64,256]{3,2,1,0:T(8,128)(2,1)} copy(bf16[1,4,64,256]{3,2,1,0:T(8,128)(2,1)S(1)} %bitcast.11) | data formatting | bytes 262144
  33.0 0.8 %collective-permute-done.11.rest_3_ = f32[8,256]{1,0:T(8,128)S(1)} collective-permute-done((f32[8,256]{1,0:T(8,128)S(1)}, f32[8,256]{1,0:T(8,128)S(1)}, u32[]{:S(2)}, u32[]{:S(2)}) %collective-permute-start.11) | collective-permute-done | bytes 8224 | tf_op jit(solution)/shard_map/ppermute | solution.py:503
  33.8 1.1 %weight.1 = (f32[256,512]{1,0:T(8,128)}, f32[1,512]{1,0:T(1,128)}) custom-call(f32[8,256]{1,0:T(8,128)S(1)} %pairs.1.rest_0_, f32[8,256]{1,0:T(8,128)S(1)} %collective-permute-done.9.rest_1_, f32[8,256]{1,0:T(8,128)S(1)} %collective-permute-done.10.rest_2_, f32[8,256]{1,0:T(8,128)S(1)} %collective-permute-done.11.rest_3_), custom_call_target="tpu_custom_call" | custom-call | flops 1000 | bytes 32768 | tf_op jit(solution)/shard_map/weight/pallas_call | solution.py:488
  (9 shorter events, 0.0 us)
Async XLA Ops:
  1.9 10.1 %collective-permute-start = (bf16[144,256]{1,0:T(8,128)(2,1)S(1)}, bf16[144,256]{1,0:T(8,128)(2,1)S(1)}, u32[]{:S(2)}, u32[]{:S(2)}) collective-permute-start(bf16[144,256]{1,0:T(8,128)(2,1)S(1)} %get-tuple-element.38), channel_id=1, source_target_pairs={{0,4},{4,0},{8,12},{12,8},{1,5},{5,1},{9,13},{13,9},{2,6},{6,2},{1... | collective-permute-start | bytes 221192 | tf_op jit(solution)/shard_map/ppermute | solution.py:503
  5.0 7.0 %collective-permute-start.1 = (bf16[144,256]{1,0:T(8,128)(2,1)S(1)}, bf16[144,256]{1,0:T(8,128)(2,1)S(1)}, u32[]{:S(2)}, u32[]{:S(2)}) collective-permute-start(bf16[144,256]{1,0:T(8,128)(2,1)S(1)} %get-tuple-element.39), channel_id=1, source_target_pairs={{0,12},{4,8},{8,4},{12,0},{1,13},{5,9},{9,5},{13,1},{2,14},{6,10},... | collective-permute-start | bytes 221192 | tf_op jit(solution)/shard_map/ppermute | solution.py:503
  7.5 4.5 %collective-permute-start.2 = (bf16[16,256]{1,0:T(8,128)(2,1)S(1)}, bf16[16,256]{1,0:T(8,128)(2,1)S(1)}, u32[]{:S(2)}, u32[]{:S(2)}) collective-permute-start(bf16[16,256]{1,0:T(8,128)(2,1)S(1)} %get-tuple-element.47.rest_0_), channel_id=1, source_target_pairs={{0,8},{4,12},{8,0},{12,4},{1,9},{5,13},{9,1},{13,5},{2,10},{6,14},... | collective-permute-start | bytes 24584 | tf_op jit(solution)/shard_map/ppermute | solution.py:503
  11.0 5.7 %copy-start = (bf16[3,3,256,256]{3,2,1,0:T(8,128)(2,1)S(1)}, bf16[3,3,256,256]{3,2,1,0:T(8,128)(2,1)}, u32[]{:S(2)}) copy-start(bf16[3,3,256,256]{3,2,1,0:T(8,128)(2,1)} %param.20) | copy-start | bytes 3538948
  13.0 8.2 %collective-permute-start.3 = (bf16[80,256]{1,0:T(8,128)(2,1)S(1)}, bf16[80,256]{1,0:T(8,128)(2,1)S(1)}, u32[]{:S(2)}, u32[]{:S(2)}) collective-permute-start(bf16[80,256]{1,0:T(8,128)(2,1)S(1)} %get-tuple-element.49), channel_id=1, source_target_pairs={{0,4},{4,0},{8,12},{12,8},{1,5},{5,1},{9,13},{13,9},{2,6},{6,2},{1... | collective-permute-start | bytes 122888 | tf_op jit(solution)/shard_map/ppermute | solution.py:503
  14.1 7.0 %collective-permute-start.4 = (bf16[80,256]{1,0:T(8,128)(2,1)S(1)}, bf16[80,256]{1,0:T(8,128)(2,1)S(1)}, u32[]{:S(2)}, u32[]{:S(2)}) collective-permute-start(bf16[80,256]{1,0:T(8,128)(2,1)S(1)} %get-tuple-element.50), channel_id=1, source_target_pairs={{0,12},{4,8},{8,4},{12,0},{1,13},{5,9},{9,5},{13,1},{2,14},{6,10},... | collective-permute-start | bytes 122888 | tf_op jit(solution)/shard_map/ppermute | solution.py:503
  16.6 4.5 %collective-permute-start.5 = (bf16[16,256]{1,0:T(8,128)(2,1)S(1)}, bf16[16,256]{1,0:T(8,128)(2,1)S(1)}, u32[]{:S(2)}, u32[]{:S(2)}) collective-permute-start(bf16[16,256]{1,0:T(8,128)(2,1)S(1)} %get-tuple-element.58.rest_0_), channel_id=1, source_target_pairs={{0,8},{4,12},{8,0},{12,4},{1,9},{5,13},{9,1},{13,5},{2,10},{6,14},... | collective-permute-start | bytes 24584 | tf_op jit(solution)/shard_map/ppermute | solution.py:503
  22.1 7.0 %collective-permute-start.6 = (bf16[112,256]{1,0:T(8,128)(2,1)S(1)}, bf16[112,256]{1,0:T(8,128)(2,1)S(1)}, u32[]{:S(2)}, u32[]{:S(2)}) collective-permute-start(bf16[112,256]{1,0:T(8,128)(2,1)S(1)} %get-tuple-element.63), channel_id=1, source_target_pairs={{0,4},{4,0},{8,12},{12,8},{1,5},{5,1},{9,13},{13,9},{2,6},{6,2},{1... | collective-permute-start | bytes 172040 | tf_op jit(solution)/shard_map/ppermute | solution.py:503
  22.1 7.0 %collective-permute-start.7 = (bf16[112,256]{1,0:T(8,128)(2,1)S(1)}, bf16[112,256]{1,0:T(8,128)(2,1)S(1)}, u32[]{:S(2)}, u32[]{:S(2)}) collective-permute-start(bf16[112,256]{1,0:T(8,128)(2,1)S(1)} %get-tuple-element.64), channel_id=1, source_target_pairs={{0,12},{4,8},{8,4},{12,0},{1,13},{5,9},{9,5},{13,1},{2,14},{6,10},... | collective-permute-start | bytes 172040 | tf_op jit(solution)/shard_map/ppermute | solution.py:503
  24.2 4.9 %collective-permute-start.8 = (bf16[48,256]{1,0:T(8,128)(2,1)S(1)}, bf16[48,256]{1,0:T(8,128)(2,1)S(1)}, u32[]{:S(2)}, u32[]{:S(2)}) collective-permute-start(bf16[48,256]{1,0:T(8,128)(2,1)S(1)} %get-tuple-element.67.rest_0_), channel_id=1, source_target_pairs={{0,8},{4,12},{8,0},{12,4},{1,9},{5,13},{9,1},{13,5},{2,10},{6,14},... | collective-permute-start | bytes 73736 | tf_op jit(solution)/shard_map/ppermute | solution.py:503
  29.1 3.9 %collective-permute-start.10 = (f32[8,256]{1,0:T(8,128)S(1)}, f32[8,256]{1,0:T(8,128)S(1)}, u32[]{:S(2)}, u32[]{:S(2)}) collective-permute-start(f32[8,256]{1,0:T(8,128)S(1)} %pairs.1.rest_0_), channel_id=1, source_target_pairs={{0,2},{1,3},{2,0},{3,1},{4,6},{5,7},{6,4},{7,5},{8,10},{9,11},{10,... | collective-permute-start | bytes 24584 | tf_op jit(solution)/shard_map/ppermute | solution.py:503
  30.7 3.1 %collective-permute-start.11 = (f32[8,256]{1,0:T(8,128)S(1)}, f32[8,256]{1,0:T(8,128)S(1)}, u32[]{:S(2)}, u32[]{:S(2)}) collective-permute-start(f32[8,256]{1,0:T(8,128)S(1)} %pairs.1.rest_0_), channel_id=1, source_target_pairs={{0,3},{1,2},{2,1},{3,0},{4,7},{5,6},{6,5},{7,4},{8,11},{9,10},{10,... | collective-permute-start | bytes 24584 | tf_op jit(solution)/shard_map/ppermute | solution.py:503
  30.7 3.1 %collective-permute-start.9 = (f32[8,256]{1,0:T(8,128)S(1)}, f32[8,256]{1,0:T(8,128)S(1)}, u32[]{:S(2)}, u32[]{:S(2)}) collective-permute-start(f32[8,256]{1,0:T(8,128)S(1)} %pairs.1.rest_0_), channel_id=1, source_target_pairs={{0,1},{1,0},{2,3},{3,2},{4,5},{5,4},{6,7},{7,6},{8,9},{9,8},{10,11... | collective-permute-start | bytes 24584 | tf_op jit(solution)/shard_map/ppermute | solution.py:503

commit v7 on v6

--- a/solution.py
+++ b/solution.py
@@ -87,7 +87,7 @@
     return lax.bitwise_and(index, cols - 1)
 
 
-def conv(padded_ref, kernel_ref, cells, cols, flipped, turned=False):
+def conv(padded_ref, kernel_ref, cells, cols, flipped):
     parts = []
     for j in range(3):
         total = None
@@ -96,7 +96,7 @@
             product = lax.dot_general(
                 padded_ref[start : start + cells],
                 kernel_ref[3 * i + j],
-                (((1,), (1 if flipped and not turned else 0,)), ((), ())),
+                (((1,), (1 if flipped else 0,)), ((), ())),
                 preferred_element_type=F32,
             )
             total = product if total is None else total + product
@@ -170,7 +170,7 @@
         copy.wait()
 
 
-def embed_kernel(instant, table, time_weight, time_bias, adaptive_weight, out):
+def embedding(step, label, table, time_weight, time_bias, adaptive_weight):
     channels = adaptive_weight.shape[1] // 2
     half = time_weight.shape[0] // 2
 
@@ -178,16 +178,16 @@
         return joined(jnp.dot(terms(rows8(vector)), weights, preferred_element_type=F32))[0:1]
 
     place = lax.broadcasted_iota(jnp.int32, (8, half), 1).astype(F32)
-    angles = instant[0:1, 0:1].astype(F32) * jnp.exp(-math.log(10000.0) * place / half)
+    angles = step.astype(F32) * jnp.exp(-math.log(10000.0) * place / half)
     sinusoid = jnp.concatenate([jnp.cos(angles), jnp.sin(angles)], axis=1)[0:1]
     classes = lax.broadcasted_iota(jnp.int32, (16, table.shape[0]), 1)
-    onehot = (classes == instant[1:2, 0:1]).astype(F32).astype(BF16)
+    onehot = (classes == label).astype(F32).astype(BF16)
     row = jnp.dot(onehot, table[...], preferred_element_type=F32)[0:1]
     hidden = times(sinusoid, time_weight[...]) + time_bias[...]
-    embedding = hidden * sigmoid(hidden) + row
-    activated = embedding * sigmoid(embedding)
+    embedded = hidden * sigmoid(hidden) + row
+    activated = embedded * sigmoid(embedded)
     partial = times(activated, adaptive_weight[...])
-    out[...] = rows8(partial[:, :channels], partial[:, channels:], activated)
+    return rows8(partial[:, :channels], partial[:, channels:], activated)
 
 
 def second_kernel(dims, n_stats, images, one, three, weights, gain, bias, embed, *rest):
@@ -225,27 +225,27 @@
     return (1.0 * (row == lax.broadcasted_iota(jnp.int32, (size, size), 1))).astype(BF16)
 
 
-def turn_kernel(count, source, *refs):
-    sources, weights, copies_to = refs[:count], refs[count], refs[count + 1 : 2 * count + 1]
-    turned, grouped, sems = refs[2 * count + 1 :]
-    main = pltpu.make_async_copy(source, weights, sems.at[count])
+def turn_kernel(step, label, table, time_weight, time_bias, mix, source, bias_source, weights, bias, embed, grouped, sems):
     copies = [
-        pltpu.make_async_copy(start, end, sems.at[k])
-        for k, (start, end) in enumerate(zip(sources, copies_to, strict=True))
+        pltpu.make_async_copy(source, weights, sems.at[0]),
+        pltpu.make_async_copy(bias_source, bias, sems.at[1]),
     ]
-    for copy in (main, *copies):
+    for copy in copies:
         copy.start()
-    channels = weights.shape[1]
-    rows = jnp.concatenate([identity(channels), group_columns(channels, 0, GN_GROUPS, 0)], axis=0)
-    main.wait()
-    for k in range(source.shape[0]):
-        product = lax.dot_general(
-            rows, weights[k], (((1,), (1,)), ((), ())), preferred_element_type=F32
-        )
-        turned[k] = product[:channels].astype(BF16)
-        grouped[k] = product[channels:]
+    embed[...] = embedding(step[0], label[0], table, time_weight, time_bias, mix)
+    columns = tiled_columns(weights.shape[1])
     for copy in copies:
         copy.wait()
+    for k in range(source.shape[0]):
+        grouped[k] = jnp.dot(weights[k], columns, preferred_element_type=F32)
+
+
+def tiled_columns(channels):
+    size = (channels, 4 * GN_GROUPS)
+    shift = (channels // GN_GROUPS).bit_length() - 1
+    group = lax.shift_right_logical(lax.broadcasted_iota(jnp.int32, size, 0), shift)
+    column = lax.bitwise_and(lax.broadcasted_iota(jnp.int32, size, 1), GN_GROUPS - 1)
+    return (1.0 * (group == column)).astype(BF16)
 
 
 def group_columns(channels, offset, length, axis):
@@ -273,7 +273,7 @@
 
 
 def cross_kernel(
-    dims, images, one, three, stat_one, gain, bias, hidden, turned, grouped, slope, factors, matrix, left, products
+    dims, images, one, three, stat_one, gain, bias, hidden, weights, grouped, slope, factors, matrix, left, products
 ):
     cells, cols, channels, tiles = dims
     place = standing(tiles)
@@ -292,56 +292,60 @@
         factors[which, 0:cols] = jnp.where(place[0] > 0, top, 0.0).astype(BF16)
         factors[which, cols : cols + cells] = own[which].astype(BF16)
         factors[which, cols + cells :] = jnp.where(place[0] < tiles - 1, bottom, 0.0).astype(BF16)
+    unit = identity(channels)
+    for which in range(2):
+        for i in range(3):
+            place_at = (3 * which + i) * channels
+            left[place_at : place_at + channels] = lax.dot_general(
+                unit,
+                factors[which, i * cols : i * cols + cells],
+                (((1,), (1,)), ((), ())),
+                preferred_element_type=F32,
+            ).astype(BF16)
     wide = hidden[...].astype(F32)
-    unit = identity(channels)
-    for j, line in enumerate((shifted(wide, cols, -1).astype(BF16), hidden[...], shifted(wide, cols, 1).astype(BF16))):
-        left[j * channels : (j + 1) * channels] = lax.dot_general(
-            unit, line, (((1,), (1,)), ((), ())), preferred_element_type=F32
-        ).astype(BF16)
-    row = lax.broadcasted_iota(jnp.int32, (16, cells), 0)
-    column = lax.bitwise_and(lax.broadcasted_iota(jnp.int32, (16, cells), 1), cols - 1)
-    inside = jnp.where(row == 0, 1.0 * (column < cols - 1), jnp.where(row == 2, 1.0 * (column > 0), 1.0))
-    left[3 * channels :] = inside.astype(BF16)
-    for i in range(3):
-        for which in range(2):
-            products[which, i] = jnp.dot(
-                left[...], factors[which, i * cols : i * cols + cells], preferred_element_type=F32
-            )
+    lines = (shifted(wide, cols, -1).astype(BF16), hidden[...], shifted(wide, cols, 1).astype(BF16))
+    for j, line in enumerate(lines):
+        products[j] = jnp.dot(left[...], line, preferred_element_type=F32)
+    column = lax.bitwise_and(lax.broadcasted_iota(jnp.int32, (cells, 128), 0), cols - 1)
+    which_column = lax.broadcasted_iota(jnp.int32, (cells, 128), 1)
+    inside = jnp.where(
+        which_column == 0, 1.0 * (column < cols - 1), jnp.where(which_column == 2, 1.0 * (column > 0), 1.0)
+    )
+    plain_sums = jnp.dot(left[...], inside.astype(BF16), preferred_element_type=F32)
     step = channels // 8
     totals = ([], [])
     for start in range(0, channels, step):
         parts = ([], [])
         for k in range(9):
-            matrix_rows = turned[k, start : start + step].astype(F32)
+            matrix_rows = weights[k, start : start + step].astype(F32)
             for which in range(2):
-                begin = (k % 3) * channels + start
-                parts[which].append(products[which, k // 3, begin : begin + step] * matrix_rows)
+                begin = (3 * which + k // 3) * channels + start
+                parts[which].append(products[k % 3, begin : begin + step] * matrix_rows)
         for which in range(2):
             totals[which].append(tree_sum(parts[which]))
+    block = lax.shift_right_logical(
+        lax.broadcasted_iota(jnp.int32, (channels, 4 * GN_GROUPS), 1), GN_GROUPS.bit_length() - 1
+    )
     spread = jnp.zeros((channels, 4 * GN_GROUPS), F32)
-    flat = jnp.zeros((GN_GROUPS, 4 * GN_GROUPS), F32)
     for which in range(2):
-        total = jnp.concatenate(totals[which], axis=0)
+        for part in halves(jnp.concatenate(totals[which], axis=0)):
+            spread += jnp.dot(
+                part, group_columns(channels, which * GN_GROUPS, 4 * GN_GROUPS, 1), preferred_element_type=F32
+            )
         plain = tree_sum(
             [
-                grouped[k] * products[which, k // 3, 3 * channels + k % 3 : 3 * channels + k % 3 + 1]
+                grouped[k]
+                * plain_sums[(3 * which + k // 3) * channels : (3 * which + k // 3 + 1) * channels, k % 3 : k % 3 + 1]
                 for k in range(9)
             ]
         )
-        for part in halves(total):
-            spread += jnp.dot(
-                part, group_columns(channels, which * GN_GROUPS, 4 * GN_GROUPS, 1), preferred_element_type=F32
-            )
-        for part in halves(plain):
-            flat += jnp.dot(
-                part, group_columns(channels, (2 + which) * GN_GROUPS, 4 * GN_GROUPS, 1), preferred_element_type=F32
-            )
+        spread += jnp.where(block == 2 + which, plain, 0.0)
     summed = jnp.sum(spread.reshape(GN_GROUPS, channels // GN_GROUPS, 4 * GN_GROUPS), axis=1)
-    matrix[...] = jnp.concatenate(halves(summed + flat), axis=1)
+    matrix[...] = jnp.concatenate(halves(summed), axis=1)
 
 
 def third_kernel(
-    dims, n_stats, hidden, one, three, grad_active, adaptive_bias, turned, factors, matrix, *rest
+    dims, n_stats, hidden, one, three, grad_active, adaptive_bias, weights, factors, matrix, *rest
 ):
     cells, cols, channels, tiles = dims
     place = standing(tiles)
@@ -369,7 +373,7 @@
     padded[0 : 2 * cols] = edge
     padded[2 * cols : 2 * cols + cells] = (grad * inverse).astype(BF16)
     padded[2 * cols + cells :] = edge
-    base = conv(padded, turned, cells + 2 * cols, cols, True, True)
+    base = conv(padded, weights, cells + 2 * cols, cols, True)
     _, pre, gate = pieces(above)
     active[0:cols] = jnp.where(place[0] > 0, pre * gate, 0.0).astype(BF16)
     _, pre, gate = pieces(below)
@@ -403,7 +407,7 @@
 
 
 def fourth_kernel(
-    dims, n_stats, token, grad_norm, grad_one, grad_three, hidden, one, three, stat_two, turned, images, stat_one, slope, *rest
+    dims, n_stats, token, grad_norm, grad_one, grad_three, hidden, one, three, stat_two, weights, images, stat_one, slope, *rest
 ):
     cells, cols, channels, tiles = dims
     place = standing(tiles)
@@ -433,22 +437,31 @@
     padded[cols + cells :] = jnp.where(
         place[0] < tiles - 1, grad_hidden(grad_below, below), 0.0
     ).astype(BF16)
-    grad = conv(padded, turned, cells, cols, True, True) * slope[...]
+    grad = conv(padded, weights, cells, cols, True) * slope[...]
     beta = paired * inverse * inverse
     alpha = plain * inverse - beta * mean
     per = channels // GN_GROUPS
-    weights = terms(rows8(alpha / per, beta / per))
     picked = joined(
-        jnp.dot(weights, group_columns(channels, 0, GN_GROUPS, 1), preferred_element_type=F32)
-    )
-    found = jnp.dot(picked, matrix, precision=lax.Precision.HIGHEST, preferred_element_type=F32)
-    found = terms(rows8(pltpu.roll(found, width // 2, 1)[0:1] + found[1:2]))
-    means = []
-    for which in range(2):
-        back = joined(
-            jnp.dot(found, group_columns(channels, which * GN_GROUPS, width, 0), preferred_element_type=F32)
-        )
-        means.append((reduced[2 + which : 3 + which] - back[0:1]) / total)
+        jnp.dot(terms(rows8(alpha / per, beta / per)), tiled_columns(channels), preferred_element_type=F32)
+    )
+    block = lax.shift_right_logical(
+        lax.broadcasted_iota(jnp.int32, (1, width), 1), GN_GROUPS.bit_length() - 1
+    )
+    vectors = [
+        jnp.where(block == which, picked[1:2], jnp.where(block == 2 + which, picked[0:1], 0.0))
+        for which in range(2)
+    ]
+    found = lax.dot_general(
+        rows8(*vectors),
+        matrix,
+        (((1,), (1,)), ((), ())),
+        precision=lax.Precision.HIGHEST,
+        preferred_element_type=F32,
+    )
+    back = joined(
+        jnp.dot(terms(found), group_columns(channels, 0, GN_GROUPS, 0), preferred_element_type=F32)
+    )
+    means = [(reduced[2 + which : 3 + which] - back[which : which + 1]) / total for which in range(2)]
     normed = (images[...].astype(F32) - stat_one[0:1]) * stat_one[1:2]
     out[...] = (stat_one[1:2] * (grad - means[0] - normed * means[1])).astype(BF16)
 
@@ -558,8 +571,12 @@
         cotangent.reshape(cells, channels),
         norm_gain[None],
         norm_bias[None],
-    )
-    flat, flat_cot, gain, bias, one, two, three = call(
+        class_table,
+        time_weight,
+        time_bias,
+        mix,
+    )
+    flat, flat_cot, gain, bias, class_table, time_weight, time_bias, mix, one, two, three = call(
         functools.partial(first_kernel, dims),
         (*like(loads), halos, small, halos),
         tuple(pin(part) for part in loads),
@@ -570,22 +587,19 @@
     image_one, image_three, stats = exchange(one, two, three)
     taps = conv_first.reshape(9, channels, channels)
     weights_second = conv_second.reshape(9, channels, channels)
-    loads = (time_weight, mix, class_table, time_bias, adaptive_bias[None])
-    weights_first, time_weight, mix, class_table, time_bias, adaptive_bias, turned, grouped = call(
-        functools.partial(turn_kernel, len(loads)),
-        (*like((taps, *loads)), shape(taps.shape, BF16), shape((9, GN_GROUPS, channels), F32)),
-        tuple(pin(part) for part in (taps, *loads)),
-        (pltpu.SemaphoreType.DMA((len(loads) + 1,)),),
+    weights_first, adaptive_bias, embed, grouped = call(
+        turn_kernel,
+        (
+            shape(taps.shape, BF16),
+            shape((1, 2 * channels), F32),
+            block,
+            shape((9, channels, 4 * GN_GROUPS), F32),
+        ),
+        (timesteps, class_ids, class_table, time_weight, time_bias, mix, pin(taps), pin(adaptive_bias[None])),
+        (pltpu.SemaphoreType.DMA((2,)),),
         flops=conv_flops,
         name="turn",
-        spaces={k: pl.ANY for k in range(len(loads) + 1)},
-    )
-    instant = jnp.broadcast_to(jnp.concatenate([timesteps[:1], class_ids[:1]])[:, None], (2, 128))
-    embed = call(
-        embed_kernel,
-        block,
-        (instant, class_table, time_weight, time_bias, mix),
-        name="embed",
+        spaces={0: pltpu.SMEM, 1: pltpu.SMEM, 6: pl.ANY, 7: pl.ANY},
     )
 
     hidden, stat_one, one, two, three = call(
@@ -608,10 +622,10 @@
     slope, factors, matrix = call(
         functools.partial(cross_kernel, dims),
         (wide, shape((2, cells + 2 * cols, channels), BF16), shape((GN_GROUPS, 8 * GN_GROUPS), BF16)),
-        (flat, image_one, image_three, stat_one, gain, bias, hidden, turned, grouped),
+        (flat, image_one, image_three, stat_one, gain, bias, hidden, weights_first, grouped),
         (
-            pltpu.VMEM((3 * channels + 16, cells), BF16),
-            pltpu.VMEM((2, 3, 3 * channels + 16, channels), F32),
+            pltpu.VMEM((6 * channels, cells), BF16),
+            pltpu.VMEM((3, 6 * channels, channels), F32),
         ),
         conv_flops,
         name="cross",
@@ -621,7 +635,7 @@
     active, grad_norm, stat_two, one, two, three = call(
         functools.partial(third_kernel, dims, len(stats)),
         (shape((cells + 2 * cols, channels), BF16), wide, block, mail_halo, mail, mail_halo),
-        (hidden, hidden_one, hidden_three, grad_active, adaptive_bias, turned, factors, matrix, *stats),
+        (hidden, hidden_one, hidden_three, grad_active, adaptive_bias, weights_first, factors, matrix, *stats),
         (pltpu.VMEM((cells + 4 * cols, channels), BF16),),
         conv_flops,
         name="third",
@@ -644,7 +658,7 @@
     input_grad = call(
         functools.partial(fourth_kernel, dims, len(stats)),
         pltpu.VMEM((cells, channels), BF16),
-        (token, grad_norm, grad_one, grad_three, hidden, hidden_one, hidden_three, stat_two, turned, flat, stat_one, slope, *stats),
+        (token, grad_norm, grad_one, grad_three, hidden, hidden_one, hidden_three, stat_two, weights_first, flat, stat_one, slope, *stats),
         (padded,),
         conv_flops,
         name="fourth",

time: 35 us -> 34.7 us (level)
    pallas_call x11 -> x10, Pallas kernels: 10.1 us -> 9.92 us  [call(): pl.pallas_call(kernel, out_shape=out_shapes, in_specs=[pl.BlockSpec(memor...]
  transfers between devices with their start and end apart: 12 -> 12, of which waited for: 4 -> 4; matrix products, arithmetic and copies ran while one was open for 4% -> 4% of each run, Pallas kernels for 17% -> 16%
where the time goes in v7:
time: 34.7 us; the launch traced here: 34.5 us
  starting transfers between devices  15 us (43%)
  Pallas kernels  9.92 us (29%)
  waiting for transfers between devices  6.25 us (18%)
  between operations  2.01 us (6%)
  local copies, waits for them, and re-layouts  1.32 us (4%)
    ppermute x12, starting transfers between devices, swap(): return lax.ppermute(values, axis, [(i, i ^ distance) for i in range(size)])  15 us
    pallas_call x10, Pallas kernels, call(): pl.pallas_call(kernel, out_shape=out_shapes, in_specs=[pl.BlockSpec(memor...  9.92 us
    ppermute x12, waiting for transfers between devices, swap(): return lax.ppermute(values, axis, [(i, i ^ distance) for i in range(size)])  6.25 us
    unnamed x4, local copies, waits for them, and re-layouts  1.32 us
  transfers between devices with their start and end apart: 12, of which 4 were waited for; matrix products, arithmetic and copies ran while one was open for 4% of the time, Pallas kernels for 16%

profile of v7, /device:TPU:0, one launch (start us, length us, event | category | flops | bytes accessed | tf_op | source)
XLA Modules:
  0.0 34.5 jit_solution(15171788753232413233)
XLA Ops:
  0.6 1.4 %first.1 = (bf16[256,256]{1,0:T(8,128)(2,1)S(1)}, bf16[256,256]{1,0:T(8,128)(2,1)S(1)}, f32[1,256]{1,0:T(1,128)S(1)}, f32[1,256]{1,0:T(1,128)S(1)}, bf16[1000,25...) custom-call(bf16[256,256]{1,0:T(8,128)(2,1)} %bitcast.16, ...), custom_call_target="tpu_custom_call" | custom-call | flops 1000 | bytes 1170432 | tf_op jit(solution)/shard_map/first/pallas_call | solution.py:501
  2.0 3.1 %collective-permute-start = (bf16[144,256]{1,0:T(8,128)(2,1)S(1)}, bf16[144,256]{1,0:T(8,128)(2,1)S(1)}, u32[]{:S(2)}, u32[]{:S(2)}) collective-permute-start(bf16[144,256]{1,0:T(8,128)(2,1)S(1)} %get-tuple-element.38), channel_id=1, source_target_pairs={{0,4},{4,0},{8,12},{12,8},{1,5},{5,1},{9,13},{13,9},{2,6},{6,2},{1... | collective-permute-start | bytes 221192 | tf_op jit(solution)/shard_map/ppermute | solution.py:516
  5.1 2.5 %collective-permute-start.1 = (bf16[144,256]{1,0:T(8,128)(2,1)S(1)}, bf16[144,256]{1,0:T(8,128)(2,1)S(1)}, u32[]{:S(2)}, u32[]{:S(2)}) collective-permute-start(bf16[144,256]{1,0:T(8,128)(2,1)S(1)} %get-tuple-element.39), channel_id=1, source_target_pairs={{0,12},{4,8},{8,4},{12,0},{1,13},{5,9},{9,5},{13,1},{2,14},{6,10},... | collective-permute-start | bytes 221192 | tf_op jit(solution)/shard_map/ppermute | solution.py:516
  7.6 0.1 collective-permute-start.2
  9.0 1.8 %turn.1 = (bf16[9,256,256]{2,1,0:T(8,128)(2,1)S(1)}, f32[1,512]{1,0:T(1,128)S(1)}, f32[8,256]{1,0:T(8,128)S(1)}, f32[9,256,128]{2,1,0:T(8,128)S(1)}) custom-call(s32[1]{0:T(128)S(6)} %copy.19.step, s32[1]{0:T(128)S(6)} %copy.20.label, bf16[1000,256]{1,0:T(8,128)(2,1)S(1)} %get-tuple-element.40.table, bf16[256,256]{1,0:T(8,128)(2,1)S(1)} %get-tuple-element.41.time_weight, ...), custom_call_target="tpu_custom_call" | custom-call | flops 301989888 | bytes 2087944 | tf_op jit(solution)/shard_map/turn/pallas_call | solution.py:501
  10.8 0.0 copy-start
  10.8 1.3 %collective-permute-done.2.rest_2_ = bf16[16,256]{1,0:T(8,128)(2,1)S(1)} collective-permute-done((bf16[16,256]{1,0:T(8,128)(2,1)S(1)}, bf16[16,256]{1,0:T(8,128)(2,1)S(1)}, u32[]{:S(2)}, u32[]{:S(2)}) %collective-permute-start.2) | collective-permute-done | bytes 8224 | tf_op jit(solution)/shard_map/ppermute | solution.py:516
  12.2 0.0 collective-permute-done.one.rest_1_
  12.2 0.0 collective-permute-done.1.three.rest_3_
  12.2 0.9 %second.1 = (bf16[256,256]{1,0:T(8,128)(2,1)S(1)}, f32[8,256]{1,0:T(8,128)S(1)}, bf16[80,256]{1,0:T(8,128)(2,1)S(1)}, bf16[16,256]{1,0:T(8,128)(2,1)S(1)}, bf16[80,256]{1,0:T(8,128)(2,1)S(1)}) custom-call(bf16[256,256]{1,0:T(8,128)(2,1)S(1)} %get-tuple-element.37.images, bf16[144,256]{1,0:T(8,128)(2,1)S(1)} %collective-permute-done.one.rest_1_, ...), custom_call_target="tpu_custom_call" | custom-call | flops 301989888 | bytes 1632256 | tf_op jit(solution)/shard_map/second/pallas_call | solution.py:501
  13.1 0.7 %collective-permute-start.3 = (bf16[80,256]{1,0:T(8,128)(2,1)S(1)}, bf16[80,256]{1,0:T(8,128)(2,1)S(1)}, u32[]{:S(2)}, u32[]{:S(2)}) collective-permute-start(bf16[80,256]{1,0:T(8,128)(2,1)S(1)} %get-tuple-element.50), channel_id=1, source_target_pairs={{0,4},{4,0},{8,12},{12,8},{1,5},{5,1},{9,13},{13,9},{2,6},{6,2},{1... | collective-permute-start | bytes 122888 | tf_op jit(solution)/shard_map/ppermute | solution.py:516
  13.8 2.3 %collective-permute-start.4 = (bf16[80,256]{1,0:T(8,128)(2,1)S(1)}, bf16[80,256]{1,0:T(8,128)(2,1)S(1)}, u32[]{:S(2)}, u32[]{:S(2)}) collective-permute-start(bf16[80,256]{1,0:T(8,128)(2,1)S(1)} %get-tuple-element.51), channel_id=1, source_target_pairs={{0,12},{4,8},{8,4},{12,0},{1,13},{5,9},{9,5},{13,1},{2,14},{6,10},... | collective-permute-start | bytes 122888 | tf_op jit(solution)/shard_map/ppermute | solution.py:516
  16.1 0.5 %collective-permute-start.5 = (bf16[16,256]{1,0:T(8,128)(2,1)S(1)}, bf16[16,256]{1,0:T(8,128)(2,1)S(1)}, u32[]{:S(2)}, u32[]{:S(2)}) collective-permute-start(bf16[16,256]{1,0:T(8,128)(2,1)S(1)} %get-tuple-element.58.rest_0_), channel_id=1, source_target_pairs={{0,8},{4,12},{8,0},{12,4},{1,9},{5,13},{9,1},{13,5},{2,10},{6,14},... | collective-permute-start | bytes 24584 | tf_op jit(solution)/shard_map/ppermute | solution.py:516
  16.6 0.5 %grad.1.grad_active = f32[256,256]{1,0:T(8,128)S(1)} custom-call(bf16[256,256]{1,0:T(8,128)(2,1)S(1)} %get-tuple-element.52.cotangent, bf16[144,256]{1,0:T(8,128)(2,1)S(1)} %collective-permute-done.one.rest_1_, bf16[144,256]{1,0:T(8,128)(2,1)S(1)} %collective-permute-done.1.three.rest_3_, bf16[9,256,256]{2,1,0:T(8,128)(2,1)S(1)} %bitcast.13), custom_call_target="tpu_custom_call" | custom-call | flops 301989888 | bytes 1458176 | tf_op jit(solution)/shard_map/grad/pallas_call | solution.py:501
  17.1 1.9 %cross.1 = (f32[256,256]{1,0:T(8,128)S(1)}, bf16[2,384,256]{2,1,0:T(8,128)(2,1)S(1)}, bf16[32,256]{1,0:T(8,128)(2,1)S(1)}) custom-call(bf16[256,256]{1,0:T(8,128)(2,1)S(1)} %get-tuple-element.37.images, bf16[144,256]{1,0:T(8,128)(2,1)S(1)} %collective-permute-done.one.rest_1_, bf16[144,256]{1,0:T(8,128)(2,1)S(1)} %collective-permute-done.1.three.rest_3_, ...), custom_call_target="tpu_custom_call" | custom-call | flops 301989888 | bytes 2779136 | tf_op jit(solution)/shard_map/cross/pallas_call | solution.py:501
  19.0 1.6 %collective-permute-done.5.rest_2_ = bf16[16,256]{1,0:T(8,128)(2,1)S(1)} collective-permute-done((bf16[16,256]{1,0:T(8,128)(2,1)S(1)}, bf16[16,256]{1,0:T(8,128)(2,1)S(1)}, u32[]{:S(2)}, u32[]{:S(2)}) %collective-permute-start.5) | collective-permute-done | bytes 8224 | tf_op jit(solution)/shard_map/ppermute | solution.py:516
  20.6 0.0 collective-permute-done.3.one.rest_1_
  20.6 0.0 collective-permute-done.4.three.rest_3_
  20.6 1.0 %third.1 = (bf16[384,256]{1,0:T(8,128)(2,1)S(1)}, f32[256,256]{1,0:T(8,128)S(1)}, f32[8,256]{1,0:T(8,128)S(1)}, bf16[112,256]{1,0:T(8,128)(2,1)S(1)}, bf16[48,25...) custom-call(bf16[256,256]{1,0:T(8,128)(2,1)S(1)} %get-tuple-element.49.hidden, ...), custom_call_target="tpu_custom_call" | custom-call | flops 301989888 | bytes 2164736 | tf_op jit(solution)/shard_map/third/pallas_call | solution.py:501
  21.6 0.3 %collective-permute-start.6 = (bf16[112,256]{1,0:T(8,128)(2,1)S(1)}, bf16[112,256]{1,0:T(8,128)(2,1)S(1)}, u32[]{:S(2)}, u32[]{:S(2)}) collective-permute-start(bf16[112,256]{1,0:T(8,128)(2,1)S(1)} %get-tuple-element.63), channel_id=1, source_target_pairs={{0,4},{4,0},{8,12},{12,8},{1,5},{5,1},{9,13},{13,9},{2,6},{6,2},{1... | collective-permute-start | bytes 172040 | tf_op jit(solution)/shard_map/ppermute | solution.py:516
  22.0 2.0 %collective-permute-start.7 = (bf16[112,256]{1,0:T(8,128)(2,1)S(1)}, bf16[112,256]{1,0:T(8,128)(2,1)S(1)}, u32[]{:S(2)}, u32[]{:S(2)}) collective-permute-start(bf16[112,256]{1,0:T(8,128)(2,1)S(1)} %get-tuple-element.64), channel_id=1, source_target_pairs={{0,12},{4,8},{8,4},{12,0},{1,13},{5,9},{9,5},{13,1},{2,14},{6,10},... | collective-permute-start | bytes 172040 | tf_op jit(solution)/shard_map/ppermute | solution.py:516
  24.0 1.2 %collective-permute-start.8 = (bf16[48,256]{1,0:T(8,128)(2,1)S(1)}, bf16[48,256]{1,0:T(8,128)(2,1)S(1)}, u32[]{:S(2)}, u32[]{:S(2)}) collective-permute-start(bf16[48,256]{1,0:T(8,128)(2,1)S(1)} %get-tuple-element.67.rest_0_), channel_id=1, source_target_pairs={{0,8},{4,12},{8,0},{12,4},{1,9},{5,13},{9,1},{13,5},{2,10},{6,14},... | collective-permute-start | bytes 73736 | tf_op jit(solution)/shard_map/ppermute | solution.py:516
  25.2 0.5 %branch.1 = (bf16[256,256]{1,0:T(8,128)(2,1)S(1)}, f32[8,128]{1,0:T(8,128)S(1)}) custom-call(bf16[384,256]{1,0:T(8,128)(2,1)S(1)} %get-tuple-element.59.active, bf16[9,256,256]{2,1,0:T(8,128)(2,1)S(1)} %bitcast.14), custom_call_target="tpu_custom_call" | custom-call | flops 301989888 | bytes 1376256 | tf_op jit(solution)/shard_map/branch/pallas_call | solution.py:501
  25.7 0.7 %copy.17 = bf16[1,4,64,256]{3,2,1,0:T(8,128)(2,1)} copy(bf16[1,4,64,256]{3,2,1,0:T(8,128)(2,1)S(1)} %bitcast.12) | data formatting | bytes 262144
  26.3 2.5 %collective-permute-done.8.rest_2_ = bf16[48,256]{1,0:T(8,128)(2,1)S(1)} collective-permute-done((bf16[48,256]{1,0:T(8,128)(2,1)S(1)}, bf16[48,256]{1,0:T(8,128)(2,1)S(1)}, u32[]{:S(2)}, u32[]{:S(2)}) %collective-permute-start.8) | collective-permute-done | bytes 24608 | tf_op jit(solution)/shard_map/ppermute | solution.py:516
  28.8 0.0 collective-permute-done.7.grad_three.rest_3_
  28.8 1.6 %collective-permute-start.10 = (f32[8,256]{1,0:T(8,128)S(1)}, f32[8,256]{1,0:T(8,128)S(1)}, u32[]{:S(2)}, u32[]{:S(2)}) collective-permute-start(f32[8,256]{1,0:T(8,128)S(1)} %pairs.1.rest_0_), channel_id=1, source_target_pairs={{0,2},{1,3},{2,0},{3,1},{4,6},{5,7},{6,4},{7,5},{8,10},{9,11},{10,... | collective-permute-start | bytes 24584 | tf_op jit(solution)/shard_map/ppermute | solution.py:516
  30.4 0.6 %collective-permute-start.9 = (f32[8,256]{1,0:T(8,128)S(1)}, f32[8,256]{1,0:T(8,128)S(1)}, u32[]{:S(2)}, u32[]{:S(2)}) collective-permute-start(f32[8,256]{1,0:T(8,128)S(1)} %pairs.1.rest_0_), channel_id=1, source_target_pairs={{0,1},{1,0},{2,3},{3,2},{4,5},{5,4},{6,7},{7,6},{8,9},{9,8},{10,11... | collective-permute-start | bytes 24584 | tf_op jit(solution)/shard_map/ppermute | solution.py:516
  31.0 0.9 %fourth.1 = bf16[256,256]{1,0:T(8,128)(2,1)S(1)} custom-call(f32[8,128]{1,0:T(8,128)S(1)} %get-tuple-element.61.token, f32[256,256]{1,0:T(8,128)S(1)} %get-tuple-element.62.grad_norm, bf16[112,256]{1,0:T(8,128)(2,1)S(1)} %collective-permute-done.6.grad_one.rest_1_, bf16[112,256]{1,0:T(8,128)(2,1)S(1)} %collective-permute-done.7.grad_three.rest_3_, ...), custom_call_target="tpu_custom_call" | custom-call | flops 301989888 | bytes 2347008 | tf_op jit(solution)/shard_map/fourth/pallas_call | solution.py:501
  31.9 0.7 %copy.18 = bf16[1,4,64,256]{3,2,1,0:T(8,128)(2,1)} copy(bf16[1,4,64,256]{3,2,1,0:T(8,128)(2,1)S(1)} %bitcast.11) | data formatting | bytes 262144
  32.6 0.8 %collective-permute-done.11.rest_3_ = f32[8,256]{1,0:T(8,128)S(1)} collective-permute-done((f32[8,256]{1,0:T(8,128)S(1)}, f32[8,256]{1,0:T(8,128)S(1)}, u32[]{:S(2)}, u32[]{:S(2)}) %collective-permute-start.11) | collective-permute-done | bytes 8224 | tf_op jit(solution)/shard_map/ppermute | solution.py:516
  33.4 1.1 %weight.1 = (f32[256,512]{1,0:T(8,128)}, f32[1,512]{1,0:T(1,128)}) custom-call(f32[8,256]{1,0:T(8,128)S(1)} %pairs.1.rest_0_, f32[8,256]{1,0:T(8,128)S(1)} %collective-permute-done.9.rest_1_, f32[8,256]{1,0:T(8,128)S(1)} %collective-permute-done.10.rest_2_, f32[8,256]{1,0:T(8,128)S(1)} %collective-permute-done.11.rest_3_), custom_call_target="tpu_custom_call" | custom-call | flops 1000 | bytes 32768 | tf_op jit(solution)/shard_map/weight/pallas_call | solution.py:501
  (6 shorter events, 0.0 us)
Async XLA Ops:
  2.0 10.1 %collective-permute-start = (bf16[144,256]{1,0:T(8,128)(2,1)S(1)}, bf16[144,256]{1,0:T(8,128)(2,1)S(1)}, u32[]{:S(2)}, u32[]{:S(2)}) collective-permute-start(bf16[144,256]{1,0:T(8,128)(2,1)S(1)} %get-tuple-element.38), channel_id=1, source_target_pairs={{0,4},{4,0},{8,12},{12,8},{1,5},{5,1},{9,13},{13,9},{2,6},{6,2},{1... | collective-permute-start | bytes 221192 | tf_op jit(solution)/shard_map/ppermute | solution.py:516
  5.1 7.0 %collective-permute-start.1 = (bf16[144,256]{1,0:T(8,128)(2,1)S(1)}, bf16[144,256]{1,0:T(8,128)(2,1)S(1)}, u32[]{:S(2)}, u32[]{:S(2)}) collective-permute-start(bf16[144,256]{1,0:T(8,128)(2,1)S(1)} %get-tuple-element.39), channel_id=1, source_target_pairs={{0,12},{4,8},{8,4},{12,0},{1,13},{5,9},{9,5},{13,1},{2,14},{6,10},... | collective-permute-start | bytes 221192 | tf_op jit(solution)/shard_map/ppermute | solution.py:516
  7.6 4.5 %collective-permute-start.2 = (bf16[16,256]{1,0:T(8,128)(2,1)S(1)}, bf16[16,256]{1,0:T(8,128)(2,1)S(1)}, u32[]{:S(2)}, u32[]{:S(2)}) collective-permute-start(bf16[16,256]{1,0:T(8,128)(2,1)S(1)} %get-tuple-element.48.rest_0_), channel_id=1, source_target_pairs={{0,8},{4,12},{8,0},{12,4},{1,9},{5,13},{9,1},{13,5},{2,10},{6,14},... | collective-permute-start | bytes 24584 | tf_op jit(solution)/shard_map/ppermute | solution.py:516
  10.8 5.8 %copy-start = (bf16[3,3,256,256]{3,2,1,0:T(8,128)(2,1)S(1)}, bf16[3,3,256,256]{3,2,1,0:T(8,128)(2,1)}, u32[]{:S(2)}) copy-start(bf16[3,3,256,256]{3,2,1,0:T(8,128)(2,1)} %param.20) | copy-start | bytes 3538948
  13.1 7.6 %collective-permute-start.3 = (bf16[80,256]{1,0:T(8,128)(2,1)S(1)}, bf16[80,256]{1,0:T(8,128)(2,1)S(1)}, u32[]{:S(2)}, u32[]{:S(2)}) collective-permute-start(bf16[80,256]{1,0:T(8,128)(2,1)S(1)} %get-tuple-element.50), channel_id=1, source_target_pairs={{0,4},{4,0},{8,12},{12,8},{1,5},{5,1},{9,13},{13,9},{2,6},{6,2},{1... | collective-permute-start | bytes 122888 | tf_op jit(solution)/shard_map/ppermute | solution.py:516
  13.8 6.8 %collective-permute-start.4 = (bf16[80,256]{1,0:T(8,128)(2,1)S(1)}, bf16[80,256]{1,0:T(8,128)(2,1)S(1)}, u32[]{:S(2)}, u32[]{:S(2)}) collective-permute-start(bf16[80,256]{1,0:T(8,128)(2,1)S(1)} %get-tuple-element.51), channel_id=1, source_target_pairs={{0,12},{4,8},{8,4},{12,0},{1,13},{5,9},{9,5},{13,1},{2,14},{6,10},... | collective-permute-start | bytes 122888 | tf_op jit(solution)/shard_map/ppermute | solution.py:516
  16.1 4.5 %collective-permute-start.5 = (bf16[16,256]{1,0:T(8,128)(2,1)S(1)}, bf16[16,256]{1,0:T(8,128)(2,1)S(1)}, u32[]{:S(2)}, u32[]{:S(2)}) collective-permute-start(bf16[16,256]{1,0:T(8,128)(2,1)S(1)} %get-tuple-element.58.rest_0_), channel_id=1, source_target_pairs={{0,8},{4,12},{8,0},{12,4},{1,9},{5,13},{9,1},{13,5},{2,10},{6,14},... | collective-permute-start | bytes 24584 | tf_op jit(solution)/shard_map/ppermute | solution.py:516
  21.6 7.2 %collective-permute-start.6 = (bf16[112,256]{1,0:T(8,128)(2,1)S(1)}, bf16[112,256]{1,0:T(8,128)(2,1)S(1)}, u32[]{:S(2)}, u32[]{:S(2)}) collective-permute-start(bf16[112,256]{1,0:T(8,128)(2,1)S(1)} %get-tuple-element.63), channel_id=1, source_target_pairs={{0,4},{4,0},{8,12},{12,8},{1,5},{5,1},{9,13},{13,9},{2,6},{6,2},{1... | collective-permute-start | bytes 172040 | tf_op jit(solution)/shard_map/ppermute | solution.py:516
  22.0 6.8 %collective-permute-start.7 = (bf16[112,256]{1,0:T(8,128)(2,1)S(1)}, bf16[112,256]{1,0:T(8,128)(2,1)S(1)}, u32[]{:S(2)}, u32[]{:S(2)}) collective-permute-start(bf16[112,256]{1,0:T(8,128)(2,1)S(1)} %get-tuple-element.64), channel_id=1, source_target_pairs={{0,12},{4,8},{8,4},{12,0},{1,13},{5,9},{9,5},{13,1},{2,14},{6,10},... | collective-permute-start | bytes 172040 | tf_op jit(solution)/shard_map/ppermute | solution.py:516
  24.0 4.8 %collective-permute-start.8 = (bf16[48,256]{1,0:T(8,128)(2,1)S(1)}, bf16[48,256]{1,0:T(8,128)(2,1)S(1)}, u32[]{:S(2)}, u32[]{:S(2)}) collective-permute-start(bf16[48,256]{1,0:T(8,128)(2,1)S(1)} %get-tuple-element.67.rest_0_), channel_id=1, source_target_pairs={{0,8},{4,12},{8,0},{12,4},{1,9},{5,13},{9,1},{13,5},{2,10},{6,14},... | collective-permute-start | bytes 73736 | tf_op jit(solution)/shard_map/ppermute | solution.py:516
  28.8 3.8 %collective-permute-start.10 = (f32[8,256]{1,0:T(8,128)S(1)}, f32[8,256]{1,0:T(8,128)S(1)}, u32[]{:S(2)}, u32[]{:S(2)}) collective-permute-start(f32[8,256]{1,0:T(8,128)S(1)} %pairs.1.rest_0_), channel_id=1, source_target_pairs={{0,2},{1,3},{2,0},{3,1},{4,6},{5,7},{6,4},{7,5},{8,10},{9,11},{10,... | collective-permute-start | bytes 24584 | tf_op jit(solution)/shard_map/ppermute | solution.py:516
  30.4 3.1 %collective-permute-start.11 = (f32[8,256]{1,0:T(8,128)S(1)}, f32[8,256]{1,0:T(8,128)S(1)}, u32[]{:S(2)}, u32[]{:S(2)}) collective-permute-start(f32[8,256]{1,0:T(8,128)S(1)} %pairs.1.rest_0_), channel_id=1, source_target_pairs={{0,3},{1,2},{2,1},{3,0},{4,7},{5,6},{6,5},{7,4},{8,11},{9,10},{10,... | collective-permute-start | bytes 24584 | tf_op jit(solution)/shard_map/ppermute | solution.py:516
  30.4 3.1 %collective-permute-start.9 = (f32[8,256]{1,0:T(8,128)S(1)}, f32[8,256]{1,0:T(8,128)S(1)}, u32[]{:S(2)}, u32[]{:S(2)}) collective-permute-start(f32[8,256]{1,0:T(8,128)S(1)} %pairs.1.rest_0_), channel_id=1, source_target_pairs={{0,1},{1,0},{2,3},{3,2},{4,5},{5,4},{6,7},{7,6},{8,9},{9,8},{10,11... | collective-permute-start | bytes 24584 | tf_op jit(solution)/shard_map/ppermute | solution.py:516

commit v8 on v7

--- a/solution.py
+++ b/solution.py
@@ -104,6 +104,26 @@
     if flipped:
         parts = parts[::-1]
     return parts[1] + (shifted(parts[0], cols, 1) + shifted(parts[2], cols, -1))
+
+
+def scattered(values, kernel_ref, cols):
+    rows = values.shape[0] // cols
+    parts = []
+    for j in range(3):
+        products = [
+            lax.dot_general(
+                values, kernel_ref[3 * i + j], (((1,), (1,)), ((), ())), preferred_element_type=F32
+            )
+            for i in range(3)
+        ]
+        lines = []
+        for line in range(rows + 2):
+            terms_of = [
+                products[i][(line - i) * cols : (line - i + 1) * cols] for i in range(3) if 0 <= line - i < rows
+            ]
+            lines.append(tree_sum(terms_of))
+        parts.append(jnp.concatenate(lines, axis=0))
+    return parts[1] + (shifted(parts[2], cols, 1) + shifted(parts[0], cols, -1))
 
 
 def shifted(values, cols, step):
@@ -349,7 +369,7 @@
 ):
     cells, cols, channels, tiles = dims
     place = standing(tiles)
-    stat_refs, (active, grad_norm, stat, out_one, out_two, out_three, padded) = rest[:n_stats], rest[n_stats:]
+    stat_refs, (active, grad_norm, stat, out_one, out_two, out_three) = rest[:n_stats], rest[n_stats:]
     count = cells * (channels // GN_GROUPS)
     stats = stat_list(stat_refs, (0, cols, 0, cols), tiles)
     mean, inverse = joint_moments(stats, count)
@@ -369,11 +389,7 @@
     grad_pre = grad_active[...] * (gate * (1.0 + pre * (1.0 - gate)))
     grad = grad_pre * factor
     grad_norm[...] = grad
-    edge = jnp.zeros((2 * cols, channels), BF16)
-    padded[0 : 2 * cols] = edge
-    padded[2 * cols : 2 * cols + cells] = (grad * inverse).astype(BF16)
-    padded[2 * cols + cells :] = edge
-    base = conv(padded, weights, cells + 2 * cols, cols, True)
+    base = scattered((grad * inverse).astype(BF16), weights, cols)
     _, pre, gate = pieces(above)
     active[0:cols] = jnp.where(place[0] > 0, pre * gate, 0.0).astype(BF16)
     _, pre, gate = pieces(below)
@@ -636,8 +652,7 @@
         functools.partial(third_kernel, dims, len(stats)),
         (shape((cells + 2 * cols, channels), BF16), wide, block, mail_halo, mail, mail_halo),
         (hidden, hidden_one, hidden_three, grad_active, adaptive_bias, weights_first, factors, matrix, *stats),
-        (pltpu.VMEM((cells + 4 * cols, channels), BF16),),
-        conv_flops,
+        flops=conv_flops,
         name="third",
     )
     grad_one, grad_three, stats = exchange(one, two, three)

time: 34.7 us -> 34.5 us (level)
  no operation moved by 1% of the time
where the time goes in v8:
time: 34.5 us; the launch traced here: 34.3 us
  starting transfers between devices  15 us (43%)
  Pallas kernels  9.76 us (28%)
  waiting for transfers between devices  6.25 us (18%)
  between operations  2.01 us (6%)
  local copies, waits for them, and re-layouts  1.32 us (4%)
    ppermute x12, starting transfers between devices, swap(): return lax.ppermute(values, axis, [(i, i ^ distance) for i in range(size)])  15 us
    pallas_call x10, Pallas kernels, call(): pl.pallas_call(kernel, out_shape=out_shapes, in_specs=[pl.BlockSpec(memor...  9.76 us
    ppermute x12, waiting for transfers between devices, swap(): return lax.ppermute(values, axis, [(i, i ^ distance) for i in range(size)])  6.25 us
    unnamed x4, local copies, waits for them, and re-layouts  1.32 us
  transfers between devices with their start and end apart: 12, of which 4 were waited for; matrix products, arithmetic and copies ran while one was open for 4% of the time, Pallas kernels for 16%

profile of v8, /device:TPU:0, one launch (start us, length us, event | category | flops | bytes accessed | tf_op | source)
XLA Modules:
  0.0 34.3 jit_solution(12442779198962965257)
XLA Ops:
  0.6 1.4 %first.1 = (bf16[256,256]{1,0:T(8,128)(2,1)S(1)}, bf16[256,256]{1,0:T(8,128)(2,1)S(1)}, f32[1,256]{1,0:T(1,128)S(1)}, f32[1,256]{1,0:T(1,128)S(1)}, bf16[1000,25...) custom-call(bf16[256,256]{1,0:T(8,128)(2,1)} %bitcast.16, ...), custom_call_target="tpu_custom_call" | custom-call | flops 1000 | bytes 1170432 | tf_op jit(solution)/shard_map/first/pallas_call | solution.py:517
  2.0 3.1 %collective-permute-start = (bf16[144,256]{1,0:T(8,128)(2,1)S(1)}, bf16[144,256]{1,0:T(8,128)(2,1)S(1)}, u32[]{:S(2)}, u32[]{:S(2)}) collective-permute-start(bf16[144,256]{1,0:T(8,128)(2,1)S(1)} %get-tuple-element.38), channel_id=1, source_target_pairs={{0,4},{4,0},{8,12},{12,8},{1,5},{5,1},{9,13},{13,9},{2,6},{6,2},{1... | collective-permute-start | bytes 221192 | tf_op jit(solution)/shard_map/ppermute | solution.py:532
  5.1 2.5 %collective-permute-start.1 = (bf16[144,256]{1,0:T(8,128)(2,1)S(1)}, bf16[144,256]{1,0:T(8,128)(2,1)S(1)}, u32[]{:S(2)}, u32[]{:S(2)}) collective-permute-start(bf16[144,256]{1,0:T(8,128)(2,1)S(1)} %get-tuple-element.39), channel_id=1, source_target_pairs={{0,12},{4,8},{8,4},{12,0},{1,13},{5,9},{9,5},{13,1},{2,14},{6,10},... | collective-permute-start | bytes 221192 | tf_op jit(solution)/shard_map/ppermute | solution.py:532
  7.6 0.1 collective-permute-start.2
  9.0 1.8 %turn.1 = (bf16[9,256,256]{2,1,0:T(8,128)(2,1)S(1)}, f32[1,512]{1,0:T(1,128)S(1)}, f32[8,256]{1,0:T(8,128)S(1)}, f32[9,256,128]{2,1,0:T(8,128)S(1)}) custom-call(s32[1]{0:T(128)S(6)} %copy.19.step, s32[1]{0:T(128)S(6)} %copy.20.label, bf16[1000,256]{1,0:T(8,128)(2,1)S(1)} %get-tuple-element.40.table, bf16[256,256]{1,0:T(8,128)(2,1)S(1)} %get-tuple-element.41.time_weight, ...), custom_call_target="tpu_custom_call" | custom-call | flops 301989888 | bytes 2087944 | tf_op jit(solution)/shard_map/turn/pallas_call | solution.py:517
  10.8 0.0 copy-start
  10.8 1.3 %collective-permute-done.2.rest_2_ = bf16[16,256]{1,0:T(8,128)(2,1)S(1)} collective-permute-done((bf16[16,256]{1,0:T(8,128)(2,1)S(1)}, bf16[16,256]{1,0:T(8,128)(2,1)S(1)}, u32[]{:S(2)}, u32[]{:S(2)}) %collective-permute-start.2) | collective-permute-done | bytes 8224 | tf_op jit(solution)/shard_map/ppermute | solution.py:532
  12.2 0.0 collective-permute-done.one.rest_1_
  12.2 0.0 collective-permute-done.1.three.rest_3_
  12.2 0.9 %second.1 = (bf16[256,256]{1,0:T(8,128)(2,1)S(1)}, f32[8,256]{1,0:T(8,128)S(1)}, bf16[80,256]{1,0:T(8,128)(2,1)S(1)}, bf16[16,256]{1,0:T(8,128)(2,1)S(1)}, bf16[80,256]{1,0:T(8,128)(2,1)S(1)}) custom-call(bf16[256,256]{1,0:T(8,128)(2,1)S(1)} %get-tuple-element.37.images, bf16[144,256]{1,0:T(8,128)(2,1)S(1)} %collective-permute-done.one.rest_1_, ...), custom_call_target="tpu_custom_call" | custom-call | flops 301989888 | bytes 1632256 | tf_op jit(solution)/shard_map/second/pallas_call | solution.py:517
  13.1 0.7 %collective-permute-start.3 = (bf16[80,256]{1,0:T(8,128)(2,1)S(1)}, bf16[80,256]{1,0:T(8,128)(2,1)S(1)}, u32[]{:S(2)}, u32[]{:S(2)}) collective-permute-start(bf16[80,256]{1,0:T(8,128)(2,1)S(1)} %get-tuple-element.50), channel_id=1, source_target_pairs={{0,4},{4,0},{8,12},{12,8},{1,5},{5,1},{9,13},{13,9},{2,6},{6,2},{1... | collective-permute-start | bytes 122888 | tf_op jit(solution)/shard_map/ppermute | solution.py:532
  13.8 2.3 %collective-permute-start.4 = (bf16[80,256]{1,0:T(8,128)(2,1)S(1)}, bf16[80,256]{1,0:T(8,128)(2,1)S(1)}, u32[]{:S(2)}, u32[]{:S(2)}) collective-permute-start(bf16[80,256]{1,0:T(8,128)(2,1)S(1)} %get-tuple-element.51), channel_id=1, source_target_pairs={{0,12},{4,8},{8,4},{12,0},{1,13},{5,9},{9,5},{13,1},{2,14},{6,10},... | collective-permute-start | bytes 122888 | tf_op jit(solution)/shard_map/ppermute | solution.py:532
  16.1 0.5 %collective-permute-start.5 = (bf16[16,256]{1,0:T(8,128)(2,1)S(1)}, bf16[16,256]{1,0:T(8,128)(2,1)S(1)}, u32[]{:S(2)}, u32[]{:S(2)}) collective-permute-start(bf16[16,256]{1,0:T(8,128)(2,1)S(1)} %get-tuple-element.58.rest_0_), channel_id=1, source_target_pairs={{0,8},{4,12},{8,0},{12,4},{1,9},{5,13},{9,1},{13,5},{2,10},{6,14},... | collective-permute-start | bytes 24584 | tf_op jit(solution)/shard_map/ppermute | solution.py:532
  16.6 0.5 %grad.1.grad_active = f32[256,256]{1,0:T(8,128)S(1)} custom-call(bf16[256,256]{1,0:T(8,128)(2,1)S(1)} %get-tuple-element.52.cotangent, bf16[144,256]{1,0:T(8,128)(2,1)S(1)} %collective-permute-done.one.rest_1_, bf16[144,256]{1,0:T(8,128)(2,1)S(1)} %collective-permute-done.1.three.rest_3_, bf16[9,256,256]{2,1,0:T(8,128)(2,1)S(1)} %bitcast.13), custom_call_target="tpu_custom_call" | custom-call | flops 301989888 | bytes 1458176 | tf_op jit(solution)/shard_map/grad/pallas_call | solution.py:517
  17.1 1.9 %cross.1 = (f32[256,256]{1,0:T(8,128)S(1)}, bf16[2,384,256]{2,1,0:T(8,128)(2,1)S(1)}, bf16[32,256]{1,0:T(8,128)(2,1)S(1)}) custom-call(bf16[256,256]{1,0:T(8,128)(2,1)S(1)} %get-tuple-element.37.images, bf16[144,256]{1,0:T(8,128)(2,1)S(1)} %collective-permute-done.one.rest_1_, bf16[144,256]{1,0:T(8,128)(2,1)S(1)} %collective-permute-done.1.three.rest_3_, ...), custom_call_target="tpu_custom_call" | custom-call | flops 301989888 | bytes 2779136 | tf_op jit(solution)/shard_map/cross/pallas_call | solution.py:517
  19.0 1.6 %collective-permute-done.5.rest_2_ = bf16[16,256]{1,0:T(8,128)(2,1)S(1)} collective-permute-done((bf16[16,256]{1,0:T(8,128)(2,1)S(1)}, bf16[16,256]{1,0:T(8,128)(2,1)S(1)}, u32[]{:S(2)}, u32[]{:S(2)}) %collective-permute-start.5) | collective-permute-done | bytes 8224 | tf_op jit(solution)/shard_map/ppermute | solution.py:532
  20.6 0.0 collective-permute-done.3.one.rest_1_
  20.6 0.0 collective-permute-done.4.three.rest_3_
  20.6 0.8 %third.1 = (bf16[384,256]{1,0:T(8,128)(2,1)S(1)}, f32[256,256]{1,0:T(8,128)S(1)}, f32[8,256]{1,0:T(8,128)S(1)}, bf16[112,256]{1,0:T(8,128)(2,1)S(1)}, bf16[48,25...) custom-call(bf16[256,256]{1,0:T(8,128)(2,1)S(1)} %get-tuple-element.49.hidden, ...), custom_call_target="tpu_custom_call" | custom-call | flops 301989888 | bytes 2164736 | tf_op jit(solution)/shard_map/third/pallas_call | solution.py:517
  21.5 0.4 %collective-permute-start.6 = (bf16[112,256]{1,0:T(8,128)(2,1)S(1)}, bf16[112,256]{1,0:T(8,128)(2,1)S(1)}, u32[]{:S(2)}, u32[]{:S(2)}) collective-permute-start(bf16[112,256]{1,0:T(8,128)(2,1)S(1)} %get-tuple-element.63), channel_id=1, source_target_pairs={{0,4},{4,0},{8,12},{12,8},{1,5},{5,1},{9,13},{13,9},{2,6},{6,2},{1... | collective-permute-start | bytes 172040 | tf_op jit(solution)/shard_map/ppermute | solution.py:532
  21.8 2.0 %collective-permute-start.7 = (bf16[112,256]{1,0:T(8,128)(2,1)S(1)}, bf16[112,256]{1,0:T(8,128)(2,1)S(1)}, u32[]{:S(2)}, u32[]{:S(2)}) collective-permute-start(bf16[112,256]{1,0:T(8,128)(2,1)S(1)} %get-tuple-element.64), channel_id=1, source_target_pairs={{0,12},{4,8},{8,4},{12,0},{1,13},{5,9},{9,5},{13,1},{2,14},{6,10},... | collective-permute-start | bytes 172040 | tf_op jit(solution)/shard_map/ppermute | solution.py:532
  23.8 1.2 %collective-permute-start.8 = (bf16[48,256]{1,0:T(8,128)(2,1)S(1)}, bf16[48,256]{1,0:T(8,128)(2,1)S(1)}, u32[]{:S(2)}, u32[]{:S(2)}) collective-permute-start(bf16[48,256]{1,0:T(8,128)(2,1)S(1)} %get-tuple-element.67.rest_0_), channel_id=1, source_target_pairs={{0,8},{4,12},{8,0},{12,4},{1,9},{5,13},{9,1},{13,5},{2,10},{6,14},... | collective-permute-start | bytes 73736 | tf_op jit(solution)/shard_map/ppermute | solution.py:532
  25.0 0.5 %branch.1 = (bf16[256,256]{1,0:T(8,128)(2,1)S(1)}, f32[8,128]{1,0:T(8,128)S(1)}) custom-call(bf16[384,256]{1,0:T(8,128)(2,1)S(1)} %get-tuple-element.59.active, bf16[9,256,256]{2,1,0:T(8,128)(2,1)S(1)} %bitcast.14), custom_call_target="tpu_custom_call" | custom-call | flops 301989888 | bytes 1376256 | tf_op jit(solution)/shard_map/branch/pallas_call | solution.py:517
  25.5 0.7 %copy.17 = bf16[1,4,64,256]{3,2,1,0:T(8,128)(2,1)} copy(bf16[1,4,64,256]{3,2,1,0:T(8,128)(2,1)S(1)} %bitcast.12) | data formatting | bytes 262144
  26.2 2.5 %collective-permute-done.8.rest_2_ = bf16[48,256]{1,0:T(8,128)(2,1)S(1)} collective-permute-done((bf16[48,256]{1,0:T(8,128)(2,1)S(1)}, bf16[48,256]{1,0:T(8,128)(2,1)S(1)}, u32[]{:S(2)}, u32[]{:S(2)}) %collective-permute-start.8) | collective-permute-done | bytes 24608 | tf_op jit(solution)/shard_map/ppermute | solution.py:532
  28.6 0.0 collective-permute-done.6.grad_one.rest_1_
  28.7 1.6 %collective-permute-start.10 = (f32[8,256]{1,0:T(8,128)S(1)}, f32[8,256]{1,0:T(8,128)S(1)}, u32[]{:S(2)}, u32[]{:S(2)}) collective-permute-start(f32[8,256]{1,0:T(8,128)S(1)} %pairs.1.rest_0_), channel_id=1, source_target_pairs={{0,2},{1,3},{2,0},{3,1},{4,6},{5,7},{6,4},{7,5},{8,10},{9,11},{10,... | collective-permute-start | bytes 24584 | tf_op jit(solution)/shard_map/ppermute | solution.py:532
  30.2 0.7 %collective-permute-start.9 = (f32[8,256]{1,0:T(8,128)S(1)}, f32[8,256]{1,0:T(8,128)S(1)}, u32[]{:S(2)}, u32[]{:S(2)}) collective-permute-start(f32[8,256]{1,0:T(8,128)S(1)} %pairs.1.rest_0_), channel_id=1, source_target_pairs={{0,1},{1,0},{2,3},{3,2},{4,5},{5,4},{6,7},{7,6},{8,9},{9,8},{10,11... | collective-permute-start | bytes 24584 | tf_op jit(solution)/shard_map/ppermute | solution.py:532
  30.9 0.9 %fourth.1 = bf16[256,256]{1,0:T(8,128)(2,1)S(1)} custom-call(f32[8,128]{1,0:T(8,128)S(1)} %get-tuple-element.61.token, f32[256,256]{1,0:T(8,128)S(1)} %get-tuple-element.62.grad_norm, bf16[112,256]{1,0:T(8,128)(2,1)S(1)} %collective-permute-done.6.grad_one.rest_1_, bf16[112,256]{1,0:T(8,128)(2,1)S(1)} %collective-permute-done.7.grad_three.rest_3_, ...), custom_call_target="tpu_custom_call" | custom-call | flops 301989888 | bytes 2347008 | tf_op jit(solution)/shard_map/fourth/pallas_call | solution.py:517
  31.8 0.7 %copy.18 = bf16[1,4,64,256]{3,2,1,0:T(8,128)(2,1)} copy(bf16[1,4,64,256]{3,2,1,0:T(8,128)(2,1)S(1)} %bitcast.11) | data formatting | bytes 262144
  32.5 0.8 %collective-permute-done.11.rest_3_ = f32[8,256]{1,0:T(8,128)S(1)} collective-permute-done((f32[8,256]{1,0:T(8,128)S(1)}, f32[8,256]{1,0:T(8,128)S(1)}, u32[]{:S(2)}, u32[]{:S(2)}) %collective-permute-start.11) | collective-permute-done | bytes 8224 | tf_op jit(solution)/shard_map/ppermute | solution.py:532
  33.3 1.1 %weight.1 = (f32[256,512]{1,0:T(8,128)}, f32[1,512]{1,0:T(1,128)}) custom-call(f32[8,256]{1,0:T(8,128)S(1)} %pairs.1.rest_0_, f32[8,256]{1,0:T(8,128)S(1)} %collective-permute-done.9.rest_1_, f32[8,256]{1,0:T(8,128)S(1)} %collective-permute-done.10.rest_2_, f32[8,256]{1,0:T(8,128)S(1)} %collective-permute-done.11.rest_3_), custom_call_target="tpu_custom_call" | custom-call | flops 1000 | bytes 32768 | tf_op jit(solution)/shard_map/weight/pallas_call | solution.py:517
  (6 shorter events, 0.0 us)
Async XLA Ops:
  2.0 10.1 %collective-permute-start = (bf16[144,256]{1,0:T(8,128)(2,1)S(1)}, bf16[144,256]{1,0:T(8,128)(2,1)S(1)}, u32[]{:S(2)}, u32[]{:S(2)}) collective-permute-start(bf16[144,256]{1,0:T(8,128)(2,1)S(1)} %get-tuple-element.38), channel_id=1, source_target_pairs={{0,4},{4,0},{8,12},{12,8},{1,5},{5,1},{9,13},{13,9},{2,6},{6,2},{1... | collective-permute-start | bytes 221192 | tf_op jit(solution)/shard_map/ppermute | solution.py:532
  5.1 7.0 %collective-permute-start.1 = (bf16[144,256]{1,0:T(8,128)(2,1)S(1)}, bf16[144,256]{1,0:T(8,128)(2,1)S(1)}, u32[]{:S(2)}, u32[]{:S(2)}) collective-permute-start(bf16[144,256]{1,0:T(8,128)(2,1)S(1)} %get-tuple-element.39), channel_id=1, source_target_pairs={{0,12},{4,8},{8,4},{12,0},{1,13},{5,9},{9,5},{13,1},{2,14},{6,10},... | collective-permute-start | bytes 221192 | tf_op jit(solution)/shard_map/ppermute | solution.py:532
  7.6 4.5 %collective-permute-start.2 = (bf16[16,256]{1,0:T(8,128)(2,1)S(1)}, bf16[16,256]{1,0:T(8,128)(2,1)S(1)}, u32[]{:S(2)}, u32[]{:S(2)}) collective-permute-start(bf16[16,256]{1,0:T(8,128)(2,1)S(1)} %get-tuple-element.48.rest_0_), channel_id=1, source_target_pairs={{0,8},{4,12},{8,0},{12,4},{1,9},{5,13},{9,1},{13,5},{2,10},{6,14},... | collective-permute-start | bytes 24584 | tf_op jit(solution)/shard_map/ppermute | solution.py:532
  10.8 5.8 %copy-start = (bf16[3,3,256,256]{3,2,1,0:T(8,128)(2,1)S(1)}, bf16[3,3,256,256]{3,2,1,0:T(8,128)(2,1)}, u32[]{:S(2)}) copy-start(bf16[3,3,256,256]{3,2,1,0:T(8,128)(2,1)} %param.20) | copy-start | bytes 3538948
  13.1 7.6 %collective-permute-start.3 = (bf16[80,256]{1,0:T(8,128)(2,1)S(1)}, bf16[80,256]{1,0:T(8,128)(2,1)S(1)}, u32[]{:S(2)}, u32[]{:S(2)}) collective-permute-start(bf16[80,256]{1,0:T(8,128)(2,1)S(1)} %get-tuple-element.50), channel_id=1, source_target_pairs={{0,4},{4,0},{8,12},{12,8},{1,5},{5,1},{9,13},{13,9},{2,6},{6,2},{1... | collective-permute-start | bytes 122888 | tf_op jit(solution)/shard_map/ppermute | solution.py:532
  13.8 6.8 %collective-permute-start.4 = (bf16[80,256]{1,0:T(8,128)(2,1)S(1)}, bf16[80,256]{1,0:T(8,128)(2,1)S(1)}, u32[]{:S(2)}, u32[]{:S(2)}) collective-permute-start(bf16[80,256]{1,0:T(8,128)(2,1)S(1)} %get-tuple-element.51), channel_id=1, source_target_pairs={{0,12},{4,8},{8,4},{12,0},{1,13},{5,9},{9,5},{13,1},{2,14},{6,10},... | collective-permute-start | bytes 122888 | tf_op jit(solution)/shard_map/ppermute | solution.py:532
  16.1 4.5 %collective-permute-start.5 = (bf16[16,256]{1,0:T(8,128)(2,1)S(1)}, bf16[16,256]{1,0:T(8,128)(2,1)S(1)}, u32[]{:S(2)}, u32[]{:S(2)}) collective-permute-start(bf16[16,256]{1,0:T(8,128)(2,1)S(1)} %get-tuple-element.58.rest_0_), channel_id=1, source_target_pairs={{0,8},{4,12},{8,0},{12,4},{1,9},{5,13},{9,1},{13,5},{2,10},{6,14},... | collective-permute-start | bytes 24584 | tf_op jit(solution)/shard_map/ppermute | solution.py:532
  21.5 7.2 %collective-permute-start.6 = (bf16[112,256]{1,0:T(8,128)(2,1)S(1)}, bf16[112,256]{1,0:T(8,128)(2,1)S(1)}, u32[]{:S(2)}, u32[]{:S(2)}) collective-permute-start(bf16[112,256]{1,0:T(8,128)(2,1)S(1)} %get-tuple-element.63), channel_id=1, source_target_pairs={{0,4},{4,0},{8,12},{12,8},{1,5},{5,1},{9,13},{13,9},{2,6},{6,2},{1... | collective-permute-start | bytes 172040 | tf_op jit(solution)/shard_map/ppermute | solution.py:532
  21.8 6.8 %collective-permute-start.7 = (bf16[112,256]{1,0:T(8,128)(2,1)S(1)}, bf16[112,256]{1,0:T(8,128)(2,1)S(1)}, u32[]{:S(2)}, u32[]{:S(2)}) collective-permute-start(bf16[112,256]{1,0:T(8,128)(2,1)S(1)} %get-tuple-element.64), channel_id=1, source_target_pairs={{0,12},{4,8},{8,4},{12,0},{1,13},{5,9},{9,5},{13,1},{2,14},{6,10},... | collective-permute-start | bytes 172040 | tf_op jit(solution)/shard_map/ppermute | solution.py:532
  23.8 4.8 %collective-permute-start.8 = (bf16[48,256]{1,0:T(8,128)(2,1)S(1)}, bf16[48,256]{1,0:T(8,128)(2,1)S(1)}, u32[]{:S(2)}, u32[]{:S(2)}) collective-permute-start(bf16[48,256]{1,0:T(8,128)(2,1)S(1)} %get-tuple-element.67.rest_0_), channel_id=1, source_target_pairs={{0,8},{4,12},{8,0},{12,4},{1,9},{5,13},{9,1},{13,5},{2,10},{6,14},... | collective-permute-start | bytes 73736 | tf_op jit(solution)/shard_map/ppermute | solution.py:532
  28.7 3.8 %collective-permute-start.10 = (f32[8,256]{1,0:T(8,128)S(1)}, f32[8,256]{1,0:T(8,128)S(1)}, u32[]{:S(2)}, u32[]{:S(2)}) collective-permute-start(f32[8,256]{1,0:T(8,128)S(1)} %pairs.1.rest_0_), channel_id=1, source_target_pairs={{0,2},{1,3},{2,0},{3,1},{4,6},{5,7},{6,4},{7,5},{8,10},{9,11},{10,... | collective-permute-start | bytes 24584 | tf_op jit(solution)/shard_map/ppermute | solution.py:532
  30.2 3.1 %collective-permute-start.11 = (f32[8,256]{1,0:T(8,128)S(1)}, f32[8,256]{1,0:T(8,128)S(1)}, u32[]{:S(2)}, u32[]{:S(2)}) collective-permute-start(f32[8,256]{1,0:T(8,128)S(1)} %pairs.1.rest_0_), channel_id=1, source_target_pairs={{0,3},{1,2},{2,1},{3,0},{4,7},{5,6},{6,5},{7,4},{8,11},{9,10},{10,... | collective-permute-start | bytes 24584 | tf_op jit(solution)/shard_map/ppermute | solution.py:532
  30.2 3.1 %collective-permute-start.9 = (f32[8,256]{1,0:T(8,128)S(1)}, f32[8,256]{1,0:T(8,128)S(1)}, u32[]{:S(2)}, u32[]{:S(2)}) collective-permute-start(f32[8,256]{1,0:T(8,128)S(1)} %pairs.1.rest_0_), channel_id=1, source_target_pairs={{0,1},{1,0},{2,3},{3,2},{4,5},{5,4},{6,7},{7,6},{8,9},{9,8},{10,11... | collective-permute-start | bytes 24584 | tf_op jit(solution)/shard_map/ppermute | solution.py:532
